TPU v7x, 32 devices: a whole 2x2x4 slice. The times are simulated.
32 devices in a mesh: period: 2 (over x), gx: 16 (over z, y, core).
Axes of the slice: x: 2, y: 2, z: 4, core: 2. Of those that a mesh axis runs over, the one named last changes fastest.
Arguments:
- site_owner: int32 [4096], P(('period', 'gx')), parts along dimension 0, may hold values from 0 to 15, as said below
- site_cell: int32 [3, 4096], P(None, ('period', 'gx')), parts along dimension 1, may hold values from 0 to 125, as said below
- stencil_code: int32 [8, 4096], P(None, ('period', 'gx')), parts along dimension 1, may hold values from 0 to 26
- site_residual: float32 [6, 8, 4096], P(None, None, ('period', 'gx')), parts along dimension 2, may hold values from -4 to 4
- conductivity: float32 [3, 64, 32, 128], P(None, 'gx'), may hold values from 0.2 to 2
- omega: float32 [2], P('period'), parts along dimension 0, may hold values from 0.5 to 1.5
Outputs:
- adjoint_field: float32 [12, 64, 32, 128], P('period', 'gx'), parts along dimension 0
- residual: float32 [12, 64, 32, 128], P('period', 'gx'), parts along dimension 0
There are 2 independent parts, one for each index of `period`. A program takes and returns all parts, laid end to end along the dimension named above; an argument that names none is the same for every part. Nothing has to cross between parts.
Inputs may be any that keep to these rules, and one draw needn't show every extreme that they name: `site_owner`: in each aligned block of 128 sites (the sites of one device) no slab is named more than 16 times, and in every block some slab is named exactly 16 times. `site_cell`: row 0 is the base cell along the first dimension within the owning slab, 0 to 1; row 1 along the second dimension, 0 to 29; row 2 along the third, 0 to 125.
All inputs are finite; a program needn't handle non-finite values.
Results may differ from a plain program's by a relative error of at most 0.0003.
Values sent between devices are 32-bit elements; how exact they have to be, the bound alone decides.
No kernel may reach another device: no remote copies, remote signals or barrier semaphores. Data moves between devices by JAX's collectives and lax.ppermute only.
A program may use at most 128 MiB of HBM per device.

v0:
```python
import jax
import jax.numpy as jnp
from jax import lax
from jax.sharding import PartitionSpec as P

ITERS = 4


def padded(x, sides, width):
    for axis, dim in sides:
        peers, length = (lax.axis_size(axis), x.shape[dim])
        up = [(i, (i + 1) % peers) for i in range(peers - 1)]
        down = [(j, i) for i, j in up]
        last = lax.slice_in_dim(x, length - width, length, axis=dim)
        first = lax.slice_in_dim(x, 0, width, axis=dim)
        before = lax.ppermute(last, axis, up)
        after = lax.ppermute(first, axis, down)
        x = jnp.concatenate([before, x, after], axis=dim)
    return x


def ahead(array, which_axis):
    extent = array.shape[which_axis]
    following = jnp.concatenate(
        [
            lax.slice_in_dim(array, 1, extent, axis=which_axis),
            jnp.zeros_like(lax.slice_in_dim(array, 0, 1, axis=which_axis)),
        ],
        axis=which_axis,
    )
    return following - array


def behind(array, which_axis):
    extent = array.shape[which_axis]
    preceding = jnp.concatenate(
        [
            jnp.zeros_like(lax.slice_in_dim(array, 0, 1, axis=which_axis)),
            lax.slice_in_dim(array, 0, extent - 1, axis=which_axis),
        ],
        axis=which_axis,
    )
    return array - preceding


def ahead_of(array, top_plane):
    return jnp.concatenate([array[:, 1:], top_plane], axis=1) - array


def behind_of(array, low_plane):
    return array - jnp.concatenate([low_plane, array[:, :-1]], axis=1)


def face_terms(edge_x, edge_y, edge_z, top_y, top_z):
    face_x = ahead(edge_z, 2) - ahead(edge_y, 3)
    face_y = ahead(edge_x, 3) - ahead_of(edge_z, top_z)
    face_z = ahead_of(edge_y, top_y) - ahead(edge_x, 2)
    return (face_x, face_y, face_z)


def edge_terms(face_x, face_y, face_z, low_y, low_z):
    curl_x = behind(face_z, 2) - behind(face_y, 3)
    curl_y = behind(face_x, 3) - behind_of(face_z, low_z)
    curl_z = behind_of(face_y, low_y) - behind(face_x, 2)
    return jnp.stack([curl_x, curl_y, curl_z], axis=1)


def couple(curl_curl, halves, coupling):
    real_part = curl_curl[0] + coupling * halves[1]
    imag_part = curl_curl[1] - coupling * halves[0]
    return jnp.concatenate([real_part, imag_part], axis=0)


def pair_form(first_field, second_field):
    real_sum = jnp.sum(first_field[:3] * second_field[:3]) - jnp.sum(
        first_field[3:] * second_field[3:]
    )
    imag_sum = jnp.sum(first_field[:3] * second_field[3:]) + jnp.sum(
        first_field[3:] * second_field[:3]
    )
    return jnp.stack([real_sum, imag_sum])


def divide_complex(numer, denom):
    modulus = denom[0] * denom[0] + denom[1] * denom[1]
    return jnp.stack(
        [
            (numer[0] * denom[0] + numer[1] * denom[1]) / modulus,
            (numer[1] * denom[0] - numer[0] * denom[1]) / modulus,
        ]
    )


def scale_field(factor, field):
    return jnp.concatenate(
        [
            factor[0] * field[:3] - factor[1] * field[3:],
            factor[0] * field[3:] + factor[1] * field[:3],
        ],
        axis=0,
    )


def square_form(residual):
    return lax.psum(pair_form(residual, residual), "gx")


def per_device(site_owner, site_cell, stencil_code, site_residual, conductivity, omega):
    slab_depth, grid_rows, grid_cols = (
        conductivity.shape[1],
        conductivity.shape[2],
        conductivity.shape[3],
    )
    site_count = site_owner.shape[0]
    own_index = lax.axis_index("gx")
    first_slab = own_index == 0
    target = (
        (
            (site_cell[0][None, :] + stencil_code // 9) * grid_rows
            + site_cell[1][None, :]
            + stencil_code // 3 % 3
        )
        * grid_cols
        + site_cell[2][None, :]
        + stencil_code % 3
    )
    tagged = target.astype(jnp.float32)
    values = site_residual.reshape(-1, site_count)
    owner_tag = site_owner.astype(jnp.float32)[None, :]
    all_values, all_tags = (
        lax.all_gather(values, "gx", axis=1, tiled=True),
        lax.all_gather(jnp.concatenate([tagged, owner_tag], axis=0), "gx", axis=1, tiled=True),
    )
    owned_mask = (all_tags[-1:] == own_index.astype(jnp.float32)).astype(jnp.float32)
    placed_values = all_values * owned_mask
    placed_targets = all_tags[:-1].astype(jnp.int32)
    source = (
        jnp.zeros((6, slab_depth * grid_rows * grid_cols), jnp.float32)
        .at[:, placed_targets.reshape(-1)]
        .add(placed_values.reshape(6, -1))
    )
    source = source.reshape(6, slab_depth, grid_rows, grid_cols)
    coupling = omega[0] * conductivity
    solution = jnp.zeros_like(source)
    residual = source
    direction = source
    form_now = square_form(residual)
    for sweep in range(ITERS):
        halves = direction.reshape(2, 3, slab_depth, grid_rows, grid_cols)
        extended = padded(direction, (("gx", 1),), 1)
        wide_halves = extended.reshape(2, 3, slab_depth + 2, grid_rows, grid_cols)
        face_x, face_y, face_z = face_terms(
            wide_halves[:, 0, :-1],
            wide_halves[:, 1, :-1],
            wide_halves[:, 2, :-1],
            wide_halves[:, 1, -1:],
            wide_halves[:, 2, -1:],
        )
        low_y = jnp.where(first_slab, jnp.zeros_like(face_y[:, :1]), face_y[:, :1])
        low_z = jnp.where(first_slab, jnp.zeros_like(face_z[:, :1]), face_z[:, :1])
        curl_curl = edge_terms(face_x[:, 1:], face_y[:, 1:], face_z[:, 1:], low_y, low_z)
        applied = couple(curl_curl, halves, coupling)
        curvature = lax.psum(pair_form(direction, applied), "gx")
        step_size = divide_complex(form_now, curvature)
        solution = solution + scale_field(step_size, direction)
        residual = residual - scale_field(step_size, applied)
        if sweep + 1 < ITERS:
            form_next = square_form(residual)
            direction = residual + scale_field(divide_complex(form_next, form_now), direction)
            form_now = form_next
    return (solution, residual)


def solution(mesh):
    placed = (
        P(("period", "gx")),
        P(None, ("period", "gx")),
        P(None, ("period", "gx")),
        P(None, None, ("period", "gx")),
        P(None, "gx", None, None),
        P("period"),
    )
    return jax.shard_map(
        per_device,
        mesh=mesh,
        in_specs=placed,
        out_specs=(P("period", "gx", None, None), P("period", "gx", None, None)),
        check_vma=False,
    )
```

profile of v0, /device:TPU:0, one launch (start us, length us, event | category | flops | bytes accessed | tf_op | source)
XLA Modules:
  0.0 507.1 jit_solution(9631231731130776067)
XLA Ops:
  2.8 23.4 %all_gather.6 = f32[9,2048]{1,0:T(8,128)S(1)} all-gather(f32[9,128]{1,0:T(8,128)S(1)} %pad_maximum_fusion.8), channel_id=1, replica_groups=mesh['period'=2,'gx'=16] {'gx'}, dimensions={1}, use_global_device_ids=true | all-gather | bytes 78336 | tf_op jit(solution)/shard_map/all_gather | solution.py:132
  26.4 18.8 %all_gather.7 = f32[48,2048]{1,0:T(8,128)S(1)} all-gather(f32[48,128]{1,0:T(8,128)} %bitcast.270), channel_id=1, replica_groups=mesh['period'=2,'gx'=16] {'gx'}, dimensions={1}, use_global_device_ids=true | all-gather | bytes 417792 | tf_op jit(solution)/shard_map/all_gather | solution.py:131
  45.4 5.4 %copy.84 = f32[16384,6]{1,0:T(8,128)} copy(f32[16384,6]{0,1:T(8,128)S(1)} %bitcast.263) | data formatting | bytes 786432 | tf_op jit(solution)/shard_map/reshape | solution.py:140
  50.8 91.3 %scatter_custom_fusion = f32[6,16384]{0,1:T(8,128)} fusion(s32[16384]{0:T(1024)S(1)} %bitcast.267, f32[16384,6]{1,0:T(8,128)} %copy.84, f32[]{:T(128)} %constant.20.clone.1), kind=kCustom, calls=%fused_computation.4 | custom fusion | flops 98304 | bytes 393728 | tf_op jit(solution)/shard_map/scatter-add | solution.py:140
  142.1 4.0 fusion.61
  146.1 2.2 copy.126
  148.4 2.3 collective-permute-start
  151.3 1.3 collective-permute-start.1
  152.6 13.2 %multiply_reduce_fusion.1 = (f32[]{:T(128)}, f32[]{:T(128)}, f32[]{:T(128)}, f32[3,16384]{0,1:T(8,128)}, f32[3,16384]{0,1:T(8,128)}) fusion(f32[6,16384]{0,1:T(8,128)} %scatter_custom_fusion), kind=kLoop, calls=%fused_computation.2 | loop fusion | flops 294909 | bytes 786444 | tf_op jit(solution)/shard_map/reduce_sum | solution.py:75
  165.7 5.7 %copy.86 = f32[6,16384]{1,0:T(8,128)S(1)} copy(f32[6,16384]{0,1:T(8,128)} %scatter_custom_fusion) | data formatting | bytes 786432 | tf_op jit(solution)/shard_map/scatter-add | solution.py:140
  171.4 5.2 %copy.94 = f32[3,4,32,128]{3,2,1,0:T(8,128)S(1)} copy(f32[3,4,32,128]{0,3,2,1:T(8,128)} %bitcast.252) | data formatting | bytes 393216 | tf_op jit(solution)/shard_map/squeeze | solution.py:69
  176.6 5.3 %copy.95 = f32[3,4,32,128]{3,2,1,0:T(8,128)S(1)} copy(f32[3,4,32,128]{0,3,2,1:T(8,128)} %bitcast.251) | data formatting | bytes 393216 | tf_op jit(solution)/shard_map/slice | solution.py:75
  189.5 5.3 %copy.104 = f32[6,4,32,128]{3,2,1,0:T(8,128)S(1)} copy(f32[6,4,32,128]{0,3,2,1:T(8,128)} %bitcast.250) | data formatting | bytes 786432 | tf_op jit(solution)/shard_map/reshape | solution.py:142
  194.8 31.8 %all-reduce.32 = (f32[2]{0:T(128)S(1)}, f32[2]{0:T(128)S(1)}) all-reduce(f32[2]{0:T(128)S(1)} %pad_maximum_fusion.9, f32[2]{0:T(128)S(1)} %pad_maximum_fusion.10), channel_id=1, replica_groups=mesh['period'=2,'gx'=16] {'gx'}, use_global_device_ids=true, to_apply=%region_4.5 | all-reduce | flops 4 | bytes 32 | tf_op jit(solution)/shard_map/psum | solution.py:105
  241.6 29.5 %psum.58 = f32[2]{0:T(128)S(1)} all-reduce(f32[2]{0:T(128)S(1)} %pad_maximum_fusion.11), channel_id=1, replica_groups=mesh['period'=2,'gx'=16] {'gx'}, use_global_device_ids=true, to_apply=%region_13.14 | all-reduce | flops 2 | bytes 16 | tf_op jit(solution)/shard_map/psum | solution.py:105
  277.1 1.3 collective-permute-start.3
  278.4 3.0 collective-permute-start.2
  288.4 31.1 %psum.59 = f32[2]{0:T(128)S(1)} all-reduce(f32[2]{0:T(128)S(1)} %pad_maximum_fusion.12), channel_id=1, replica_groups=mesh['period'=2,'gx'=16] {'gx'}, use_global_device_ids=true, to_apply=%region_18.19 | all-reduce | flops 2 | bytes 16 | tf_op jit(solution)/shard_map/psum | solution.py:163
  331.3 29.5 %psum.60 = f32[2]{0:T(128)S(1)} all-reduce(f32[2]{0:T(128)S(1)} %pad_maximum_fusion.13), channel_id=1, replica_groups=mesh['period'=2,'gx'=16] {'gx'}, use_global_device_ids=true, to_apply=%region_22.23 | all-reduce | flops 2 | bytes 16 | tf_op jit(solution)/shard_map/psum | solution.py:105
  368.0 3.0 collective-permute-start.4
  377.9 30.8 %psum.61 = f32[2]{0:T(128)S(1)} all-reduce(f32[2]{0:T(128)S(1)} %pad_maximum_fusion.14), channel_id=1, replica_groups=mesh['period'=2,'gx'=16] {'gx'}, use_global_device_ids=true, to_apply=%region_27.28 | all-reduce | flops 2 | bytes 16 | tf_op jit(solution)/shard_map/psum | solution.py:163
  420.5 29.5 %psum.62 = f32[2]{0:T(128)S(1)} all-reduce(f32[2]{0:T(128)S(1)} %pad_maximum_fusion.15), channel_id=1, replica_groups=mesh['period'=2,'gx'=16] {'gx'}, use_global_device_ids=true, to_apply=%region_31.32 | all-reduce | flops 2 | bytes 16 | tf_op jit(solution)/shard_map/psum | solution.py:105
  457.2 3.0 collective-permute-start.6
  465.6 31.3 %psum.63 = f32[2]{0:T(128)S(1)} all-reduce(f32[2]{0:T(128)S(1)} %pad_maximum_fusion.16), channel_id=1, replica_groups=mesh['period'=2,'gx'=16] {'gx'}, use_global_device_ids=true, to_apply=%region_36.37 | all-reduce | flops 2 | bytes 16 | tf_op jit(solution)/shard_map/psum | solution.py:163
  (144 shorter events, 23.5 us)
Async XLA Ops:
  148.4 36.9 %collective-permute-start = (f32[6,1,32,128]{3,2,0,1:T(8,128)S(1)}, f32[6,1,32,128]{3,2,0,1:T(8,128)S(1)}, u32[]{:S(2)}, u32[]{:S(2)}) collective-permute-start(f32[6,1,32,128]{3,2,0,1:T(8,128)S(1)} %copy.126), channel_id=1, source_target_pairs={{0,1},{1,2},{2,3},{3,4},{4,5},{5,6},{6,7},{7,8},{8,9},{9,10},{10,1... | collective-permute-start | bytes 294920 | tf_op jit(solution)/shard_map/ppermute | solution.py:16
  151.3 34.4 %collective-permute-start.1 = (f32[6,1,32,128]{3,2,0,1:T(8,128)S(1)}, f32[6,1,32,128]{3,2,0,1:T(8,128)S(1)}, u32[]{:S(2)}, u32[]{:S(2)}) collective-permute-start(f32[6,1,32,128]{3,2,0,1:T(8,128)S(1)} %copy.128), channel_id=1, source_target_pairs={{1,0},{2,1},{3,2},{4,3},{5,4},{6,5},{7,6},{8,7},{9,8},{10,9},{11,1... | collective-permute-start | bytes 294920 | tf_op jit(solution)/shard_map/ppermute | solution.py:17
  176.6 9.5 %copy-start = (f32[3,4,32,128]{3,2,1,0:T(8,128)S(1)}, f32[3,4,32,128]{3,2,1,0:T(8,128)}, u32[]{:S(2)}) copy-start(f32[3,4,32,128]{3,2,1,0:T(8,128)} %param.10) | copy-start | bytes 589828
  277.1 5.6 %collective-permute-start.3 = (f32[6,1,32,128]{3,2,1,0:T(8,128)S(1)}, f32[6,1,32,128]{3,2,1,0:T(8,128)S(1)}, u32[]{:S(2)}, u32[]{:S(2)}) collective-permute-start(f32[6,1,32,128]{3,2,1,0:T(8,128)S(1)} %get-tuple-element.98), channel_id=1, source_target_pairs={{1,0},{2,1},{3,2},{4,3},{5,4},{6,5},{7,6},{8,7},{9,8},{10,9},{11,1... | collective-permute-start | bytes 294920 | tf_op jit(solution)/shard_map/ppermute | solution.py:17
  278.4 4.3 collective-permute-start.2
  366.7 5.7 %collective-permute-start.5 = (f32[6,1,32,128]{3,2,1,0:T(8,128)S(1)}, f32[6,1,32,128]{3,2,1,0:T(8,128)S(1)}, u32[]{:S(2)}, u32[]{:S(2)}) collective-permute-start(f32[6,1,32,128]{3,2,1,0:T(8,128)S(1)} %get-tuple-element.90), channel_id=1, source_target_pairs={{1,0},{2,1},{3,2},{4,3},{5,4},{6,5},{7,6},{8,7},{9,8},{10,9},{11,1... | collective-permute-start | bytes 294920 | tf_op jit(solution)/shard_map/ppermute | solution.py:17
  368.0 4.4 collective-permute-start.4
  455.9 4.3 collective-permute-start.7
  457.2 4.0 collective-permute-start.6
where the time goes:
time: 509 us; the launch traced here: 507 us
  blocking collectives  256 us (50%)
  other arithmetic  116 us (23%)
  between operations  76.5 us (15%)
  local copies, waits for them, and re-layouts  41.1 us (8%)
  starting transfers between devices  16.5 us (3%)
    psum x4, blocking collectives, square_form(): return lax.psum(pair_form(residual, residual), 'gx')  120 us
    psum x3, blocking collectives, per_device(): curvature = lax.psum(pair_form(direction, applied), 'gx')  93.1 us
    scatter-add x1, other arithmetic, per_device(): source = jnp.zeros((6, slab_depth * grid_rows * grid_cols), jnp.float32)....  91.3 us
    all_gather x1, blocking collectives, per_device(): lax.all_gather(jnp.concatenate([tagged, owner_tag], axis=0), 'gx', axis=1...  23.4 us
    all_gather x1, blocking collectives, per_device(): lax.all_gather(values, 'gx', axis=1, tiled=True)  18.8 us
    reduce_sum x8, other arithmetic, pair_form(): jnp.sum(first_field[3:] * second_field[3:])  18.6 us
    ppermute x4, starting transfers between devices, padded(): before = lax.ppermute(last, axis, up)  11.4 us
  transfers between devices with their start and end apart: 8, of which 1 were waited for; matrix products, arithmetic and copies ran while one was open for 6% of the time, Pallas kernels for 0%

commit v1 on v0

v1 whole, which is shorter than its diff:
```python
import functools

import jax
import jax.numpy as jnp
from jax import lax
from jax.experimental import pallas as pl
from jax.experimental.pallas import tpu as pltpu
from jax.sharding import PartitionSpec as P

ITERS = 4
CENTRE = 5.0
RADIUS = 5.0
BASIS = ITERS + 1
FORMS = 2 * ITERS
PAIRS = [(i // 2, (i + 1) // 2) for i in range(FORMS)]
VMEM_LIMIT = 40 * 1024 * 1024
CONTRACT_LANES = (((1,), (1,)), ((), ()))


def vmem():
    return pl.BlockSpec(memory_space=pltpu.VMEM)


def smem():
    return pl.BlockSpec(memory_space=pltpu.SMEM)


def split_bf16(x):
    high = x.astype(jnp.bfloat16)
    return high, (x - high.astype(jnp.float32)).astype(jnp.bfloat16)


def bin_kernel(n, half, rows, cols, half_depth, owner_ref, cell_ref, code_ref, value_ref, out_ref):
    sites = owner_ref.shape[1]
    owner = owner_ref[...]
    code = code_ref[...]
    dx = (code >= 9).astype(jnp.int32) + (code >= 18).astype(jnp.int32)
    rest = code - 9 * dx
    dy = (rest >= 3).astype(jnp.int32) + (rest >= 6).astype(jnp.int32)
    dz = rest - 3 * dy
    x = cell_ref[0:1] + dx
    y = cell_ref[1:2] + dy
    z = cell_ref[2:3] + dz
    upper = (x >= half_depth).astype(jnp.int32)
    row = (x - half_depth * upper) * rows + y
    lane = z + cols * upper
    channels, points = value_ref.shape[0], value_ref.shape[1]
    data = jnp.concatenate(
        [value_ref[...].reshape(channels * points, sites), row.astype(jnp.float32), lane.astype(jnp.float32)],
        axis=0,
    )
    blank = jnp.zeros_like(data)

    named = lax.broadcasted_iota(jnp.int32, (n, sites), 0) == owner
    earlier = lax.broadcasted_iota(jnp.int32, (sites, sites), 0) < lax.broadcasted_iota(
        jnp.int32, (sites, sites), 1
    )
    named_f = named.astype(jnp.float32)
    counts = jnp.dot(
        named_f.astype(jnp.bfloat16),
        earlier.astype(jnp.float32).astype(jnp.bfloat16),
        preferred_element_type=jnp.float32,
    )
    rank = jnp.sum(counts * named_f, axis=0, keepdims=True).astype(jnp.int32)
    second = rank >= half
    place = jnp.where(second, rank - half, rank)

    slot = lax.broadcasted_iota(jnp.int32, (out_ref.shape[0], sites), 0)
    hit = jnp.zeros(slot.shape, jnp.bool_)
    for j in range(3):
        hit = hit | (slot == ((owner - j + 1) * 3 + j) * half + place)
    total = jnp.zeros(out_ref.shape, jnp.float32)
    for part, stacked in (
        (jnp.logical_not(second), [data, blank]),
        (second, [blank, data]),
    ):
        chosen = jnp.where(hit & part, 1.0, 0.0).astype(jnp.bfloat16)
        for piece in split_bf16(jnp.concatenate(stacked, axis=0)):
            total = total + lax.dot_general(
                chosen, piece, CONTRACT_LANES, preferred_element_type=jnp.float32
            )
    out_ref[...] = total


def field_kernel(
    n, recv_ref, cond_ref, low_ref, high_ref, omega_ref, forms_ref, own_ref, basis, coupling, left, right
):
    depth, rows, cols = cond_ref.shape[1], cond_ref.shape[2], cond_ref.shape[3]
    half_depth = depth // 2
    channels = 6
    points = 8
    group = recv_ref.shape[1] // 3
    me = lax.axis_index("gx")
    keep_low = jnp.where(me > 0, 1.0, 0.0).astype(jnp.float32)
    keep_high = jnp.where(me < n - 1, 1.0, 0.0).astype(jnp.float32)

    scale = omega_ref[0] * (2.0 / RADIUS)
    halo = low_ref.shape[1]
    coupling[:, 0:halo] = low_ref[...] * scale
    coupling[:, halo : halo + depth] = cond_ref[...] * scale
    coupling[:, halo + depth : 2 * halo + depth] = high_ref[...] * scale

    row_count = half_depth * rows
    lane_count = 2 * cols
    slots = 2 * recv_ref.shape[0] * group
    width = (channels + 2) * points
    row_iota = lax.broadcasted_iota(jnp.int32, (row_count, slots), 0)
    lane_iota = lax.broadcasted_iota(jnp.int32, (lane_count, slots), 0)

    def scatter(j, _):
        packed = recv_ref[:, pl.ds(pl.multiple_of(j * group, 8), group), :].reshape(slots // 2, 2 * width)
        turned = packed.T
        table = jnp.concatenate([turned[:width], turned[width:]], axis=1)
        table_high = table.astype(jnp.bfloat16).astype(jnp.float32)
        table_low = table - table_high
        cell_row = table[channels * points : (channels + 1) * points].astype(jnp.int32)
        cell_lane = table[(channels + 1) * points :].astype(jnp.int32)
        for k in range(points):
            span = slice(k * slots, (k + 1) * slots)
            right[:, span] = jnp.where(lane_iota == cell_lane[k : k + 1], 1.0, 0.0).astype(jnp.bfloat16)
            mask = row_iota == cell_row[k : k + 1]
            for c in range(channels):
                at = c * points + k
                for piece, part in enumerate((table_high, table_low)):
                    first = (piece * channels + c) * row_count
                    left[first : first + row_count, span] = jnp.where(mask, part[at : at + 1], 0.0).astype(
                        jnp.bfloat16
                    )
        both = lax.dot_general(left[...], right[...], CONTRACT_LANES, preferred_element_type=jnp.float32)
        summed = both[: channels * row_count] + both[channels * row_count :]
        for c in range(channels):
            for x in range(depth):
                first = c * row_count + (x % half_depth) * rows
                lanes = slice((x // half_depth) * cols, (x // half_depth + 1) * cols)
                basis[0, c, j * depth + x] = summed[first : first + rows, lanes]
        return 0

    lax.fori_loop(0, 3, scatter, 0)

    y_iota = lax.broadcasted_iota(jnp.int32, (rows, cols), 0)
    z_iota = lax.broadcasted_iota(jnp.int32, (rows, cols), 1)
    y_first, y_last = y_iota == 0, y_iota == rows - 1
    z_first, z_last = z_iota == 0, z_iota == cols - 1

    def ahead_y(f):
        return jnp.where(y_last, 0.0, pltpu.roll(f, rows - 1, 0)) - f

    def ahead_z(f):
        return jnp.where(z_last, 0.0, pltpu.roll(f, cols - 1, 1)) - f

    def behind_y(f):
        return f - jnp.where(y_first, 0.0, pltpu.roll(f, 1, 0))

    def behind_z(f):
        return f - jnp.where(z_first, 0.0, pltpu.roll(f, 1, 1))

    def faces(k, part, p):
        ex, ey, ez = (basis[k, 3 * part + q, p] for q in range(3))
        ey_next, ez_next = basis[k, 3 * part + 1, p + 1], basis[k, 3 * part + 2, p + 1]
        keep = jnp.where(p < depth, keep_low, 1.0)
        hx = ahead_y(ez) - ahead_z(ey)
        hy = (ahead_z(ex) - (ez_next - ez)) * keep
        hz = ((ey_next - ey) - ahead_y(ex)) * keep
        return hx, hy, hz, (ex, ey, ez)

    for k in range(ITERS):
        weight = (1.0 if k == 0 else 2.0) / RADIUS

        def plane(p, carried):
            keep = jnp.where(p >= 2 * depth, keep_high, 1.0)
            result = []
            for part in range(2):
                hy_before, hz_before = carried[2 * part], carried[2 * part + 1]
                hx, hy, hz, edges = faces(k, part, p)
                curls = (
                    behind_y(hz) - behind_z(hy),
                    behind_z(hx) - (hz - hz_before),
                    (hy - hy_before) - behind_y(hx),
                )
                for q in range(3):
                    other = coupling[q, p - (ITERS - halo)] * basis[k, 3 * (1 - part) + q, p]
                    if k == 0:
                        other = 0.5 * other
                    shifted = weight * (curls[q] - CENTRE * edges[q])
                    new = shifted + other if part == 0 else shifted - other
                    if k > 0:
                        new = new - basis[k - 1, 3 * part + q, p]
                    basis[k + 1, 3 * part + q, p] = new * keep
                result += [hy, hz]
            return tuple(result)

        start = []
        for part in range(2):
            _, hy, hz, _ = faces(k, part, k)
            start += [hy, hz]
        lax.fori_loop(k + 1, 3 * depth - k - 1, plane, tuple(start))

    def plane_forms(p, sums):
        sums = list(sums)
        for q in range(3):
            re = [basis[k, q, p] for k in range(BASIS)]
            im = [basis[k, 3 + q, p] for k in range(BASIS)]
            for f, (i, j) in enumerate(PAIRS):
                real = re[i] * re[j] - im[i] * im[j]
                imag = re[i] * im[j] + im[i] * re[j] if i != j else 2.0 * (re[i] * im[i])
                for half, term in ((0, real), (1, imag)):
                    sums[2 * f + half] = sums[2 * f + half] + jnp.sum(term.reshape(rows // 8, 8, cols), axis=0)
        return tuple(sums)

    zero = jnp.zeros((8, cols), jnp.float32)
    sums = lax.fori_loop(depth, 2 * depth, plane_forms, (zero,) * (2 * FORMS))
    for f in range(2 * FORMS):
        forms_ref[f : f + 1] = jnp.sum(sums[f], axis=0, keepdims=True)
    own_ref[...] = basis[:, :, depth : 2 * depth]


def c_add(a, b):
    return a[0] + b[0], a[1] + b[1]


def c_sub(a, b):
    return a[0] - b[0], a[1] - b[1]


def c_mul(a, b):
    return a[0] * b[0] - a[1] * b[1], a[0] * b[1] + a[1] * b[0]


def c_scale(s, a):
    return s * a[0], s * a[1]


def c_div(a, b):
    inverse = 1.0 / (b[0] * b[0] + b[1] * b[1])
    return (a[0] * b[0] + a[1] * b[1]) * inverse, (a[1] * b[0] - a[0] * b[1]) * inverse


def step_scalars(moments):
    resid = list(moments)
    direc = list(moments)
    none = (jnp.zeros_like(moments[0][0]),) * 2
    one = (jnp.ones_like(moments[0][0]), jnp.zeros_like(moments[0][0]))
    resid_at = [one] + [none] * ITERS
    direc_at = [one] + [none] * ITERS
    field_at = [none] * BASIS
    rho = moments[0]
    for n in range(ITERS):
        applied = [c_add(c_scale(CENTRE, direc[0]), c_scale(RADIUS, direc[1]))]
        for l in range(1, len(direc) - 1):
            near = c_scale(RADIUS / 2, c_add(direc[l + 1], direc[l - 1]))
            applied.append(c_add(c_scale(CENTRE, direc[l]), near))
        step = c_div(rho, c_mul(direc_at[n], applied[n]))
        applied_at = [c_scale(CENTRE, direc_at[j]) if j <= n else none for j in range(BASIS)]
        for j in range(n + 1):
            if j == 0:
                applied_at[1] = c_add(applied_at[1], c_scale(RADIUS, direc_at[0]))
            else:
                spread = c_scale(RADIUS / 2, direc_at[j])
                applied_at[j + 1] = c_add(applied_at[j + 1], spread)
                applied_at[j - 1] = c_add(applied_at[j - 1], spread)
        for j in range(n + 1):
            field_at[j] = c_add(field_at[j], c_mul(step, direc_at[j]))
        for j in range(n + 2):
            resid_at[j] = c_sub(resid_at[j], c_mul(step, applied_at[j]))
        if n + 1 < ITERS:
            resid = [c_sub(resid[l], c_mul(step, applied[l])) for l in range(len(applied))]
            rho_next = c_mul(resid_at[n + 1], resid[n + 1])
            ratio = c_div(rho_next, rho)
            direc = [c_add(resid[l], c_mul(ratio, direc[l])) for l in range(len(resid))]
            direc_at = [
                c_add(resid_at[j], c_mul(ratio, direc_at[j])) if j <= n else resid_at[j] for j in range(BASIS)
            ]
            rho = rho_next
    return field_at, resid_at


def combine_kernel(forms_ref, own_ref, field_ref, resid_ref):
    totals = jnp.sum(forms_ref[...], axis=1, keepdims=True)
    forms = [(totals[2 * f : 2 * f + 1], totals[2 * f + 1 : 2 * f + 2]) for f in range(FORMS)]
    moments = forms[:2]
    for f in range(2, FORMS):
        moments.append(c_sub(c_scale(2.0, forms[f]), forms[f % 2]))
    field_at, resid_at = step_scalars(moments)
    depth, rows, cols = field_ref.shape[1:]

    def spread(factors):
        return [tuple(jnp.broadcast_to(half, (rows, cols)) for half in factor) for factor in factors]

    field_at, resid_at = spread(field_at[:ITERS]), spread(resid_at)

    def plane(p, _):
        for q in range(3):
            re = [own_ref[k, q, p] for k in range(BASIS)]
            im = [own_ref[k, 3 + q, p] for k in range(BASIS)]
            for out_ref, factors in ((field_ref, field_at), (resid_ref, resid_at)):
                real = sum(f[0] * re[k] - f[1] * im[k] for k, f in enumerate(factors))
                imag = sum(f[0] * im[k] + f[1] * re[k] for k, f in enumerate(factors))
                out_ref[q, p] = real
                out_ref[3 + q, p] = imag
        return 0

    lax.fori_loop(0, depth, plane, 0)


def params():
    return pltpu.CompilerParams(vmem_limit_bytes=VMEM_LIMIT)


def per_device(n, site_owner, site_cell, stencil_code, site_residual, conductivity, omega):
    depth, rows, cols = conductivity.shape[1:]
    sites = site_owner.shape[0]
    cap = 2 * sites // n
    half = cap // 2
    halo = ITERS - 1
    low = lax.ppermute(conductivity[:, depth - halo :], "gx", [(i, i + 1) for i in range(n - 1)])
    high = lax.ppermute(conductivity[:, :halo], "gx", [(i + 1, i) for i in range(n - 1)])

    packed = pl.pallas_call(
        functools.partial(bin_kernel, n, half, rows, cols, depth // 2),
        out_shape=jax.ShapeDtypeStruct((n * 3 * half, 2 * 8 * 8), jnp.float32),
        in_specs=[vmem()] * 4,
        out_specs=vmem(),
        compiler_params=params(),
        name="bin_sites",
    )(site_owner.reshape(1, sites), site_cell, stencil_code, site_residual)
    recv = lax.all_to_all(packed.reshape(n, 3 * half, -1), "gx", 0, 0)
    if half % 8:
        recv = recv.reshape(n, 3, half, -1).transpose(1, 0, 2, 3).reshape(1, 3 * n * half, -1)

    slots = n * cap
    forms, own = pl.pallas_call(
        functools.partial(field_kernel, n),
        out_shape=(
            jax.ShapeDtypeStruct((2 * FORMS, cols), jnp.float32),
            jax.ShapeDtypeStruct((BASIS, 6, depth, rows, cols), jnp.float32),
        ),
        in_specs=[vmem()] * 4 + [smem()],
        out_specs=(vmem(), vmem()),
        scratch_shapes=[
            pltpu.VMEM((BASIS, 6, 3 * depth, rows, cols), jnp.float32),
            pltpu.VMEM((3, 2 * halo + depth, rows, cols), jnp.float32),
            pltpu.VMEM((2 * 6 * depth // 2 * rows, 8 * slots), jnp.bfloat16),
            pltpu.VMEM((2 * cols, 8 * slots), jnp.bfloat16),
        ],
        compiler_params=params(),
        name="krylov_basis",
    )(recv, conductivity, low, high, omega)

    bit = 1
    while bit < n:
        forms = forms + lax.ppermute(forms, "gx", [(i, i ^ bit) for i in range(n)])
        bit *= 2

    return pl.pallas_call(
        combine_kernel,
        out_shape=(jax.ShapeDtypeStruct((6, depth, rows, cols), jnp.float32),) * 2,
        in_specs=[vmem()] * 2,
        out_specs=(vmem(), vmem()),
        compiler_params=params(),
        name="combine_basis",
    )(forms, own)


def solution(mesh):
    placed = (
        P(("period", "gx")),
        P(None, ("period", "gx")),
        P(None, ("period", "gx")),
        P(None, None, ("period", "gx")),
        P(None, "gx", None, None),
        P("period"),
    )
    return jax.shard_map(
        functools.partial(per_device, mesh.shape["gx"]),
        mesh=mesh,
        in_specs=placed,
        out_specs=(P("period", "gx", None, None), P("period", "gx", None, None)),
        check_vma=False,
    )
```

time: 509 us -> 48.4 us (0.10)
  blocking collectives: 256 us -> 0 us
  other arithmetic: 116 us -> 0.01 us
  between operations: 76.5 us -> 1.34 us
  local copies, waits for them, and re-layouts: 41.1 us -> 4.69 us
  Pallas kernels: 0 us -> 11.8 us
  waiting for transfers between devices: 0.93 us -> 8.69 us
    psum x7 -> x0, blocking collectives: 213 us -> none  [the longest x4 120 us: square_form(): return lax.psum(pair_form(residual, residual), 'gx')]
    scatter-add x1 -> x0, other arithmetic: 91.3 us -> none  [per_device(): source = jnp.zeros((6, slab_depth * grid_rows * grid_cols), jnp.float32)....]
    all_gather x2 -> x0, blocking collectives: 42.2 us -> none  [the longest x1 23.4 us: per_device(): lax.all_gather(jnp.concatenate([tagged, owner_tag], axis=0), 'gx', axis=1...]
    reduce_sum x8 -> x0, other arithmetic: 18.6 us -> none  [pair_form(): jnp.sum(first_field[3:] * second_field[3:])]
    slice x61 -> x1, local copies, waits for them, and re-layouts: 15.5 us -> 1.01 us  [per_device(): conductivity[:, :halo]]
    pallas_call x0 -> x3, Pallas kernels: none -> 11.8 us  [the longest x1 9.09 us: per_device(): pl.pallas_call(functools.partial(field_kernel, n), out_shape=(jax.ShapeDt...]
    reshape x3 -> x0, local copies, waits for them, and re-layouts: 10.8 us -> none  [the longest x2 5.57 us: per_device(): placed_values.reshape(6, -1)]
    all_to_all x0 -> x1, starting transfers between devices: none -> 7.39 us  [per_device(): recv = lax.all_to_all(packed.reshape(n, 3 * half, -1), 'gx', 0, 0)]
  transfers between devices with their start and end apart: 8 -> 7, of which waited for: 1 -> 6; matrix products, arithmetic and copies ran while one was open for 6% -> 2% of each run, Pallas kernels for 0% -> 0%
where the time goes in v1:
time: 48.4 us; the launch traced here: 48 us
  starting transfers between devices  21.5 us (44%)
  Pallas kernels  11.8 us (24%)
  waiting for transfers between devices  8.69 us (18%)
  local copies, waits for them, and re-layouts  4.69 us (10%)
  between operations  1.34 us (3%)
    ppermute x4, starting transfers between devices, per_device(): forms = forms + lax.ppermute(forms, 'gx', [(i, i ^ bit) for i in range(n)])  9.79 us
    pallas_call x1, Pallas kernels, per_device(): pl.pallas_call(functools.partial(field_kernel, n), out_shape=(jax.ShapeDt...  9.09 us
    all_to_all x1, starting transfers between devices, per_device(): recv = lax.all_to_all(packed.reshape(n, 3 * half, -1), 'gx', 0, 0)  7.39 us
    ppermute x4, waiting for transfers between devices, per_device(): forms = forms + lax.ppermute(forms, 'gx', [(i, i ^ bit) for i in range(n)])  5.71 us
    unnamed x10, local copies, waits for them, and re-layouts  3.68 us
    ppermute x1, starting transfers between devices, per_device(): lax.ppermute(conductivity[:, depth - halo:], 'gx', [(i, i + 1) for i in r...  3.04 us
    all_to_all x1, waiting for transfers between devices, per_device(): recv = lax.all_to_all(packed.reshape(n, 3 * half, -1), 'gx', 0, 0)  2.65 us
    pallas_call x1, Pallas kernels, per_device(): pl.pallas_call(combine_kernel, out_shape=(jax.ShapeDtypeStruct((6, depth,...  1.59 us
  transfers between devices with their start and end apart: 7, of which 6 were waited for; matrix products, arithmetic and copies ran while one was open for 2% of the time, Pallas kernels for 0%

profile of v1, /device:TPU:0, one launch (start us, length us, event | category | flops | bytes accessed | tf_op | source)
XLA Modules:
  0.0 48.0 jit_solution(5576847483057608587)
XLA Ops:
  0.6 0.0 copy-start.1
  0.6 0.7 %copy-done.1 = f32[6,8,128]{2,1,0:T(8,128)S(1)} copy-done((f32[6,8,128]{2,1,0:T(8,128)S(1)}, f32[6,8,128]{2,1,0:T(8,128)}, u32[]{:S(2)}) %copy-start.1) | copy-done | bytes 24600
  1.4 0.7 %copy-done.2 = s32[8,128]{1,0:T(8,128)S(1)} copy-done((s32[8,128]{1,0:T(8,128)S(1)}, s32[8,128]{1,0:T(8,128)}, u32[]{:S(2)}) %copy-start.2) | copy-done | bytes 4120
  2.1 0.7 %copy-done.3 = s32[3,128]{1,0:T(4,128)S(1)} copy-done((s32[3,128]{1,0:T(4,128)S(1)}, s32[3,128]{1,0:T(4,128)}, u32[]{:S(2)}) %copy-start.3) | copy-done | bytes 1560
  2.7 0.7 %copy-done.4 = s32[128]{0:T(128)S(1)} copy-done((s32[128]{0:T(128)S(1)}, s32[128]{0:T(128)}, u32[]{:S(2)}) %copy-start.4) | copy-done | bytes 536
  3.4 1.1 %bin_sites.1 = f32[384,128]{1,0:T(8,128)} custom-call(s32[1,128]{1,0:T(1,128)S(1)} %bitcast.2, s32[3,128]{1,0:T(4,128)S(1)} %copy-done.3, s32[8,128]{1,0:T(8,128)S(1)} %copy-done.2, f32[6,8,128]{2,1,0:T(8,128)S(1)} %copy-done.1), custom_call_target="tpu_custom_call" | custom-call | tf_op jit(solution)/shard_map/bin_sites/pallas_call | solution.py:318
  4.5 7.4 %all-to-all-start = ((f32[16,24,128]{2,1,0:T(8,128)}), f32[16,24,128]{2,1,0:T(8,128)S(1)}, u32[]{:S(2)}, u32[]{:S(2)}) async-start(f32[16,24,128]{2,1,0:T(8,128)} %bitcast.1), calls=%async_computation | async-start | bytes 393216 | tf_op jit(solution)/shard_map/all_to_all | solution.py:326
  11.9 1.0 %fusion = (f32[3,3,32,128]{3,2,1,0:T(8,128)S(1)}, f32[3,3,32,128]{3,2,1,0:T(8,128)S(1)}) fusion(f32[3,4,32,128]{3,2,1,0:T(8,128)} %cond_ref.1), kind=kLoop, calls=%fused_computation | loop fusion | bytes 589824 | tf_op jit(solution)/shard_map/slice | solution.py:316
  12.9 1.3 %collective-permute-start.1 = (f32[3,3,32,128]{3,2,1,0:T(8,128)S(1)}, f32[3,3,32,128]{3,2,1,0:T(8,128)S(1)}, u32[]{:S(2)}, u32[]{:S(2)}) collective-permute-start(f32[3,3,32,128]{3,2,1,0:T(8,128)S(1)} %get-tuple-element.6), channel_id=1, source_target_pairs={{1,0},{2,1},{3,2},{4,3},{5,4},{6,5},{7,6},{8,7},{9,8},{10,9},{11,1... | collective-permute-start | bytes 442376 | tf_op jit(solution)/shard_map/ppermute | solution.py:316
  14.2 3.0 %collective-permute-start = (f32[3,3,32,128]{3,2,1,0:T(8,128)S(1)}, f32[3,3,32,128]{3,2,1,0:T(8,128)S(1)}, u32[]{:S(2)}, u32[]{:S(2)}) collective-permute-start(f32[3,3,32,128]{3,2,1,0:T(8,128)S(1)} %get-tuple-element.7), channel_id=1, source_target_pairs={{0,1},{1,2},{2,3},{3,4},{4,5},{5,6},{6,7},{7,8},{8,9},{9,10},{10,1... | collective-permute-start | bytes 442376 | tf_op jit(solution)/shard_map/ppermute | solution.py:315
  17.9 0.0 collective-permute-done.1.high_ref
  17.9 0.3 collective-permute-done.low_ref
  18.2 2.6 %all-to-all-done.recv_ref = f32[16,24,128]{2,1,0:T(8,128)S(1)} async-done(((f32[16,24,128]{2,1,0:T(8,128)}), f32[16,24,128]{2,1,0:T(8,128)S(1)}, u32[]{:S(2)}, u32[]{:S(2)}) %all-to-all-start) | async-done | bytes 196640 | tf_op jit(solution)/shard_map/all_to_all | solution.py:326
  20.9 0.9 %copy-done = f32[3,4,32,128]{3,2,1,0:T(8,128)S(1)} copy-done((f32[3,4,32,128]{3,2,1,0:T(8,128)S(1)}, f32[3,4,32,128]{3,2,1,0:T(8,128)}, u32[]{:S(2)}) %copy-start) | copy-done | bytes 196632
  21.8 9.1 %krylov_basis.1 = (f32[16,128]{1,0:T(8,128)S(1)}, f32[5,6,4,32,128]{4,3,2,1,0:T(8,128)S(1)}) custom-call(f32[16,24,128]{2,1,0:T(8,128)S(1)} %all-to-all-done.recv_ref, f32[3,4,32,128]{3,2,1,0:T(8,128)S(1)} %copy-done, f32[3,3,32,128]{3,2,1,0:T(8,128)S(1)} %collective-permute-done.low_ref, f32[3,3,32,128]{3,2,1,0:T(8,128)S(1)} %collective-permute-done.1.high_ref, ...), custom_call_target="tpu_custom_call" | custom-call | tf_op jit(solution)/shard_map/krylov_basis/pallas_call | solution.py:331
  30.9 1.1 %collective-permute-start.2 = (f32[16,128]{1,0:T(8,128)S(1)}, f32[16,128]{1,0:T(8,128)S(1)}, u32[]{:S(2)}, u32[]{:S(2)}) collective-permute-start(f32[16,128]{1,0:T(8,128)S(1)} %get-tuple-element.4), channel_id=1, source_target_pairs={{0,1},{1,0},{2,3},{3,2},{4,5},{5,4},{6,7},{7,6},{8,9},{9,8},{10,11... | collective-permute-start | bytes 24584 | tf_op jit(solution)/shard_map/ppermute | solution.py:351
  32.0 0.8 %collective-permute-done.2 = f32[16,128]{1,0:T(8,128)S(1)} collective-permute-done((f32[16,128]{1,0:T(8,128)S(1)}, f32[16,128]{1,0:T(8,128)S(1)}, u32[]{:S(2)}, u32[]{:S(2)}) %collective-permute-start.2) | collective-permute-done | bytes 8224 | tf_op jit(solution)/shard_map/ppermute | solution.py:351
  32.8 2.7 %collective-permute-start.3 = (f32[16,128]{1,0:T(8,128)S(1)}, f32[16,128]{1,0:T(8,128)S(1)}, u32[]{:S(2)}, u32[]{:S(2)}) collective-permute-start(f32[16,128]{1,0:T(8,128)S(1)} %add.12), channel_id=1, source_target_pairs={{0,2},{1,3},{2,0},{3,1},{4,6},{5,7},{6,4},{7,5},{8,10},{9,11},{10,... | collective-permute-start | bytes 24584 | tf_op jit(solution)/shard_map/ppermute | solution.py:351
  35.5 1.6 %collective-permute-done.3 = f32[16,128]{1,0:T(8,128)S(1)} collective-permute-done((f32[16,128]{1,0:T(8,128)S(1)}, f32[16,128]{1,0:T(8,128)S(1)}, u32[]{:S(2)}, u32[]{:S(2)}) %collective-permute-start.3) | collective-permute-done | bytes 8224 | tf_op jit(solution)/shard_map/ppermute | solution.py:351
  37.1 3.1 %collective-permute-start.4 = (f32[16,128]{1,0:T(8,128)S(1)}, f32[16,128]{1,0:T(8,128)S(1)}, u32[]{:S(2)}, u32[]{:S(2)}) collective-permute-start(f32[16,128]{1,0:T(8,128)S(1)} %add.13), channel_id=1, source_target_pairs={{0,4},{1,5},{2,6},{3,7},{4,0},{5,1},{6,2},{7,3},{8,12},{9,13},{10,... | collective-permute-start | bytes 24584 | tf_op jit(solution)/shard_map/ppermute | solution.py:351
  40.2 1.6 %collective-permute-done.4 = f32[16,128]{1,0:T(8,128)S(1)} collective-permute-done((f32[16,128]{1,0:T(8,128)S(1)}, f32[16,128]{1,0:T(8,128)S(1)}, u32[]{:S(2)}, u32[]{:S(2)}) %collective-permute-start.4) | collective-permute-done | bytes 8224 | tf_op jit(solution)/shard_map/ppermute | solution.py:351
  41.9 2.9 %collective-permute-start.5 = (f32[16,128]{1,0:T(8,128)S(1)}, f32[16,128]{1,0:T(8,128)S(1)}, u32[]{:S(2)}, u32[]{:S(2)}) collective-permute-start(f32[16,128]{1,0:T(8,128)S(1)} %add.14), channel_id=1, source_target_pairs={{0,8},{1,9},{2,10},{3,11},{4,12},{5,13},{6,14},{7,15},{8,0},{9,1},... | collective-permute-start | bytes 24584 | tf_op jit(solution)/shard_map/ppermute | solution.py:351
  44.8 1.6 %collective-permute-done.5 = f32[16,128]{1,0:T(8,128)S(1)} collective-permute-done((f32[16,128]{1,0:T(8,128)S(1)}, f32[16,128]{1,0:T(8,128)S(1)}, u32[]{:S(2)}, u32[]{:S(2)}) %collective-permute-start.5) | collective-permute-done | bytes 8224 | tf_op jit(solution)/shard_map/ppermute | solution.py:351
  46.4 1.6 %combine_basis.1 = (f32[6,4,32,128]{3,2,1,0:T(8,128)}, f32[6,4,32,128]{3,2,1,0:T(8,128)}) custom-call(f32[16,128]{1,0:T(8,128)S(1)} %add.15.forms_ref, f32[5,6,4,32,128]{4,3,2,1,0:T(8,128)S(1)} %get-tuple-element.5.own_ref), custom_call_target="tpu_custom_call" | custom-call | tf_op jit(solution)/shard_map/combine_basis/pallas_call | solution.py:354
  (8 shorter events, 0.0 us)
Async XLA Ops:
  0.6 0.7 %copy-start.1 = (f32[6,8,128]{2,1,0:T(8,128)S(1)}, f32[6,8,128]{2,1,0:T(8,128)}, u32[]{:S(2)}) copy-start(f32[6,8,128]{2,1,0:T(8,128)} %value_ref.1) | copy-start | bytes 73732
  1.4 0.7 %copy-start.2 = (s32[8,128]{1,0:T(8,128)S(1)}, s32[8,128]{1,0:T(8,128)}, u32[]{:S(2)}) copy-start(s32[8,128]{1,0:T(8,128)} %code_ref.1) | copy-start | bytes 12292
  2.1 0.7 %copy-start.3 = (s32[3,128]{1,0:T(4,128)S(1)}, s32[3,128]{1,0:T(4,128)}, u32[]{:S(2)}) copy-start(s32[3,128]{1,0:T(4,128)} %cell_ref.1) | copy-start | bytes 4612
  2.7 0.7 %copy-start.4 = (s32[128]{0:T(128)S(1)}, s32[128]{0:T(128)}, u32[]{:S(2)}) copy-start(s32[128]{0:T(128)} %param.6) | copy-start | bytes 1540
  4.5 16.4 %all-to-all-start = ((f32[16,24,128]{2,1,0:T(8,128)}), f32[16,24,128]{2,1,0:T(8,128)S(1)}, u32[]{:S(2)}, u32[]{:S(2)}) async-start(f32[16,24,128]{2,1,0:T(8,128)} %bitcast.1), calls=%async_computation | async-start | bytes 393216 | tf_op jit(solution)/shard_map/all_to_all | solution.py:326
  12.9 5.0 %collective-permute-start.1 = (f32[3,3,32,128]{3,2,1,0:T(8,128)S(1)}, f32[3,3,32,128]{3,2,1,0:T(8,128)S(1)}, u32[]{:S(2)}, u32[]{:S(2)}) collective-permute-start(f32[3,3,32,128]{3,2,1,0:T(8,128)S(1)} %get-tuple-element.6), channel_id=1, source_target_pairs={{1,0},{2,1},{3,2},{4,3},{5,4},{6,5},{7,6},{8,7},{9,8},{10,9},{11,1... | collective-permute-start | bytes 442376 | tf_op jit(solution)/shard_map/ppermute | solution.py:316
  14.2 4.0 %collective-permute-start = (f32[3,3,32,128]{3,2,1,0:T(8,128)S(1)}, f32[3,3,32,128]{3,2,1,0:T(8,128)S(1)}, u32[]{:S(2)}, u32[]{:S(2)}) collective-permute-start(f32[3,3,32,128]{3,2,1,0:T(8,128)S(1)} %get-tuple-element.7), channel_id=1, source_target_pairs={{0,1},{1,2},{2,3},{3,4},{4,5},{5,6},{6,7},{7,8},{8,9},{9,10},{10,1... | collective-permute-start | bytes 442376 | tf_op jit(solution)/shard_map/ppermute | solution.py:315
  20.9 0.9 %copy-start = (f32[3,4,32,128]{3,2,1,0:T(8,128)S(1)}, f32[3,4,32,128]{3,2,1,0:T(8,128)}, u32[]{:S(2)}) copy-start(f32[3,4,32,128]{3,2,1,0:T(8,128)} %cond_ref.1) | copy-start | bytes 589828
  30.9 1.9 %collective-permute-start.2 = (f32[16,128]{1,0:T(8,128)S(1)}, f32[16,128]{1,0:T(8,128)S(1)}, u32[]{:S(2)}, u32[]{:S(2)}) collective-permute-start(f32[16,128]{1,0:T(8,128)S(1)} %get-tuple-element.4), channel_id=1, source_target_pairs={{0,1},{1,0},{2,3},{3,2},{4,5},{5,4},{6,7},{7,6},{8,9},{9,8},{10,11... | collective-permute-start | bytes 24584 | tf_op jit(solution)/shard_map/ppermute | solution.py:351
  32.8 4.3 %collective-permute-start.3 = (f32[16,128]{1,0:T(8,128)S(1)}, f32[16,128]{1,0:T(8,128)S(1)}, u32[]{:S(2)}, u32[]{:S(2)}) collective-permute-start(f32[16,128]{1,0:T(8,128)S(1)} %add.12), channel_id=1, source_target_pairs={{0,2},{1,3},{2,0},{3,1},{4,6},{5,7},{6,4},{7,5},{8,10},{9,11},{10,... | collective-permute-start | bytes 24584 | tf_op jit(solution)/shard_map/ppermute | solution.py:351
  37.1 4.7 %collective-permute-start.4 = (f32[16,128]{1,0:T(8,128)S(1)}, f32[16,128]{1,0:T(8,128)S(1)}, u32[]{:S(2)}, u32[]{:S(2)}) collective-permute-start(f32[16,128]{1,0:T(8,128)S(1)} %add.13), channel_id=1, source_target_pairs={{0,4},{1,5},{2,6},{3,7},{4,0},{5,1},{6,2},{7,3},{8,12},{9,13},{10,... | collective-permute-start | bytes 24584 | tf_op jit(solution)/shard_map/ppermute | solution.py:351
  41.9 4.5 %collective-permute-start.5 = (f32[16,128]{1,0:T(8,128)S(1)}, f32[16,128]{1,0:T(8,128)S(1)}, u32[]{:S(2)}, u32[]{:S(2)}) collective-permute-start(f32[16,128]{1,0:T(8,128)S(1)} %add.14), channel_id=1, source_target_pairs={{0,8},{1,9},{2,10},{3,11},{4,12},{5,13},{6,14},{7,15},{8,0},{9,1},... | collective-permute-start | bytes 24584 | tf_op jit(solution)/shard_map/ppermute | solution.py:351

commit v2 on v1

v2 whole, which is shorter than its diff:
```python
import functools

import jax
import jax.numpy as jnp
from jax import lax
from jax.experimental import pallas as pl
from jax.experimental.pallas import tpu as pltpu
from jax.sharding import PartitionSpec as P

ITERS = 4
CENTRE = 5.0
RADIUS = 5.0
BASIS = ITERS + 1
FORMS = 2 * ITERS
PAIRS = [(i // 2, (i + 1) // 2) for i in range(FORMS)]
HALO = ITERS - 1
VMEM_LIMIT = 40 * 1024 * 1024
FULL_LIMIT = 62 * 1024 * 1024
CONTRACT_LANES = (((1,), (1,)), ((), ()))


def vmem():
    return pl.BlockSpec(memory_space=pltpu.VMEM)


def hbm():
    return pl.BlockSpec(memory_space=pltpu.HBM)


def split_bf16(x):
    high = x.astype(jnp.bfloat16)
    return high, (x - high.astype(jnp.float32)).astype(jnp.bfloat16)


def bin_kernel(n, half, rows, cols, half_depth, *refs):
    count = len(refs) // 2 - 1
    sources, out_ref, held, arrived = refs[:count], refs[count], refs[count + 1 : -1], refs[-1]
    copies = [pltpu.make_async_copy(sources[i], held[i], arrived.at[i]) for i in range(count)]
    for copy in copies:
        copy.start()
    for copy in copies:
        copy.wait()
    owner_ref, cell_ref, code_ref, value_ref = held
    sites = owner_ref.shape[1]
    owner = owner_ref[...]
    code = code_ref[...]
    dx = (code >= 9).astype(jnp.int32) + (code >= 18).astype(jnp.int32)
    rest = code - 9 * dx
    dy = (rest >= 3).astype(jnp.int32) + (rest >= 6).astype(jnp.int32)
    dz = rest - 3 * dy
    x = cell_ref[0:1] + dx
    y = cell_ref[1:2] + dy
    z = cell_ref[2:3] + dz
    upper = (x >= half_depth).astype(jnp.int32)
    folds = rows // 8
    row = (x - half_depth * upper) * rows + (y % folds) * 8 + y // folds
    lane = z + cols * upper
    channels, points = value_ref.shape[0], value_ref.shape[1]
    data = jnp.concatenate(
        [value_ref[...].reshape(channels * points, sites), row.astype(jnp.float32), lane.astype(jnp.float32)],
        axis=0,
    )
    blank = jnp.zeros_like(data)

    named = lax.broadcasted_iota(jnp.int32, (n, sites), 0) == owner
    earlier = lax.broadcasted_iota(jnp.int32, (sites, sites), 0) < lax.broadcasted_iota(
        jnp.int32, (sites, sites), 1
    )
    named_f = named.astype(jnp.float32)
    counts = jnp.dot(
        named_f.astype(jnp.bfloat16),
        earlier.astype(jnp.float32).astype(jnp.bfloat16),
        preferred_element_type=jnp.float32,
    )
    rank = jnp.sum(counts * named_f, axis=0, keepdims=True).astype(jnp.int32)
    second = rank >= half
    place = jnp.where(second, rank - half, rank)

    slot = lax.broadcasted_iota(jnp.int32, (out_ref.shape[0], sites), 0)
    hit = jnp.zeros(slot.shape, jnp.bool_)
    for j in range(3):
        hit = hit | (slot == ((owner - j + 1) * 3 + j) * half + place)
    total = jnp.zeros(out_ref.shape, jnp.float32)
    for part, stacked in (
        (jnp.logical_not(second), [data, blank]),
        (second, [blank, data]),
    ):
        chosen = jnp.where(hit & part, 1.0, 0.0).astype(jnp.bfloat16)
        for piece in split_bf16(jnp.concatenate(stacked, axis=0)):
            total = total + lax.dot_general(
                chosen, piece, CONTRACT_LANES, preferred_element_type=jnp.float32
            )
    out_ref[...] = total


def field_kernel(n, recv_ref, coupling, forms_ref, basis, left, right):
    depth, folds, cols = basis.shape[2] // 3, basis.shape[3], basis.shape[5]
    rows = 8 * folds
    half_depth = depth // 2
    channels = 6
    points = 8
    group = recv_ref.shape[1] // 3
    me = lax.axis_index("gx")
    keep_low = jnp.where(me > 0, 1.0, 0.0).astype(jnp.float32)
    keep_high = jnp.where(me < n - 1, 1.0, 0.0).astype(jnp.float32)

    row_count = half_depth * rows
    lane_count = 2 * cols
    slots = 2 * recv_ref.shape[0] * group
    width = (channels + 2) * points
    row_iota = lax.broadcasted_iota(jnp.int32, (row_count, slots), 0)
    lane_iota = lax.broadcasted_iota(jnp.int32, (lane_count, slots), 0)

    def scatter(j, _):
        packed = recv_ref[:, pl.ds(pl.multiple_of(j * group, 8), group), :].reshape(slots // 2, 2 * width)
        turned = packed.T
        table = jnp.concatenate([turned[:width], turned[width:]], axis=1)
        table_high = table.astype(jnp.bfloat16).astype(jnp.float32)
        table_low = table - table_high
        cell_row = table[channels * points : (channels + 1) * points].astype(jnp.int32)
        cell_lane = table[(channels + 1) * points :].astype(jnp.int32)
        for k in range(points):
            span = slice(k * slots, (k + 1) * slots)
            right[:, span] = jnp.where(lane_iota == cell_lane[k : k + 1], 1.0, 0.0).astype(jnp.bfloat16)
            mask = row_iota == cell_row[k : k + 1]
            for c in range(channels):
                at = c * points + k
                for piece, part in enumerate((table_high, table_low)):
                    first = (piece * channels + c) * row_count
                    left[first : first + row_count, span] = jnp.where(mask, part[at : at + 1], 0.0).astype(
                        jnp.bfloat16
                    )
        both = lax.dot_general(left[...], right[...], CONTRACT_LANES, preferred_element_type=jnp.float32)
        summed = both[: channels * row_count] + both[channels * row_count :]
        for c in range(channels):
            for x in range(depth):
                first = c * row_count + (x % half_depth) * rows
                lanes = slice((x // half_depth) * cols, (x // half_depth + 1) * cols)
                basis[1, c, j * depth + x] = summed[first : first + rows, lanes].reshape(folds, 8, cols)
        return 0

    lax.fori_loop(0, 3, scatter, 0)

    basis[0] = jnp.zeros(basis.shape[1:], jnp.float32)
    s_iota = lax.broadcasted_iota(jnp.int32, (8, cols), 0)
    z_iota = lax.broadcasted_iota(jnp.int32, (folds, 8, cols), 2)
    s_first, s_last = s_iota == 0, s_iota == 7
    z_first, z_last = z_iota == 0, z_iota == cols - 1

    def ahead_y(f):
        wrapped = jnp.where(s_last, 0.0, pltpu.roll(f[0], 7, 0))
        return jnp.concatenate([f[1:], wrapped[None]], axis=0) - f

    def ahead_z(f):
        return jnp.where(z_last, 0.0, pltpu.roll(f, cols - 1, 2)) - f

    def behind_y(f):
        wrapped = jnp.where(s_first, 0.0, pltpu.roll(f[folds - 1], 1, 0))
        return f - jnp.concatenate([wrapped[None], f[:-1]], axis=0)

    def behind_z(f):
        return f - jnp.where(z_first, 0.0, pltpu.roll(f, 1, 2))

    def faces(k, part, p):
        ex, ey, ez = (basis[k, 3 * part + q, p] for q in range(3))
        ey_next, ez_next = basis[k, 3 * part + 1, p + 1], basis[k, 3 * part + 2, p + 1]
        hx = ahead_y(ez) - ahead_z(ey)
        hy = ahead_z(ex) - (ez_next - ez)
        hz = (ey_next - ey) - ahead_y(ex)
        return hx, hy, hz, (ex, ey, ez)

    weight = 2.0 / RADIUS
    centre = 2.0 * CENTRE / RADIUS

    def plane(k, p, carried):
        result = []
        for part in range(2):
            hy_before, hz_before = carried[2 * part], carried[2 * part + 1]
            hx, hy, hz, edges = faces(k, part, p)
            curls = (
                behind_y(hz) - behind_z(hy),
                behind_z(hx) - (hz - hz_before),
                (hy - hy_before) - behind_y(hx),
            )
            for q in range(3):
                other = coupling[q, p - (depth - HALO)] * basis[k, 3 * (1 - part) + q, p]
                rest = centre * edges[q] + basis[k - 1, 3 * part + q, p]
                new = weight * curls[q] - rest
                basis[k + 1, 3 * part + q, p] = new + other if part == 0 else new - other
            result += [hy, hz]
        return tuple(result)

    def apply(k, _):
        start = []
        for part in range(2):
            _, hy, hz, _ = faces(k, part, k - 1)
            start += [hy, hz]

        def pair(i, carried):
            p = k + 2 * i
            for _ in range(2):
                keep = jnp.where(p == depth, keep_low, 1.0)
                carried = plane(k, p, tuple(keep * f for f in carried))
                p = p + 1
            return carried

        lax.fori_loop(0, (3 * depth - 2 * k) // 2, pair, tuple(start))
        for c in range(channels):
            basis[k + 1, c, 2 * depth] = basis[k + 1, c, 2 * depth] * keep_high
        return 0

    lax.fori_loop(1, BASIS, apply, 0)

    def plane_forms(p, sums):
        sums = list(sums)
        for q in range(3):
            re = [basis[k + 1, q, p] for k in range(BASIS)]
            im = [basis[k + 1, 3 + q, p] for k in range(BASIS)]
            for f, (i, j) in enumerate(PAIRS):
                real = re[i] * re[j] - im[i] * im[j]
                imag = re[i] * im[j] + im[i] * re[j] if i != j else 2.0 * (re[i] * im[i])
                for half, term in ((0, real), (1, imag)):
                    sums[2 * f + half] = sums[2 * f + half] + jnp.sum(term, axis=0)
        return tuple(sums)

    zero = jnp.zeros((8, cols), jnp.float32)
    sums = lax.fori_loop(depth, 2 * depth, plane_forms, (zero,) * (2 * FORMS))
    folded = jnp.concatenate([jnp.sum(total, axis=0, keepdims=True) for total in sums], axis=0)
    totals = jnp.sum(folded, axis=1, keepdims=True)
    diagonal = lax.broadcasted_iota(jnp.int32, folded.shape, 0) == lax.broadcasted_iota(jnp.int32, folded.shape, 1)
    line = jnp.sum(jnp.where(diagonal, totals, 0.0), axis=0, keepdims=True)
    forms_ref[...] = jnp.broadcast_to(line, forms_ref.shape)


def c_add(a, b):
    return a[0] + b[0], a[1] + b[1]


def c_sub(a, b):
    return a[0] - b[0], a[1] - b[1]


def c_mul(a, b):
    return a[0] * b[0] - a[1] * b[1], a[0] * b[1] + a[1] * b[0]


def c_scale(s, a):
    return s * a[0], s * a[1]


def c_div(a, b):
    inverse = 1.0 / (b[0] * b[0] + b[1] * b[1])
    return (a[0] * b[0] + a[1] * b[1]) * inverse, (a[1] * b[0] - a[0] * b[1]) * inverse


def step_scalars(moments):
    resid = list(moments)
    direc = list(moments)
    none = (jnp.zeros_like(moments[0][0]),) * 2
    one = (jnp.ones_like(moments[0][0]), jnp.zeros_like(moments[0][0]))
    resid_at = [one] + [none] * ITERS
    direc_at = [one] + [none] * ITERS
    field_at = [none] * BASIS
    rho = moments[0]
    for n in range(ITERS):
        applied = [c_add(c_scale(CENTRE, direc[0]), c_scale(RADIUS / 2, direc[1]))]
        for l in range(1, len(direc) - 1):
            near = c_scale(RADIUS / 2, c_add(direc[l + 1], direc[l - 1]))
            applied.append(c_add(c_scale(CENTRE, direc[l]), near))
        step = c_div(rho, c_mul(direc_at[n], applied[n]))
        applied_at = [c_scale(CENTRE, direc_at[j]) if j <= n else none for j in range(BASIS)]
        for j in range(n + 1):
            spread = c_scale(RADIUS / 2, direc_at[j])
            applied_at[j + 1] = c_add(applied_at[j + 1], spread)
            if j > 0:
                applied_at[j - 1] = c_add(applied_at[j - 1], spread)
        for j in range(n + 1):
            field_at[j] = c_add(field_at[j], c_mul(step, direc_at[j]))
        for j in range(n + 2):
            resid_at[j] = c_sub(resid_at[j], c_mul(step, applied_at[j]))
        if n + 1 < ITERS:
            resid = [c_sub(resid[l], c_mul(step, applied[l])) for l in range(len(applied))]
            rho_next = c_mul(resid_at[n + 1], resid[n + 1])
            ratio = c_div(rho_next, rho)
            direc = [c_add(resid[l], c_mul(ratio, direc[l])) for l in range(len(resid))]
            direc_at = [
                c_add(resid_at[j], c_mul(ratio, direc_at[j])) if j <= n else resid_at[j] for j in range(BASIS)
            ]
            rho = rho_next
    return field_at, resid_at


def combine_kernel(forms_ref, basis, field_ref, resid_ref):
    depth, folds, cols = basis.shape[2] // 3, basis.shape[3], basis.shape[5]
    totals = jnp.broadcast_to(jnp.sum(forms_ref[...], axis=0, keepdims=True), (8, cols))
    lane = lax.broadcasted_iota(jnp.int32, (8, cols), 1)
    sums = [
        jnp.broadcast_to(jnp.sum(jnp.where(lane == i, totals, 0.0), axis=1, keepdims=True), (8, cols))
        for i in range(2 * FORMS)
    ]
    forms = [(sums[2 * f], sums[2 * f + 1]) for f in range(FORMS)]
    moments = forms[:2] + [c_sub(forms[f], forms[f - 2]) for f in range(2, FORMS)]
    field_at, resid_at = step_scalars(moments)

    def plane(p, _):
        for q in range(3):
            for j in range(folds):
                re = [basis[k + 1, q, depth + p, j] for k in range(BASIS)]
                im = [basis[k + 1, 3 + q, depth + p, j] for k in range(BASIS)]
                rows = pl.ds(j, 8, stride=folds)
                for out_ref, factors in ((field_ref, field_at[:ITERS]), (resid_ref, resid_at)):
                    out_ref[q, p, rows] = sum(f[0] * re[k] - f[1] * im[k] for k, f in enumerate(factors))
                    out_ref[3 + q, p, rows] = sum(f[0] * im[k] + f[1] * re[k] for k, f in enumerate(factors))
        return 0

    lax.fori_loop(0, depth, plane, 0)


def params(limit=VMEM_LIMIT):
    return pltpu.CompilerParams(vmem_limit_bytes=limit)


def krylov(n, recv, coupling):
    depth, folds, cols = coupling.shape[1] - 2 * HALO, coupling.shape[2], coupling.shape[4]
    slots = 2 * recv.shape[0] * recv.shape[1] // 3
    return pl.pallas_call(
        functools.partial(field_kernel, n),
        out_shape=(
            jax.ShapeDtypeStruct((n, cols), jnp.float32),
            jax.ShapeDtypeStruct((BASIS + 1, 6, 3 * depth, folds, 8, cols), jnp.float32),
        ),
        in_specs=[vmem()] * 2,
        out_specs=(vmem(), vmem()),
        scratch_shapes=[
            pltpu.VMEM((2 * 6 * depth // 2 * 8 * folds, 8 * slots), jnp.bfloat16),
            pltpu.VMEM((2 * cols, 8 * slots), jnp.bfloat16),
        ],
        compiler_params=params(),
        name="krylov_basis",
    )(recv, coupling)


def per_device(n, site_owner, site_cell, stencil_code, site_residual, conductivity, omega):
    depth, rows, cols = conductivity.shape[1:]
    sites = site_owner.shape[0]
    cap = 2 * sites // n
    half = cap // 2
    listed = (site_owner.reshape(1, sites), site_cell, stencil_code, site_residual)
    packed = pl.pallas_call(
        functools.partial(bin_kernel, n, half, rows, cols, depth // 2),
        out_shape=jax.ShapeDtypeStruct((n * 3 * half, 2 * 8 * 8), jnp.float32),
        in_specs=[hbm()] * len(listed),
        out_specs=vmem(),
        scratch_shapes=[pltpu.VMEM(x.shape, x.dtype) for x in listed] + [pltpu.SemaphoreType.DMA((len(listed),))],
        compiler_params=params(FULL_LIMIT),
        name="bin_sites",
    )(*listed)
    mate = lax.ppermute(conductivity, "gx", [(i, i ^ 1) for i in range(n)])
    other = lax.ppermute(conductivity, "gx", [(i, ((i + 1) ^ 1) - 1) for i in range(1, n - 1)])
    even = lax.axis_index("gx") % 2 == 0
    below = jnp.where(even, other[:, depth - HALO :], mate[:, depth - HALO :])
    above = jnp.where(even, mate[:, :HALO], other[:, :HALO])
    coupling = jnp.concatenate([below, conductivity, above], axis=1) * (omega[0] * (2.0 / RADIUS))
    coupling = coupling.reshape(3, 2 * HALO + depth, 8, rows // 8, cols).swapaxes(2, 3)
    recv = lax.all_to_all(packed.reshape(n, 3 * half, -1), "gx", 0, 0)
    if half % 8:
        recv = recv.reshape(n, 3, half, -1).transpose(1, 0, 2, 3).reshape(1, 3 * n * half, -1)

    forms, basis = krylov(n, recv, coupling)

    forms = lax.all_to_all(forms, "gx", 0, 0, tiled=True)

    return pl.pallas_call(
        combine_kernel,
        out_shape=(jax.ShapeDtypeStruct((6, depth, rows, cols), jnp.float32),) * 2,
        in_specs=[vmem()] * 2,
        out_specs=(vmem(), vmem()),
        compiler_params=params(),
        name="combine_basis",
    )(forms, basis)


def solution(mesh):
    placed = (
        P(("period", "gx")),
        P(None, ("period", "gx")),
        P(None, ("period", "gx")),
        P(None, None, ("period", "gx")),
        P(None, "gx", None, None),
        P("period"),
    )
    return jax.shard_map(
        functools.partial(per_device, mesh.shape["gx"]),
        mesh=mesh,
        in_specs=placed,
        out_specs=(P("period", "gx", None, None), P("period", "gx", None, None)),
        check_vma=False,
    )
```

time: 48.4 us -> 40.5 us (0.84)
  starting transfers between devices: 21.5 us -> 10.1 us
  blocking collectives: 0 us -> 8.97 us
  local copies, waits for them, and re-layouts: 4.69 us -> 0.97 us
  waiting for transfers between devices: 8.69 us -> 7.25 us
    ppermute x6 -> x2, starting transfers between devices: 14.1 us -> 5.06 us  [the longest x1 4.38 us: per_device(): mate = lax.ppermute(conductivity, 'gx', [(i, i ^ 1) for i in range(n)])]
    all_to_all x0 -> x1, blocking collectives: none -> 8.97 us  [per_device(): forms = lax.all_to_all(forms, 'gx', 0, 0, tiled=True)]
    ppermute x6 -> x2, waiting for transfers between devices: 6.04 us -> 0.01 us  [the longest x1 0.01 us: per_device(): lax.ppermute(conductivity, 'gx', [(i, (i + 1 ^ 1) - 1) for i in range(1,...]
    all_to_all x1, waiting for transfers between devices: 2.65 us -> 7.24 us  [per_device(): recv = lax.all_to_all(packed.reshape(n, 3 * half, -1), 'gx', 0, 0)]
    unnamed x10 -> x0, local copies, waits for them, and re-layouts: 3.68 us -> none
    all_to_all x1, starting transfers between devices: 7.39 us -> 5 us  [per_device(): recv = lax.all_to_all(packed.reshape(n, 3 * half, -1), 'gx', 0, 0)]
    pallas_call x1, Pallas kernels: 9.09 us -> 7.99 us  [krylov(): pl.pallas_call(functools.partial(field_kernel, n), out_shape=(jax.ShapeDt...]
    slice x1 -> x0, local copies, waits for them, and re-layouts: 1.01 us -> none  [per_device(): conductivity[:, :halo]]
  transfers between devices with their start and end apart: 7 -> 3, of which waited for: 6 -> 1; matrix products, arithmetic and copies ran while one was open for 2% -> 3% of each run, Pallas kernels for 0% -> 5%
where the time goes in v2:
time: 40.5 us; the launch traced here: 40.1 us
  Pallas kernels  11.4 us (28%)
  starting transfers between devices  10.1 us (25%)
  blocking collectives  8.97 us (22%)
  waiting for transfers between devices  7.25 us (18%)
  between operations  1.37 us (3%)
  local copies, waits for them, and re-layouts  0.97 us (2%)
    all_to_all x1, blocking collectives, per_device(): forms = lax.all_to_all(forms, 'gx', 0, 0, tiled=True)  8.97 us
    pallas_call x1, Pallas kernels, krylov(): pl.pallas_call(functools.partial(field_kernel, n), out_shape=(jax.ShapeDt...  7.99 us
    all_to_all x1, waiting for transfers between devices, per_device(): recv = lax.all_to_all(packed.reshape(n, 3 * half, -1), 'gx', 0, 0)  7.24 us
    all_to_all x1, starting transfers between devices, per_device(): recv = lax.all_to_all(packed.reshape(n, 3 * half, -1), 'gx', 0, 0)  5 us
    ppermute x1, starting transfers between devices, per_device(): mate = lax.ppermute(conductivity, 'gx', [(i, i ^ 1) for i in range(n)])  4.38 us
    pallas_call x1, Pallas kernels, per_device(): pl.pallas_call(functools.partial(bin_kernel, n, half, rows, cols, depth /...  1.91 us
    pallas_call x1, Pallas kernels, per_device(): pl.pallas_call(combine_kernel, out_shape=(jax.ShapeDtypeStruct((6, depth,...  1.54 us
    concatenate x3, local copies, waits for them, and re-layouts, per_device(): jnp.concatenate([below, conductivity, above], axis=1)  0.97 us
  transfers between devices with their start and end apart: 3, of which 1 were waited for; matrix products, arithmetic and copies ran while one was open for 3% of the time, Pallas kernels for 5%

profile of v2, /device:TPU:0, one launch (start us, length us, event | category | flops | bytes accessed | tf_op | source)
XLA Modules:
  0.0 40.1 jit_solution(8441869088419603079)
XLA Ops:
  0.6 0.7 %collective-permute-start = (f32[3,4,32,128]{3,2,1,0:T(8,128)}, f32[3,4,32,128]{3,2,1,0:T(8,128)S(1)}, u32[]{:S(2)}, u32[]{:S(2)}) collective-permute-start(f32[3,4,32,128]{3,2,1,0:T(8,128)} %param.10), channel_id=1, source_target_pairs={{1,2},{2,1},{3,4},{4,3},{5,6},{6,5},{7,8},{8,7},{9,10},{10,9},{11,... | collective-permute-start | bytes 589832 | tf_op jit(solution)/shard_map/ppermute | solution.py:359
  1.3 4.4 %collective-permute-start.1 = (f32[3,4,32,128]{3,2,1,0:T(8,128)}, f32[3,4,32,128]{3,2,1,0:T(8,128)S(1)}, u32[]{:S(2)}, u32[]{:S(2)}) collective-permute-start(f32[3,4,32,128]{3,2,1,0:T(8,128)} %param.10), channel_id=1, source_target_pairs={{0,1},{1,0},{2,3},{3,2},{4,5},{5,4},{6,7},{7,6},{8,9},{9,8},{10,11... | collective-permute-start | bytes 589832 | tf_op jit(solution)/shard_map/ppermute | solution.py:358
  5.7 1.9 %bin_sites.1 = f32[384,128]{1,0:T(8,128)} custom-call(s32[1,128]{1,0:T(1,128)} %bitcast.18, s32[3,128]{1,0:T(4,128)} %refs_1_.1, s32[8,128]{1,0:T(8,128)} %refs_2_.1, f32[6,8,128]{2,1,0:T(8,128)} %refs_3_.1), custom_call_target="tpu_custom_call" | custom-call | tf_op jit(solution)/shard_map/bin_sites/pallas_call | solution.py:349
  7.6 5.0 %all-to-all-start = ((f32[16,24,128]{2,1,0:T(8,128)}), f32[16,24,128]{2,1,0:T(8,128)S(1)}, u32[]{:S(2)}, u32[]{:S(2)}) async-start(f32[16,24,128]{2,1,0:T(8,128)} %bitcast.14), calls=%async_computation | async-start | bytes 393216 | tf_op jit(solution)/shard_map/all_to_all | solution.py:365
  13.3 0.9 %copy.12 = f32[3,4,8,4,128]{4,2,3,1,0:T(8,128)S(1)} copy(f32[3,4,8,4,128]{4,3,2,1,0:T(4,128)} %bitcast.17) | data formatting | bytes 393216 | tf_op jit(solution)/shard_map/concatenate | solution.py:363
  14.2 0.0 collective-permute-done
  14.2 0.0 collective-permute-done.1
  14.4 7.2 %all-to-all-done.recv_ref = f32[16,24,128]{2,1,0:T(8,128)S(1)} async-done(((f32[16,24,128]{2,1,0:T(8,128)}), f32[16,24,128]{2,1,0:T(8,128)S(1)}, u32[]{:S(2)}, u32[]{:S(2)}) %all-to-all-start) | async-done | bytes 196640 | tf_op jit(solution)/shard_map/all_to_all | solution.py:365
  21.6 8.0 %krylov_basis.1 = (f32[16,128]{1,0:T(8,128)S(1)}, f32[6,6,12,4,8,128]{5,4,3,2,1,0:T(8,128)S(1)}) custom-call(f32[16,24,128]{2,1,0:T(8,128)S(1)} %all-to-all-done.recv_ref, f32[3,10,4,8,128]{4,3,2,1,0:T(8,128)S(1)} %fusion.coupling), custom_call_target="tpu_custom_call" | custom-call | tf_op jit(solution)/shard_map/krylov_basis/pallas_call | solution.py:326
  29.6 9.0 %all_to_all.16 = f32[16,1,128]{2,1,0:T(1,128)S(1)} all-to-all(f32[16,1,128]{2,1,0:T(1,128)S(1)} %bitcast.13), channel_id=1, replica_groups=mesh['period'=2,'gx'=16] {'gx'}, dimensions={0} | all-to-all | bytes 16384 | tf_op jit(solution)/shard_map/all_to_all | solution.py:371
  38.6 1.5 %combine_basis.1 = (f32[6,4,32,128]{3,2,1,0:T(8,128)}, f32[6,4,32,128]{3,2,1,0:T(8,128)}) custom-call(f32[16,128]{1,0:T(8,128)S(1)} %bitcast.12, f32[6,6,12,4,8,128]{5,4,3,2,1,0:T(8,128)S(1)} %get-tuple-element.5.basis), custom_call_target="tpu_custom_call" | custom-call | tf_op jit(solution)/shard_map/combine_basis/pallas_call | solution.py:373
  (4 shorter events, 0.1 us)
Async XLA Ops:
  0.6 13.6 %collective-permute-start = (f32[3,4,32,128]{3,2,1,0:T(8,128)}, f32[3,4,32,128]{3,2,1,0:T(8,128)S(1)}, u32[]{:S(2)}, u32[]{:S(2)}) collective-permute-start(f32[3,4,32,128]{3,2,1,0:T(8,128)} %param.10), channel_id=1, source_target_pairs={{1,2},{2,1},{3,4},{4,3},{5,6},{6,5},{7,8},{8,7},{9,10},{10,9},{11,... | collective-permute-start | bytes 589832 | tf_op jit(solution)/shard_map/ppermute | solution.py:359
  1.3 12.9 %collective-permute-start.1 = (f32[3,4,32,128]{3,2,1,0:T(8,128)}, f32[3,4,32,128]{3,2,1,0:T(8,128)S(1)}, u32[]{:S(2)}, u32[]{:S(2)}) collective-permute-start(f32[3,4,32,128]{3,2,1,0:T(8,128)} %param.10), channel_id=1, source_target_pairs={{0,1},{1,0},{2,3},{3,2},{4,5},{5,4},{6,7},{7,6},{8,9},{9,8},{10,11... | collective-permute-start | bytes 589832 | tf_op jit(solution)/shard_map/ppermute | solution.py:358
  7.6 14.0 %all-to-all-start = ((f32[16,24,128]{2,1,0:T(8,128)}), f32[16,24,128]{2,1,0:T(8,128)S(1)}, u32[]{:S(2)}, u32[]{:S(2)}) async-start(f32[16,24,128]{2,1,0:T(8,128)} %bitcast.14), calls=%async_computation | async-start | bytes 393216 | tf_op jit(solution)/shard_map/all_to_all | solution.py:365

commit v3 on v2

--- a/solution.py
+++ b/solution.py
@@ -21,6 +21,10 @@
 
 def vmem():
     return pl.BlockSpec(memory_space=pltpu.VMEM)
+
+
+def smem():
+    return pl.BlockSpec(memory_space=pltpu.SMEM)
 
 
 def hbm():
@@ -93,17 +97,16 @@
     out_ref[...] = total
 
 
-def field_kernel(n, recv_ref, coupling, forms_ref, basis, left, right):
+def scatter_kernel(recv_ref, cond_hbm, omega_ref, basis, mine_ref, left, right, cond_ref, arrived):
+    conductivity = pltpu.make_async_copy(cond_hbm, cond_ref, arrived)
+    conductivity.start()
     depth, folds, cols = basis.shape[2] // 3, basis.shape[3], basis.shape[5]
     rows = 8 * folds
     half_depth = depth // 2
     channels = 6
     points = 8
     group = recv_ref.shape[1] // 3
-    me = lax.axis_index("gx")
-    keep_low = jnp.where(me > 0, 1.0, 0.0).astype(jnp.float32)
-    keep_high = jnp.where(me < n - 1, 1.0, 0.0).astype(jnp.float32)
-
+    basis[0] = jnp.zeros(basis.shape[1:], jnp.float32)
     row_count = half_depth * rows
     lane_count = 2 * cols
     slots = 2 * recv_ref.shape[0] * group
@@ -141,7 +144,34 @@
 
     lax.fori_loop(0, 3, scatter, 0)
 
-    basis[0] = jnp.zeros(basis.shape[1:], jnp.float32)
+    conductivity.wait()
+    scale = omega_ref[0] * (2.0 / RADIUS)
+    for q in range(3):
+        for j in range(folds):
+            for x in range(depth):
+                mine_ref[q, x, j] = cond_ref[q, x, pl.ds(j, 8, stride=folds)] * scale
+
+
+def field_kernel(n, mate_ref, other_ref, mine_ref, omega_ref, _, forms_ref, basis, coupling):
+    depth, folds, cols = basis.shape[2] // 3, basis.shape[3], basis.shape[5]
+    channels = 6
+    me = lax.axis_index("gx")
+    keep_low = jnp.where(me > 0, 1.0, 0.0).astype(jnp.float32)
+    keep_high = jnp.where(me < n - 1, 1.0, 0.0).astype(jnp.float32)
+
+    scale = omega_ref[0] * (2.0 / RADIUS)
+    even = me % 2 == 0
+    for q in range(3):
+        coupling[q, HALO : HALO + depth] = mine_ref[q]
+        for j in range(folds):
+            fold = pl.ds(j, 8, stride=folds)
+            for i in range(HALO):
+                below, above = depth - HALO + i, i
+                coupling[q, i, j] = jnp.where(even, other_ref[q, below, fold], mate_ref[q, below, fold]) * scale
+                coupling[q, HALO + depth + i, j] = (
+                    jnp.where(even, mate_ref[q, above, fold], other_ref[q, above, fold]) * scale
+                )
+
     s_iota = lax.broadcasted_iota(jnp.int32, (8, cols), 0)
     z_iota = lax.broadcasted_iota(jnp.int32, (folds, 8, cols), 2)
     s_first, s_last = s_iota == 0, s_iota == 7
@@ -161,50 +191,60 @@
     def behind_z(f):
         return f - jnp.where(z_first, 0.0, pltpu.roll(f, 1, 2))
 
-    def faces(k, part, p):
-        ex, ey, ez = (basis[k, 3 * part + q, p] for q in range(3))
-        ey_next, ez_next = basis[k, 3 * part + 1, p + 1], basis[k, 3 * part + 2, p + 1]
+    weight = 2.0 / RADIUS
+    centre = 2.0 * CENTRE / RADIUS
+
+    def edges(k, p):
+        return [basis[k, c, p] for c in range(channels)]
+
+    def faces(here, there, part):
+        ex, ey, ez = here[3 * part : 3 * part + 3]
+        ey_next, ez_next = there[3 * part + 1], there[3 * part + 2]
         hx = ahead_y(ez) - ahead_z(ey)
         hy = ahead_z(ex) - (ez_next - ez)
         hz = (ey_next - ey) - ahead_y(ex)
-        return hx, hy, hz, (ex, ey, ez)
-
-    weight = 2.0 / RADIUS
-    centre = 2.0 * CENTRE / RADIUS
-
-    def plane(k, p, carried):
-        result = []
+        return hx, hy, hz
+
+    def plane(here, there, older, coupled, carried):
+        new, result = [], []
         for part in range(2):
             hy_before, hz_before = carried[2 * part], carried[2 * part + 1]
-            hx, hy, hz, edges = faces(k, part, p)
+            hx, hy, hz = faces(here, there, part)
             curls = (
                 behind_y(hz) - behind_z(hy),
                 behind_z(hx) - (hz - hz_before),
                 (hy - hy_before) - behind_y(hx),
             )
             for q in range(3):
-                other = coupling[q, p - (depth - HALO)] * basis[k, 3 * (1 - part) + q, p]
-                rest = centre * edges[q] + basis[k - 1, 3 * part + q, p]
-                new = weight * curls[q] - rest
-                basis[k + 1, 3 * part + q, p] = new + other if part == 0 else new - other
+                other = coupled[q] * here[3 * (1 - part) + q]
+                value = weight * curls[q] - (centre * here[3 * part + q] + older[3 * part + q])
+                new.append(value + other if part == 0 else value - other)
             result += [hy, hz]
-        return tuple(result)
+        return new, tuple(result)
 
     def apply(k, _):
+        first, second = edges(k, k - 1), edges(k, k)
         start = []
         for part in range(2):
-            _, hy, hz, _ = faces(k, part, k - 1)
-            start += [hy, hz]
-
-        def pair(i, carried):
+            start += faces(first, second, part)[1:]
+
+        def step(i, carried):
             p = k + 2 * i
-            for _ in range(2):
-                keep = jnp.where(p == depth, keep_low, 1.0)
-                carried = plane(k, p, tuple(keep * f for f in carried))
-                p = p + 1
+            fields = [edges(k, p + d) for d in range(2 + 1)]
+            older = [edges(k - 1, p + d) for d in range(2)]
+            coupled = [[coupling[q, p + d - (depth - HALO)] for q in range(3)] for d in range(2)]
+            results = []
+            for d in range(2):
+                keep = jnp.where(p + d == depth, keep_low, 1.0)
+                carried = tuple(keep * f for f in carried)
+                new, carried = plane(fields[d], fields[d + 1], older[d], coupled[d], carried)
+                results.append(new)
+            for d in range(2):
+                for c in range(channels):
+                    basis[k + 1, c, p + d] = results[d][c]
             return carried
 
-        lax.fori_loop(0, (3 * depth - 2 * k) // 2, pair, tuple(start))
+        lax.fori_loop(0, (3 * depth - 2 * k) // 2, step, tuple(start))
         for c in range(channels):
             basis[k + 1, c, 2 * depth] = basis[k + 1, c, 2 * depth] * keep_high
         return 0
@@ -320,24 +360,38 @@
     return pltpu.CompilerParams(vmem_limit_bytes=limit)
 
 
-def krylov(n, recv, coupling):
-    depth, folds, cols = coupling.shape[1] - 2 * HALO, coupling.shape[2], coupling.shape[4]
+def krylov(n, recv, mate, other, conductivity, omega):
+    depth, folds, cols = conductivity.shape[1], conductivity.shape[2] // 8, conductivity.shape[3]
     slots = 2 * recv.shape[0] * recv.shape[1] // 3
+    left_rows, right_rows = 2 * 6 * depth // 2 * 8 * folds, 2 * cols
+    bases = jax.ShapeDtypeStruct((BASIS + 1, 6, 3 * depth, folds, 8, cols), jnp.float32)
+    basis, mine = pl.pallas_call(
+        scatter_kernel,
+        out_shape=(bases, jax.ShapeDtypeStruct((3, depth, folds, 8, cols), jnp.float32)),
+        in_specs=[vmem(), hbm(), smem()],
+        out_specs=(vmem(), vmem()),
+        scratch_shapes=[
+            pltpu.VMEM((left_rows, 8 * slots), jnp.bfloat16),
+            pltpu.VMEM((right_rows, 8 * slots), jnp.bfloat16),
+            pltpu.VMEM(conductivity.shape, jnp.float32),
+            pltpu.SemaphoreType.DMA,
+        ],
+        cost_estimate=pl.CostEstimate(
+            flops=6 * left_rows * right_rows * 8 * slots, bytes_accessed=4 * 1024 * 1024, transcendentals=0
+        ),
+        compiler_params=params(),
+        name="scatter_source",
+    )(recv, pltpu.with_memory_space_constraint(conductivity, pltpu.HBM), omega)
     return pl.pallas_call(
         functools.partial(field_kernel, n),
-        out_shape=(
-            jax.ShapeDtypeStruct((n, cols), jnp.float32),
-            jax.ShapeDtypeStruct((BASIS + 1, 6, 3 * depth, folds, 8, cols), jnp.float32),
-        ),
-        in_specs=[vmem()] * 2,
+        out_shape=(jax.ShapeDtypeStruct((n, cols), jnp.float32), bases),
+        in_specs=[vmem()] * 3 + [smem(), vmem()],
         out_specs=(vmem(), vmem()),
-        scratch_shapes=[
-            pltpu.VMEM((2 * 6 * depth // 2 * 8 * folds, 8 * slots), jnp.bfloat16),
-            pltpu.VMEM((2 * cols, 8 * slots), jnp.bfloat16),
-        ],
+        scratch_shapes=[pltpu.VMEM((3, 2 * HALO + depth, folds, 8, cols), jnp.float32)],
+        input_output_aliases={4: 1},
         compiler_params=params(),
         name="krylov_basis",
-    )(recv, coupling)
+    )(mate, other, mine, omega, basis)
 
 
 def per_device(n, site_owner, site_cell, stencil_code, site_residual, conductivity, omega):
@@ -352,21 +406,16 @@
         in_specs=[hbm()] * len(listed),
         out_specs=vmem(),
         scratch_shapes=[pltpu.VMEM(x.shape, x.dtype) for x in listed] + [pltpu.SemaphoreType.DMA((len(listed),))],
-        compiler_params=params(FULL_LIMIT),
+        compiler_params=params(),
         name="bin_sites",
-    )(*listed)
+    )(*(pltpu.with_memory_space_constraint(x, pltpu.HBM) for x in listed))
     mate = lax.ppermute(conductivity, "gx", [(i, i ^ 1) for i in range(n)])
     other = lax.ppermute(conductivity, "gx", [(i, ((i + 1) ^ 1) - 1) for i in range(1, n - 1)])
-    even = lax.axis_index("gx") % 2 == 0
-    below = jnp.where(even, other[:, depth - HALO :], mate[:, depth - HALO :])
-    above = jnp.where(even, mate[:, :HALO], other[:, :HALO])
-    coupling = jnp.concatenate([below, conductivity, above], axis=1) * (omega[0] * (2.0 / RADIUS))
-    coupling = coupling.reshape(3, 2 * HALO + depth, 8, rows // 8, cols).swapaxes(2, 3)
     recv = lax.all_to_all(packed.reshape(n, 3 * half, -1), "gx", 0, 0)
     if half % 8:
         recv = recv.reshape(n, 3, half, -1).transpose(1, 0, 2, 3).reshape(1, 3 * n * half, -1)
 
-    forms, basis = krylov(n, recv, coupling)
+    forms, basis = krylov(n, recv, mate, other, conductivity, omega)
 
     forms = lax.all_to_all(forms, "gx", 0, 0, tiled=True)
 

time: 40.5 us -> 36.9 us (0.911)
  starting transfers between devices: 10.1 us -> 8.46 us
  local copies, waits for them, and re-layouts: 0.97 us -> 0 us
  Pallas kernels: 11.4 us -> 10.5 us
    pallas_call x1, Pallas kernels: 7.99 us -> 3.64 us  [krylov(): pl.pallas_call(functools.partial(field_kernel, n), out_shape=(jax.ShapeDt...]
    ppermute x1, starting transfers between devices: 4.38 us -> 0.41 us  [per_device(): mate = lax.ppermute(conductivity, 'gx', [(i, i ^ 1) for i in range(n)])]
    pallas_call x0 -> x1, Pallas kernels: none -> 3.46 us  [krylov(): pl.pallas_call(scatter_kernel, out_shape=(bases, jax.ShapeDtypeStruct((3,...]
    all_to_all x1, starting transfers between devices: 5 us -> 7.39 us  [per_device(): recv = lax.all_to_all(packed.reshape(n, 3 * half, -1), 'gx', 0, 0)]
    concatenate x3 -> x0, local copies, waits for them, and re-layouts: 0.97 us -> none  [per_device(): jnp.concatenate([below, conductivity, above], axis=1)]
  transfers between devices with their start and end apart: 3 -> 3, of which waited for: 1 -> 1; matrix products, arithmetic and copies ran while one was open for 3% -> 0% of each run, Pallas kernels for 5% -> 9%
where the time goes in v3:
time: 36.9 us; the launch traced here: 36.6 us
  Pallas kernels  10.5 us (28%)
  blocking collectives  8.97 us (24%)
  starting transfers between devices  8.46 us (23%)
  waiting for transfers between devices  7.27 us (20%)
  between operations  1.33 us (4%)
    all_to_all x1, blocking collectives, per_device(): forms = lax.all_to_all(forms, 'gx', 0, 0, tiled=True)  8.97 us
    all_to_all x1, starting transfers between devices, per_device(): recv = lax.all_to_all(packed.reshape(n, 3 * half, -1), 'gx', 0, 0)  7.39 us
    all_to_all x1, waiting for transfers between devices, per_device(): recv = lax.all_to_all(packed.reshape(n, 3 * half, -1), 'gx', 0, 0)  7.27 us
    pallas_call x1, Pallas kernels, krylov(): pl.pallas_call(functools.partial(field_kernel, n), out_shape=(jax.ShapeDt...  3.64 us
    pallas_call x1, Pallas kernels, krylov(): pl.pallas_call(scatter_kernel, out_shape=(bases, jax.ShapeDtypeStruct((3,...  3.46 us
    pallas_call x1, Pallas kernels, per_device(): pl.pallas_call(functools.partial(bin_kernel, n, half, rows, cols, depth /...  1.91 us
    pallas_call x1, Pallas kernels, per_device(): pl.pallas_call(combine_kernel, out_shape=(jax.ShapeDtypeStruct((6, depth,...  1.54 us
  transfers between devices with their start and end apart: 3, of which 1 were waited for; matrix products, arithmetic and copies ran while one was open for 0% of the time, Pallas kernels for 9%

profile of v3, /device:TPU:0, one launch (start us, length us, event | category | flops | bytes accessed | tf_op | source)
XLA Modules:
  0.0 36.6 jit_solution(11487260175820160131)
XLA Ops:
  0.6 1.9 %bin_sites.1 = f32[384,128]{1,0:T(8,128)} custom-call(s32[1,128]{1,0:T(1,128)} %bitcast.8, s32[3,128]{1,0:T(4,128)} %refs_1_.1, s32[8,128]{1,0:T(8,128)} %refs_2_.1, f32[6,8,128]{2,1,0:T(8,128)} %refs_3_.1), custom_call_target="tpu_custom_call" | custom-call | tf_op jit(solution)/shard_map/bin_sites/pallas_call | solution.py:403
  2.6 7.4 %all-to-all-start = ((f32[16,24,128]{2,1,0:T(8,128)}), f32[16,24,128]{2,1,0:T(8,128)S(1)}, u32[]{:S(2)}, u32[]{:S(2)}) async-start(f32[16,24,128]{2,1,0:T(8,128)} %bitcast.1), calls=%async_computation | async-start | bytes 393216 | tf_op jit(solution)/shard_map/all_to_all | solution.py:414
  10.0 0.4 %collective-permute-start = (f32[3,4,32,128]{3,2,1,0:T(8,128)}, f32[3,4,32,128]{3,2,1,0:T(8,128)S(1)}, u32[]{:S(2)}, u32[]{:S(2)}) collective-permute-start(f32[3,4,32,128]{3,2,1,0:T(8,128)} %cond_hbm.1), channel_id=1, source_target_pairs={{0,1},{1,0},{2,3},{3,2},{4,5},{5,4},{6,7},{7,6},{8,9},{9,8},{10,11... | collective-permute-start | bytes 589832 | tf_op jit(solution)/shard_map/ppermute | solution.py:412
  10.4 0.7 %collective-permute-start.1 = (f32[3,4,32,128]{3,2,1,0:T(8,128)}, f32[3,4,32,128]{3,2,1,0:T(8,128)S(1)}, u32[]{:S(2)}, u32[]{:S(2)}) collective-permute-start(f32[3,4,32,128]{3,2,1,0:T(8,128)} %cond_hbm.1), channel_id=1, source_target_pairs={{1,2},{2,1},{3,4},{4,3},{5,6},{6,5},{7,8},{8,7},{9,10},{10,9},{11,... | collective-permute-start | bytes 589832 | tf_op jit(solution)/shard_map/ppermute | solution.py:413
  11.7 7.3 %all-to-all-done.recv_ref = f32[16,24,128]{2,1,0:T(8,128)S(1)} async-done(((f32[16,24,128]{2,1,0:T(8,128)}), f32[16,24,128]{2,1,0:T(8,128)S(1)}, u32[]{:S(2)}, u32[]{:S(2)}) %all-to-all-start) | async-done | bytes 196640 | tf_op jit(solution)/shard_map/all_to_all | solution.py:414
  18.9 3.5 %scatter_source.1 = (f32[6,6,12,4,8,128]{5,4,3,2,1,0:T(8,128)S(1)}, f32[3,4,4,8,128]{4,3,2,1,0:T(8,128)S(1)}) custom-call(f32[16,24,128]{2,1,0:T(8,128)S(1)} %all-to-all-done.recv_ref, f32[3,4,32,128]{3,2,1,0:T(8,128)} %cond_hbm.1, f32[1]{0:T(128)S(6)} %copy.11.omega_ref), custom_call_target="tpu_custom_call" | custom-call | flops 2415919104 | bytes 4194304 | tf_op jit(solution)/shard_map/scatter_source/pallas_call | solution.py:368
  22.4 0.0 collective-permute-done.mate_ref
  22.4 0.0 collective-permute-done.1.other_ref
  22.4 3.6 %krylov_basis.1 = (f32[16,128]{1,0:T(8,128)S(1)}, f32[6,6,12,4,8,128]{5,4,3,2,1,0:T(8,128)S(1)}) custom-call(f32[3,4,32,128]{3,2,1,0:T(8,128)S(1)} %collective-permute-done.mate_ref, f32[3,4,32,128]{3,2,1,0:T(8,128)S(1)} %collective-permute-done.1.other_ref, f32[3,4,4,8,128]{4,3,2,1,0:T(8,128)S(1)} %get-tuple-element.6.mine_ref, ...), custom_call_target="tpu_custom_call", output_to_operand_aliasing={{1}: (4, {})} | custom-call | tf_op jit(solution)/shard_map/krylov_basis/pallas_call | solution.py:385
  26.1 9.0 %all_to_all.16 = f32[16,1,128]{2,1,0:T(1,128)S(1)} all-to-all(f32[16,1,128]{2,1,0:T(1,128)S(1)} %bitcast.7), channel_id=1, replica_groups=mesh['period'=2,'gx'=16] {'gx'}, dimensions={0} | all-to-all | bytes 16384 | tf_op jit(solution)/shard_map/all_to_all | solution.py:420
  35.0 1.5 %combine_basis.1 = (f32[6,4,32,128]{3,2,1,0:T(8,128)}, f32[6,4,32,128]{3,2,1,0:T(8,128)}) custom-call(f32[16,128]{1,0:T(8,128)S(1)} %bitcast.6, f32[6,6,12,4,8,128]{5,4,3,2,1,0:T(8,128)S(1)} %get-tuple-element.9.basis), custom_call_target="tpu_custom_call" | custom-call | tf_op jit(solution)/shard_map/combine_basis/pallas_call | solution.py:422
Async XLA Ops:
  2.6 16.4 %all-to-all-start = ((f32[16,24,128]{2,1,0:T(8,128)}), f32[16,24,128]{2,1,0:T(8,128)S(1)}, u32[]{:S(2)}, u32[]{:S(2)}) async-start(f32[16,24,128]{2,1,0:T(8,128)} %bitcast.1), calls=%async_computation | async-start | bytes 393216 | tf_op jit(solution)/shard_map/all_to_all | solution.py:414
  10.0 12.5 %collective-permute-start = (f32[3,4,32,128]{3,2,1,0:T(8,128)}, f32[3,4,32,128]{3,2,1,0:T(8,128)S(1)}, u32[]{:S(2)}, u32[]{:S(2)}) collective-permute-start(f32[3,4,32,128]{3,2,1,0:T(8,128)} %cond_hbm.1), channel_id=1, source_target_pairs={{0,1},{1,0},{2,3},{3,2},{4,5},{5,4},{6,7},{7,6},{8,9},{9,8},{10,11... | collective-permute-start | bytes 589832 | tf_op jit(solution)/shard_map/ppermute | solution.py:412
  10.4 12.1 %collective-permute-start.1 = (f32[3,4,32,128]{3,2,1,0:T(8,128)}, f32[3,4,32,128]{3,2,1,0:T(8,128)S(1)}, u32[]{:S(2)}, u32[]{:S(2)}) collective-permute-start(f32[3,4,32,128]{3,2,1,0:T(8,128)} %cond_hbm.1), channel_id=1, source_target_pairs={{1,2},{2,1},{3,4},{4,3},{5,6},{6,5},{7,8},{8,7},{9,10},{10,9},{11,... | collective-permute-start | bytes 589832 | tf_op jit(solution)/shard_map/ppermute | solution.py:413

commit v4 on v3

--- a/solution.py
+++ b/solution.py
@@ -37,12 +37,13 @@
 
 
 def bin_kernel(n, half, rows, cols, half_depth, *refs):
-    count = len(refs) // 2 - 1
-    sources, out_ref, held, arrived = refs[:count], refs[count], refs[count + 1 : -1], refs[-1]
-    copies = [pltpu.make_async_copy(sources[i], held[i], arrived.at[i]) for i in range(count)]
+    sources, cond_hbm, out_ref, cut_ref, held, arrived = refs[:4], refs[4], refs[5], refs[6], refs[7:11], refs[11]
+    copies = [pltpu.make_async_copy(sources[i], held[i], arrived.at[i]) for i in range(4)]
+    first = (2 * half_depth - HALO) * (lax.axis_index("gx") % 2)
+    copies.append(pltpu.make_async_copy(cond_hbm.at[:, pl.ds(first, HALO)], cut_ref, arrived.at[4]))
     for copy in copies:
         copy.start()
-    for copy in copies:
+    for copy in copies[:4]:
         copy.wait()
     owner_ref, cell_ref, code_ref, value_ref = held
     sites = owner_ref.shape[1]
@@ -95,6 +96,7 @@
                 chosen, piece, CONTRACT_LANES, preferred_element_type=jnp.float32
             )
     out_ref[...] = total
+    copies[4].wait()
 
 
 def scatter_kernel(recv_ref, cond_hbm, omega_ref, basis, mine_ref, left, right, cond_ref, arrived):
@@ -142,7 +144,7 @@
                 basis[1, c, j * depth + x] = summed[first : first + rows, lanes].reshape(folds, 8, cols)
         return 0
 
-    lax.fori_loop(0, 3, scatter, 0)
+    lax.fori_loop(0, 3, scatter, 0, unroll=True)
 
     conductivity.wait()
     scale = omega_ref[0] * (2.0 / RADIUS)
@@ -152,7 +154,7 @@
                 mine_ref[q, x, j] = cond_ref[q, x, pl.ds(j, 8, stride=folds)] * scale
 
 
-def field_kernel(n, mate_ref, other_ref, mine_ref, omega_ref, _, forms_ref, basis, coupling):
+def field_kernel(n, mate_ref, other_ref, mine_ref, omega_ref, _, forms_ref, basis, coupling, faces):
     depth, folds, cols = basis.shape[2] // 3, basis.shape[3], basis.shape[5]
     channels = 6
     me = lax.axis_index("gx")
@@ -167,9 +169,9 @@
             fold = pl.ds(j, 8, stride=folds)
             for i in range(HALO):
                 below, above = depth - HALO + i, i
-                coupling[q, i, j] = jnp.where(even, other_ref[q, below, fold], mate_ref[q, below, fold]) * scale
+                coupling[q, i, j] = jnp.where(even, other_ref[q, i, fold], mate_ref[q, below, fold]) * scale
                 coupling[q, HALO + depth + i, j] = (
-                    jnp.where(even, mate_ref[q, above, fold], other_ref[q, above, fold]) * scale
+                    jnp.where(even, mate_ref[q, above, fold], other_ref[q, i, fold]) * scale
                 )
 
     s_iota = lax.broadcasted_iota(jnp.int32, (8, cols), 0)
@@ -197,19 +199,25 @@
     def edges(k, p):
         return [basis[k, c, p] for c in range(channels)]
 
-    def faces(here, there, part):
-        ex, ey, ez = here[3 * part : 3 * part + 3]
-        ey_next, ez_next = there[3 * part + 1], there[3 * part + 2]
-        hx = ahead_y(ez) - ahead_z(ey)
-        hy = ahead_z(ex) - (ez_next - ez)
-        hz = (ey_next - ey) - ahead_y(ex)
-        return hx, hy, hz
-
-    def plane(here, there, older, coupled, carried):
-        new, result = [], []
+    def faces_of(here, there):
+        result = []
         for part in range(2):
-            hy_before, hz_before = carried[2 * part], carried[2 * part + 1]
-            hx, hy, hz = faces(here, there, part)
+            ex, ey, ez = here[3 * part : 3 * part + 3]
+            ey_next, ez_next = there[3 * part + 1], there[3 * part + 2]
+            result.append(ahead_y(ez) - ahead_z(ey))
+            result.append(ahead_z(ex) - (ez_next - ez))
+            result.append((ey_next - ey) - ahead_y(ex))
+        return result
+
+    def keep_faces(p, values):
+        for c in range(channels):
+            faces[c, p] = values[c]
+
+    def plane(here, older, coupled, face, face_before):
+        new = []
+        for part in range(2):
+            hx, hy, hz = face[3 * part : 3 * part + 3]
+            hy_before, hz_before = face_before[2 * part], face_before[2 * part + 1]
             curls = (
                 behind_y(hz) - behind_z(hy),
                 behind_z(hx) - (hz - hz_before),
@@ -219,32 +227,38 @@
                 other = coupled[q] * here[3 * (1 - part) + q]
                 value = weight * curls[q] - (centre * here[3 * part + q] + older[3 * part + q])
                 new.append(value + other if part == 0 else value - other)
-            result += [hy, hz]
-        return new, tuple(result)
+        return new
+
+    last_pair = 3 * depth - 3
 
     def apply(k, _):
-        first, second = edges(k, k - 1), edges(k, k)
-        start = []
-        for part in range(2):
-            start += faces(first, second, part)[1:]
-
-        def step(i, carried):
+        first = [edges(k, k - 1 + d) for d in range(4)]
+        for d in range(3):
+            keep_faces(k - 1 + d, faces_of(first[d], first[d + 1]))
+
+        def step(i, _):
             p = k + 2 * i
-            fields = [edges(k, p + d) for d in range(2 + 1)]
+            ahead = jnp.minimum(p + 2, last_pair)
+            fields = [edges(k, p + d) for d in range(2)]
             older = [edges(k - 1, p + d) for d in range(2)]
             coupled = [[coupling[q, p + d - (depth - HALO)] for q in range(3)] for d in range(2)]
-            results = []
-            for d in range(2):
-                keep = jnp.where(p + d == depth, keep_low, 1.0)
-                carried = tuple(keep * f for f in carried)
-                new, carried = plane(fields[d], fields[d + 1], older[d], coupled[d], carried)
-                results.append(new)
+            face = [[faces[c, p + d] for c in range(channels)] for d in range(2)]
+            before = [faces[c, p - 1] * jnp.where(p == depth, keep_low, 1.0) for c in (1, 2, 4, 5)]
+            middle = [face[0][c] * jnp.where(p + 1 == depth, keep_low, 1.0) for c in (1, 2, 4, 5)]
+            following = [edges(k, ahead + d) for d in range(3)]
+            next_faces = [faces_of(following[d], following[d + 1]) for d in range(2)]
+            new = [
+                plane(fields[0], older[0], coupled[0], face[0], before),
+                plane(fields[1], older[1], coupled[1], face[1], middle),
+            ]
             for d in range(2):
                 for c in range(channels):
-                    basis[k + 1, c, p + d] = results[d][c]
-            return carried
-
-        lax.fori_loop(0, (3 * depth - 2 * k) // 2, step, tuple(start))
+                    basis[k + 1, c, p + d] = new[d][c]
+            for d in range(2):
+                keep_faces(ahead + d, next_faces[d])
+            return 0
+
+        lax.fori_loop(0, (3 * depth - 2 * k) // 2, step, 0)
         for c in range(channels):
             basis[k + 1, c, 2 * depth] = basis[k + 1, c, 2 * depth] * keep_high
         return 0
@@ -387,38 +401,19 @@
         out_shape=(jax.ShapeDtypeStruct((n, cols), jnp.float32), bases),
         in_specs=[vmem()] * 3 + [smem(), vmem()],
         out_specs=(vmem(), vmem()),
-        scratch_shapes=[pltpu.VMEM((3, 2 * HALO + depth, folds, 8, cols), jnp.float32)],
+        scratch_shapes=[
+            pltpu.VMEM((3, 2 * HALO + depth, folds, 8, cols), jnp.float32),
+            pltpu.VMEM((6, 3 * depth, folds, 8, cols), jnp.float32),
+        ],
         input_output_aliases={4: 1},
         compiler_params=params(),
         name="krylov_basis",
     )(mate, other, mine, omega, basis)
 
 
-def per_device(n, site_owner, site_cell, stencil_code, site_residual, conductivity, omega):
-    depth, rows, cols = conductivity.shape[1:]
-    sites = site_owner.shape[0]
-    cap = 2 * sites // n
-    half = cap // 2
-    listed = (site_owner.reshape(1, sites), site_cell, stencil_code, site_residual)
-    packed = pl.pallas_call(
-        functools.partial(bin_kernel, n, half, rows, cols, depth // 2),
-        out_shape=jax.ShapeDtypeStruct((n * 3 * half, 2 * 8 * 8), jnp.float32),
-        in_specs=[hbm()] * len(listed),
-        out_specs=vmem(),
-        scratch_shapes=[pltpu.VMEM(x.shape, x.dtype) for x in listed] + [pltpu.SemaphoreType.DMA((len(listed),))],
-        compiler_params=params(),
-        name="bin_sites",
-    )(*(pltpu.with_memory_space_constraint(x, pltpu.HBM) for x in listed))
-    mate = lax.ppermute(conductivity, "gx", [(i, i ^ 1) for i in range(n)])
-    other = lax.ppermute(conductivity, "gx", [(i, ((i + 1) ^ 1) - 1) for i in range(1, n - 1)])
-    recv = lax.all_to_all(packed.reshape(n, 3 * half, -1), "gx", 0, 0)
-    if half % 8:
-        recv = recv.reshape(n, 3, half, -1).transpose(1, 0, 2, 3).reshape(1, 3 * n * half, -1)
-
-    forms, basis = krylov(n, recv, mate, other, conductivity, omega)
-
-    forms = lax.all_to_all(forms, "gx", 0, 0, tiled=True)
-
+def combine(forms, basis):
+    depth, folds, cols = basis.shape[2] // 3, basis.shape[3], basis.shape[5]
+    rows = 8 * folds
     return pl.pallas_call(
         combine_kernel,
         out_shape=(jax.ShapeDtypeStruct((6, depth, rows, cols), jnp.float32),) * 2,
@@ -427,6 +422,37 @@
         compiler_params=params(),
         name="combine_basis",
     )(forms, basis)
+
+
+def per_device(n, site_owner, site_cell, stencil_code, site_residual, conductivity, omega):
+    depth, rows, cols = conductivity.shape[1:]
+    sites = site_owner.shape[0]
+    cap = 2 * sites // n
+    half = cap // 2
+    listed = (site_owner.reshape(1, sites), site_cell, stencil_code, site_residual)
+    packed, cut = pl.pallas_call(
+        functools.partial(bin_kernel, n, half, rows, cols, depth // 2),
+        out_shape=(
+            jax.ShapeDtypeStruct((n * 3 * half, 2 * 8 * 8), jnp.float32),
+            jax.ShapeDtypeStruct((3, HALO, rows, cols), jnp.float32),
+        ),
+        in_specs=[hbm()] * 5,
+        out_specs=(vmem(), vmem()),
+        scratch_shapes=[pltpu.VMEM(x.shape, x.dtype) for x in listed] + [pltpu.SemaphoreType.DMA((5,))],
+        compiler_params=params(),
+        name="bin_sites",
+    )(*(pltpu.with_memory_space_constraint(x, pltpu.HBM) for x in (*listed, conductivity)))
+    mate = lax.ppermute(conductivity, "gx", [(i, i ^ 1) for i in range(n)])
+    other = lax.ppermute(cut, "gx", [(i, ((i + 1) ^ 1) - 1) for i in range(1, n - 1)])
+    recv = lax.all_to_all(packed.reshape(n, 3 * half, -1), "gx", 0, 0)
+    if half % 8:
+        recv = recv.reshape(n, 3, half, -1).transpose(1, 0, 2, 3).reshape(1, 3 * n * half, -1)
+
+    forms, basis = krylov(n, recv, mate, other, conductivity, omega)
+
+    forms = lax.all_to_all(forms, "gx", 0, 0, tiled=True)
+
+    return combine(forms, basis)
 
 
 def solution(mesh):

time: 36.9 us -> 35.7 us (0.967)
  Pallas kernels: 10.5 us -> 9.4 us
    pallas_call x1, Pallas kernels: 3.46 us -> 2.76 us  [krylov(): pl.pallas_call(scatter_kernel, out_shape=(bases, jax.ShapeDtypeStruct((3,...]
    pallas_call x1, Pallas kernels: 3.64 us -> 3.18 us  [krylov(): pl.pallas_call(functools.partial(field_kernel, n), out_shape=(jax.ShapeDt...]
  transfers between devices with their start and end apart: 3 -> 3, of which waited for: 1 -> 1; matrix products, arithmetic and copies ran while one was open for 0% -> 0% of each run, Pallas kernels for 9% -> 8%
where the time goes in v4:
time: 35.7 us; the launch traced here: 35.4 us
  Pallas kernels  9.4 us (26%)
  blocking collectives  8.97 us (25%)
  starting transfers between devices  8.46 us (24%)
  waiting for transfers between devices  7.27 us (20%)
  between operations  1.33 us (4%)
    all_to_all x1, blocking collectives, per_device(): forms = lax.all_to_all(forms, 'gx', 0, 0, tiled=True)  8.97 us
    all_to_all x1, starting transfers between devices, per_device(): recv = lax.all_to_all(packed.reshape(n, 3 * half, -1), 'gx', 0, 0)  7.39 us
    all_to_all x1, waiting for transfers between devices, per_device(): recv = lax.all_to_all(packed.reshape(n, 3 * half, -1), 'gx', 0, 0)  7.27 us
    pallas_call x1, Pallas kernels, krylov(): pl.pallas_call(functools.partial(field_kernel, n), out_shape=(jax.ShapeDt...  3.18 us
    pallas_call x1, Pallas kernels, krylov(): pl.pallas_call(scatter_kernel, out_shape=(bases, jax.ShapeDtypeStruct((3,...  2.76 us
    pallas_call x1, Pallas kernels, per_device(): pl.pallas_call(functools.partial(bin_kernel, n, half, rows, cols, depth /...  1.93 us
    pallas_call x1, Pallas kernels, combine(): pl.pallas_call(combine_kernel, out_shape=(jax.ShapeDtypeStruct((6, depth,...  1.54 us
  transfers between devices with their start and end apart: 3, of which 1 were waited for; matrix products, arithmetic and copies ran while one was open for 0% of the time, Pallas kernels for 8%

profile of v4, /device:TPU:0, one launch (start us, length us, event | category | flops | bytes accessed | tf_op | source)
XLA Modules:
  0.0 35.4 jit_solution(2008218142506584535)
XLA Ops:
  0.6 1.9 %bin_sites.1 = (f32[384,128]{1,0:T(8,128)}, f32[3,3,32,128]{3,2,1,0:T(8,128)S(1)}) custom-call(s32[1,128]{1,0:T(1,128)} %bitcast.8, s32[3,128]{1,0:T(4,128)} %refs_1_.1, s32[8,128]{1,0:T(8,128)} %refs_2_.1, f32[6,8,128]{2,1,0:T(8,128)} %refs_3_.1, f32[3,4,32,128]{3,2,1,0:T(8,128)} %cond_hbm.1), custom_call_target="tpu_custom_call" | custom-call | tf_op jit(solution)/shard_map/bin_sites/pallas_call | solution.py:433
  2.6 7.4 %all-to-all-start = ((f32[16,24,128]{2,1,0:T(8,128)}), f32[16,24,128]{2,1,0:T(8,128)S(1)}, u32[]{:S(2)}, u32[]{:S(2)}) async-start(f32[16,24,128]{2,1,0:T(8,128)} %bitcast.1), calls=%async_computation | async-start | bytes 393216 | tf_op jit(solution)/shard_map/all_to_all | solution.py:447
  10.0 0.4 %collective-permute-start = (f32[3,4,32,128]{3,2,1,0:T(8,128)}, f32[3,4,32,128]{3,2,1,0:T(8,128)S(1)}, u32[]{:S(2)}, u32[]{:S(2)}) collective-permute-start(f32[3,4,32,128]{3,2,1,0:T(8,128)} %cond_hbm.1), channel_id=1, source_target_pairs={{0,1},{1,0},{2,3},{3,2},{4,5},{5,4},{6,7},{7,6},{8,9},{9,8},{10,11... | collective-permute-start | bytes 589832 | tf_op jit(solution)/shard_map/ppermute | solution.py:445
  10.4 0.7 %collective-permute-start.1 = (f32[3,3,32,128]{3,2,1,0:T(8,128)S(1)}, f32[3,3,32,128]{3,2,1,0:T(8,128)S(1)}, u32[]{:S(2)}, u32[]{:S(2)}) collective-permute-start(f32[3,3,32,128]{3,2,1,0:T(8,128)S(1)} %get-tuple-element.8), channel_id=1, source_target_pairs={{1,2},{2,1},{3,4},{4,3},{5,6},{6,5},{7,8},{8,7},{9,10},{10,9},{11,... | collective-permute-start | bytes 442376 | tf_op jit(solution)/shard_map/ppermute | solution.py:446
  11.7 7.3 %all-to-all-done.recv_ref = f32[16,24,128]{2,1,0:T(8,128)S(1)} async-done(((f32[16,24,128]{2,1,0:T(8,128)}), f32[16,24,128]{2,1,0:T(8,128)S(1)}, u32[]{:S(2)}, u32[]{:S(2)}) %all-to-all-start) | async-done | bytes 196640 | tf_op jit(solution)/shard_map/all_to_all | solution.py:447
  19.0 2.8 %scatter_source.1 = (f32[6,6,12,4,8,128]{5,4,3,2,1,0:T(8,128)S(1)}, f32[3,4,4,8,128]{4,3,2,1,0:T(8,128)S(1)}) custom-call(f32[16,24,128]{2,1,0:T(8,128)S(1)} %all-to-all-done.recv_ref, f32[3,4,32,128]{3,2,1,0:T(8,128)} %cond_hbm.1, f32[1]{0:T(128)S(6)} %copy.11.omega_ref), custom_call_target="tpu_custom_call" | custom-call | flops 2415919104 | bytes 4194304 | tf_op jit(solution)/shard_map/scatter_source/pallas_call | solution.py:382
  21.7 0.0 collective-permute-done.1.other_ref
  21.7 0.0 collective-permute-done.mate_ref
  21.7 3.2 %krylov_basis.1 = (f32[16,128]{1,0:T(8,128)S(1)}, f32[6,6,12,4,8,128]{5,4,3,2,1,0:T(8,128)S(1)}) custom-call(f32[3,4,32,128]{3,2,1,0:T(8,128)S(1)} %collective-permute-done.mate_ref, f32[3,3,32,128]{3,2,1,0:T(8,128)S(1)} %collective-permute-done.1.other_ref, f32[3,4,4,8,128]{4,3,2,1,0:T(8,128)S(1)} %get-tuple-element.10.mine_ref, ...), custom_call_target="tpu_custom_call", output_to_operand_aliasing={{1}: (4, {})} | custom-call | tf_op jit(solution)/shard_map/krylov_basis/pallas_call | solution.py:399
  24.9 9.0 %all_to_all.16 = f32[16,1,128]{2,1,0:T(1,128)S(1)} all-to-all(f32[16,1,128]{2,1,0:T(1,128)S(1)} %bitcast.7), channel_id=1, replica_groups=mesh['period'=2,'gx'=16] {'gx'}, dimensions={0} | all-to-all | bytes 16384 | tf_op jit(solution)/shard_map/all_to_all | solution.py:453
  33.9 1.5 %combine_basis.1 = (f32[6,4,32,128]{3,2,1,0:T(8,128)}, f32[6,4,32,128]{3,2,1,0:T(8,128)}) custom-call(f32[16,128]{1,0:T(8,128)S(1)} %bitcast.6, f32[6,6,12,4,8,128]{5,4,3,2,1,0:T(8,128)S(1)} %get-tuple-element.13.basis), custom_call_target="tpu_custom_call" | custom-call | tf_op jit(solution)/shard_map/combine_basis/pallas_call | solution.py:417
Async XLA Ops:
  2.6 16.4 %all-to-all-start = ((f32[16,24,128]{2,1,0:T(8,128)}), f32[16,24,128]{2,1,0:T(8,128)S(1)}, u32[]{:S(2)}, u32[]{:S(2)}) async-start(f32[16,24,128]{2,1,0:T(8,128)} %bitcast.1), calls=%async_computation | async-start | bytes 393216 | tf_op jit(solution)/shard_map/all_to_all | solution.py:447
  10.0 11.8 %collective-permute-start = (f32[3,4,32,128]{3,2,1,0:T(8,128)}, f32[3,4,32,128]{3,2,1,0:T(8,128)S(1)}, u32[]{:S(2)}, u32[]{:S(2)}) collective-permute-start(f32[3,4,32,128]{3,2,1,0:T(8,128)} %cond_hbm.1), channel_id=1, source_target_pairs={{0,1},{1,0},{2,3},{3,2},{4,5},{5,4},{6,7},{7,6},{8,9},{9,8},{10,11... | collective-permute-start | bytes 589832 | tf_op jit(solution)/shard_map/ppermute | solution.py:445
  10.4 11.4 %collective-permute-start.1 = (f32[3,3,32,128]{3,2,1,0:T(8,128)S(1)}, f32[3,3,32,128]{3,2,1,0:T(8,128)S(1)}, u32[]{:S(2)}, u32[]{:S(2)}) collective-permute-start(f32[3,3,32,128]{3,2,1,0:T(8,128)S(1)} %get-tuple-element.8), channel_id=1, source_target_pairs={{1,2},{2,1},{3,4},{4,3},{5,6},{6,5},{7,8},{8,7},{9,10},{10,9},{11,... | collective-permute-start | bytes 442376 | tf_op jit(solution)/shard_map/ppermute | solution.py:446

commit v5 on v4

--- a/solution.py
+++ b/solution.py
@@ -82,9 +82,11 @@
     place = jnp.where(second, rank - half, rank)
 
     slot = lax.broadcasted_iota(jnp.int32, (out_ref.shape[0], sites), 0)
+    odd = owner % 2
+    beside = owner + 2 * odd - 1
     hit = jnp.zeros(slot.shape, jnp.bool_)
-    for j in range(3):
-        hit = hit | (slot == ((owner - j + 1) * 3 + j) * half + place)
+    for first_row in (2 * owner + 1, 2 * beside):
+        hit = hit | (slot == first_row * half + place)
     total = jnp.zeros(out_ref.shape, jnp.float32)
     for part, stacked in (
         (jnp.logical_not(second), [data, blank]),
@@ -99,53 +101,53 @@
     copies[4].wait()
 
 
-def scatter_kernel(recv_ref, cond_hbm, omega_ref, basis, mine_ref, left, right, cond_ref, arrived):
-    conductivity = pltpu.make_async_copy(cond_hbm, cond_ref, arrived)
-    conductivity.start()
+def scatter_slab(packed, left, right, depth, folds, cols):
+    rows = 8 * folds
+    half_depth = depth // 2
+    channels, points = 6, 8
+    row_count, lane_count, slots, width = half_depth * rows, 2 * cols, 2 * packed.shape[0], packed.shape[1] // 2
+    row_iota = lax.broadcasted_iota(jnp.int32, (row_count, slots), 0)
+    lane_iota = lax.broadcasted_iota(jnp.int32, (lane_count, slots), 0)
+    turned = packed.T
+    table = jnp.concatenate([turned[:width], turned[width:]], axis=1)
+    table_high = table.astype(jnp.bfloat16).astype(jnp.float32)
+    table_low = table - table_high
+    cell_row = table[channels * points : (channels + 1) * points].astype(jnp.int32)
+    cell_lane = table[(channels + 1) * points :].astype(jnp.int32)
+    for k in range(points):
+        span = slice(k * slots, (k + 1) * slots)
+        right[:, span] = jnp.where(lane_iota == cell_lane[k : k + 1], 1.0, 0.0).astype(jnp.bfloat16)
+        mask = row_iota == cell_row[k : k + 1]
+        for c in range(channels):
+            at = c * points + k
+            for piece, part in enumerate((table_high, table_low)):
+                first = (piece * channels + c) * row_count
+                left[first : first + row_count, span] = jnp.where(mask, part[at : at + 1], 0.0).astype(jnp.bfloat16)
+    both = lax.dot_general(left[...], right[...], CONTRACT_LANES, preferred_element_type=jnp.float32)
+    return both[: channels * row_count] + both[channels * row_count :]
+
+
+def store_slab(summed, basis, first_plane):
     depth, folds, cols = basis.shape[2] // 3, basis.shape[3], basis.shape[5]
     rows = 8 * folds
     half_depth = depth // 2
-    channels = 6
-    points = 8
-    group = recv_ref.shape[1] // 3
+    row_count = half_depth * rows
+    for c in range(6):
+        for x in range(depth):
+            first = c * row_count + (x % half_depth) * rows
+            lanes = slice((x // half_depth) * cols, (x // half_depth + 1) * cols)
+            basis[1, c, first_plane + x] = summed[first : first + rows, lanes].reshape(folds, 8, cols)
+
+
+def scatter_kernel(list_ref, cond_hbm, omega_ref, basis, mine_ref, left, right, cond_ref, arrived):
+    conductivity = pltpu.make_async_copy(cond_hbm, cond_ref, arrived)
+    conductivity.start()
+    depth, folds = mine_ref.shape[1], mine_ref.shape[2]
     basis[0] = jnp.zeros(basis.shape[1:], jnp.float32)
-    row_count = half_depth * rows
-    lane_count = 2 * cols
-    slots = 2 * recv_ref.shape[0] * group
-    width = (channels + 2) * points
-    row_iota = lax.broadcasted_iota(jnp.int32, (row_count, slots), 0)
-    lane_iota = lax.broadcasted_iota(jnp.int32, (lane_count, slots), 0)
-
-    def scatter(j, _):
-        packed = recv_ref[:, pl.ds(pl.multiple_of(j * group, 8), group), :].reshape(slots // 2, 2 * width)
-        turned = packed.T
-        table = jnp.concatenate([turned[:width], turned[width:]], axis=1)
-        table_high = table.astype(jnp.bfloat16).astype(jnp.float32)
-        table_low = table - table_high
-        cell_row = table[channels * points : (channels + 1) * points].astype(jnp.int32)
-        cell_lane = table[(channels + 1) * points :].astype(jnp.int32)
-        for k in range(points):
-            span = slice(k * slots, (k + 1) * slots)
-            right[:, span] = jnp.where(lane_iota == cell_lane[k : k + 1], 1.0, 0.0).astype(jnp.bfloat16)
-            mask = row_iota == cell_row[k : k + 1]
-            for c in range(channels):
-                at = c * points + k
-                for piece, part in enumerate((table_high, table_low)):
-                    first = (piece * channels + c) * row_count
-                    left[first : first + row_count, span] = jnp.where(mask, part[at : at + 1], 0.0).astype(
-                        jnp.bfloat16
-                    )
-        both = lax.dot_general(left[...], right[...], CONTRACT_LANES, preferred_element_type=jnp.float32)
-        summed = both[: channels * row_count] + both[channels * row_count :]
-        for c in range(channels):
-            for x in range(depth):
-                first = c * row_count + (x % half_depth) * rows
-                lanes = slice((x // half_depth) * cols, (x // half_depth + 1) * cols)
-                basis[1, c, j * depth + x] = summed[first : first + rows, lanes].reshape(folds, 8, cols)
-        return 0
-
-    lax.fori_loop(0, 3, scatter, 0, unroll=True)
-
+    cols = basis.shape[5]
+    outer, own = (scatter_slab(list_ref[j], left.at[j], right.at[j], depth, folds, cols) for j in range(2))
+    store_slab(own, basis, depth)
+    store_slab(outer, basis, 2 * depth * (lax.axis_index("gx") % 2))
     conductivity.wait()
     scale = omega_ref[0] * (2.0 / RADIUS)
     for q in range(3):
@@ -154,12 +156,16 @@
                 mine_ref[q, x, j] = cond_ref[q, x, pl.ds(j, 8, stride=folds)] * scale
 
 
-def field_kernel(n, mate_ref, other_ref, mine_ref, omega_ref, _, forms_ref, basis, coupling, faces):
+def field_kernel(
+    n, list_ref, mate_ref, other_ref, mine_ref, omega_ref, _, forms_ref, basis, coupling, faces, left, right
+):
     depth, folds, cols = basis.shape[2] // 3, basis.shape[3], basis.shape[5]
     channels = 6
     me = lax.axis_index("gx")
     keep_low = jnp.where(me > 0, 1.0, 0.0).astype(jnp.float32)
     keep_high = jnp.where(me < n - 1, 1.0, 0.0).astype(jnp.float32)
+
+    store_slab(scatter_slab(list_ref[...], left, right, depth, folds, cols), basis, 2 * depth * (1 - me % 2))
 
     scale = omega_ref[0] * (2.0 / RADIUS)
     even = me % 2 == 0
@@ -344,7 +350,7 @@
     return field_at, resid_at
 
 
-def combine_kernel(forms_ref, basis, field_ref, resid_ref):
+def combine_kernel(forms_ref, basis, field_hbm, resid_hbm, field_ref, resid_ref, sent):
     depth, folds, cols = basis.shape[2] // 3, basis.shape[3], basis.shape[5]
     totals = jnp.broadcast_to(jnp.sum(forms_ref[...], axis=0, keepdims=True), (8, cols))
     lane = lax.broadcasted_iota(jnp.int32, (8, cols), 1)
@@ -356,6 +362,12 @@
     moments = forms[:2] + [c_sub(forms[f], forms[f - 2]) for f in range(2, FORMS)]
     field_at, resid_at = step_scalars(moments)
 
+    def copies(p):
+        return [
+            pltpu.make_async_copy(ref.at[:, p], hbm_ref.at[:, p], sent.at[i, p])
+            for i, (ref, hbm_ref) in enumerate(((field_ref, field_hbm), (resid_ref, resid_hbm)))
+        ]
+
     def plane(p, _):
         for q in range(3):
             for j in range(folds):
@@ -365,19 +377,24 @@
                 for out_ref, factors in ((field_ref, field_at[:ITERS]), (resid_ref, resid_at)):
                     out_ref[q, p, rows] = sum(f[0] * re[k] - f[1] * im[k] for k, f in enumerate(factors))
                     out_ref[3 + q, p, rows] = sum(f[0] * im[k] + f[1] * re[k] for k, f in enumerate(factors))
+        for copy in copies(p):
+            copy.start()
         return 0
 
     lax.fori_loop(0, depth, plane, 0)
+    for p in range(depth):
+        for copy in copies(p):
+            copy.wait()
 
 
 def params(limit=VMEM_LIMIT):
     return pltpu.CompilerParams(vmem_limit_bytes=limit)
 
 
-def krylov(n, recv, mate, other, conductivity, omega):
+def krylov(n, lists, mate_list, mate, other, conductivity, omega):
     depth, folds, cols = conductivity.shape[1], conductivity.shape[2] // 8, conductivity.shape[3]
-    slots = 2 * recv.shape[0] * recv.shape[1] // 3
-    left_rows, right_rows = 2 * 6 * depth // 2 * 8 * folds, 2 * cols
+    slots = 2 * lists.shape[1]
+    left_shape, right_shape = (2 * 6 * depth // 2 * 8 * folds, 8 * slots), (2 * cols, 8 * slots)
     bases = jax.ShapeDtypeStruct((BASIS + 1, 6, 3 * depth, folds, 8, cols), jnp.float32)
     basis, mine = pl.pallas_call(
         scatter_kernel,
@@ -385,40 +402,44 @@
         in_specs=[vmem(), hbm(), smem()],
         out_specs=(vmem(), vmem()),
         scratch_shapes=[
-            pltpu.VMEM((left_rows, 8 * slots), jnp.bfloat16),
-            pltpu.VMEM((right_rows, 8 * slots), jnp.bfloat16),
+            pltpu.VMEM((2, *left_shape), jnp.bfloat16),
+            pltpu.VMEM((2, *right_shape), jnp.bfloat16),
             pltpu.VMEM(conductivity.shape, jnp.float32),
             pltpu.SemaphoreType.DMA,
         ],
         cost_estimate=pl.CostEstimate(
-            flops=6 * left_rows * right_rows * 8 * slots, bytes_accessed=4 * 1024 * 1024, transcendentals=0
+            flops=4 * left_shape[0] * right_shape[0] * 8 * slots, bytes_accessed=4 * 1024 * 1024, transcendentals=0
         ),
         compiler_params=params(),
         name="scatter_source",
-    )(recv, pltpu.with_memory_space_constraint(conductivity, pltpu.HBM), omega)
+    )(lists, pltpu.with_memory_space_constraint(conductivity, pltpu.HBM), omega)
     return pl.pallas_call(
         functools.partial(field_kernel, n),
         out_shape=(jax.ShapeDtypeStruct((n, cols), jnp.float32), bases),
-        in_specs=[vmem()] * 3 + [smem(), vmem()],
+        in_specs=[vmem()] * 4 + [smem(), vmem()],
         out_specs=(vmem(), vmem()),
         scratch_shapes=[
             pltpu.VMEM((3, 2 * HALO + depth, folds, 8, cols), jnp.float32),
             pltpu.VMEM((6, 3 * depth, folds, 8, cols), jnp.float32),
+            pltpu.VMEM(left_shape, jnp.bfloat16),
+            pltpu.VMEM(right_shape, jnp.bfloat16),
         ],
-        input_output_aliases={4: 1},
+        input_output_aliases={5: 1},
         compiler_params=params(),
         name="krylov_basis",
-    )(mate, other, mine, omega, basis)
+    )(mate_list, mate, other, mine, omega, basis)
 
 
 def combine(forms, basis):
     depth, folds, cols = basis.shape[2] // 3, basis.shape[3], basis.shape[5]
     rows = 8 * folds
+    out = jax.ShapeDtypeStruct((6, depth, rows, cols), jnp.float32)
     return pl.pallas_call(
         combine_kernel,
-        out_shape=(jax.ShapeDtypeStruct((6, depth, rows, cols), jnp.float32),) * 2,
+        out_shape=(out, out),
         in_specs=[vmem()] * 2,
-        out_specs=(vmem(), vmem()),
+        out_specs=(hbm(), hbm()),
+        scratch_shapes=[pltpu.VMEM(out.shape, out.dtype)] * 2 + [pltpu.SemaphoreType.DMA((2, depth))],
         compiler_params=params(),
         name="combine_basis",
     )(forms, basis)
@@ -433,7 +454,7 @@
     packed, cut = pl.pallas_call(
         functools.partial(bin_kernel, n, half, rows, cols, depth // 2),
         out_shape=(
-            jax.ShapeDtypeStruct((n * 3 * half, 2 * 8 * 8), jnp.float32),
+            jax.ShapeDtypeStruct((n * 2 * half, 2 * 8 * 8), jnp.float32),
             jax.ShapeDtypeStruct((3, HALO, rows, cols), jnp.float32),
         ),
         in_specs=[hbm()] * 5,
@@ -442,13 +463,13 @@
         compiler_params=params(),
         name="bin_sites",
     )(*(pltpu.with_memory_space_constraint(x, pltpu.HBM) for x in (*listed, conductivity)))
-    mate = lax.ppermute(conductivity, "gx", [(i, i ^ 1) for i in range(n)])
     other = lax.ppermute(cut, "gx", [(i, ((i + 1) ^ 1) - 1) for i in range(1, n - 1)])
-    recv = lax.all_to_all(packed.reshape(n, 3 * half, -1), "gx", 0, 0)
-    if half % 8:
-        recv = recv.reshape(n, 3, half, -1).transpose(1, 0, 2, 3).reshape(1, 3 * n * half, -1)
-
-    forms, basis = krylov(n, recv, mate, other, conductivity, omega)
+    late, _ = lax.optimization_barrier((conductivity, cut))
+    mate = lax.ppermute(late, "gx", [(i, i ^ 1) for i in range(n)])
+    recv = lax.all_to_all(packed.reshape(n, 2 * half, -1), "gx", 0, 0)
+    lists = recv.reshape(n, 2, half, -1).transpose(1, 0, 2, 3).reshape(2, n * half, -1)
+    mate_list = lax.ppermute(lists[1], "gx", [(i, i ^ 1) for i in range(n)])
+    forms, basis = krylov(n, lists, mate_list, mate, other, conductivity, omega)
 
     forms = lax.all_to_all(forms, "gx", 0, 0, tiled=True)
 

time: 35.7 us -> 35.2 us (0.986)
  waiting for transfers between devices: 7.27 us -> 3.28 us
  starting transfers between devices: 8.46 us -> 11.4 us
  blocking collectives: 8.97 us -> 9.38 us
    all_to_all x1, waiting for transfers between devices: 7.27 us -> 3.27 us  [per_device(): recv = lax.all_to_all(packed.reshape(n, 2 * half, -1), 'gx', 0, 0)]
    ppermute x1 -> x2, starting transfers between devices: 0.41 us -> 3.34 us  [the longest x1 3.33 us: per_device(): mate = lax.ppermute(late, 'gx', [(i, i ^ 1) for i in range(n)])]
    pallas_call x1, Pallas kernels: 3.18 us -> 4.28 us  [krylov(): pl.pallas_call(functools.partial(field_kernel, n), out_shape=(jax.ShapeDt...]
    pallas_call x1, Pallas kernels: 2.76 us -> 1.95 us  [krylov(): pl.pallas_call(scatter_kernel, out_shape=(bases, jax.ShapeDtypeStruct((3,...]
    all_to_all x1, blocking collectives: 8.97 us -> 9.38 us  [per_device(): forms = lax.all_to_all(forms, 'gx', 0, 0, tiled=True)]
  transfers between devices with their start and end apart: 3 -> 4, of which waited for: 1 -> 1; matrix products, arithmetic and copies ran while one was open for 0% -> 0% of each run, Pallas kernels for 8% -> 6%
where the time goes in v5:
time: 35.2 us; the launch traced here: 34.9 us
  starting transfers between devices  11.4 us (32%)
  Pallas kernels  9.49 us (27%)
  blocking collectives  9.38 us (27%)
  waiting for transfers between devices  3.28 us (9%)
  between operations  1.35 us (4%)
    all_to_all x1, blocking collectives, per_device(): forms = lax.all_to_all(forms, 'gx', 0, 0, tiled=True)  9.38 us
    all_to_all x1, starting transfers between devices, per_device(): recv = lax.all_to_all(packed.reshape(n, 2 * half, -1), 'gx', 0, 0)  7.39 us
    pallas_call x1, Pallas kernels, krylov(): pl.pallas_call(functools.partial(field_kernel, n), out_shape=(jax.ShapeDt...  4.28 us
    ppermute x1, starting transfers between devices, per_device(): mate = lax.ppermute(late, 'gx', [(i, i ^ 1) for i in range(n)])  3.33 us
    all_to_all x1, waiting for transfers between devices, per_device(): recv = lax.all_to_all(packed.reshape(n, 2 * half, -1), 'gx', 0, 0)  3.27 us
    pallas_call x1, Pallas kernels, krylov(): pl.pallas_call(scatter_kernel, out_shape=(bases, jax.ShapeDtypeStruct((3,...  1.95 us
    pallas_call x1, Pallas kernels, per_device(): pl.pallas_call(functools.partial(bin_kernel, n, half, rows, cols, depth /...  1.85 us
    pallas_call x1, Pallas kernels, combine(): pl.pallas_call(combine_kernel, out_shape=(out, out), in_specs=[vmem()] *...  1.41 us
  transfers between devices with their start and end apart: 4, of which 1 were waited for; matrix products, arithmetic and copies ran while one was open for 0% of the time, Pallas kernels for 6%

profile of v5, /device:TPU:0, one launch (start us, length us, event | category | flops | bytes accessed | tf_op | source)
XLA Modules:
  0.0 34.9 jit_solution(16429494368369620985)
XLA Ops:
  0.6 1.9 %bin_sites.1 = (f32[256,128]{1,0:T(8,128)}, f32[3,3,32,128]{3,2,1,0:T(8,128)S(1)}) custom-call(s32[1,128]{1,0:T(1,128)} %bitcast.18, s32[3,128]{1,0:T(4,128)} %refs_1_.1, s32[8,128]{1,0:T(8,128)} %refs_2_.1, f32[6,8,128]{2,1,0:T(8,128)} %refs_3_.1, f32[3,4,32,128]{3,2,1,0:T(8,128)} %cond_hbm.1), custom_call_target="tpu_custom_call" | custom-call | tf_op jit(solution)/shard_map/bin_sites/pallas_call | solution.py:454
  2.5 7.4 %all-to-all-start = ((f32[16,16,128]{2,1,0:T(8,128)}), f32[16,16,128]{2,1,0:T(8,128)S(1)}, u32[]{:S(2)}, u32[]{:S(2)}) async-start(f32[16,16,128]{2,1,0:T(8,128)} %bitcast.1), calls=%async_computation | async-start | bytes 262144 | tf_op jit(solution)/shard_map/all_to_all | solution.py:469
  9.9 0.7 %collective-permute-start.2 = (f32[3,3,32,128]{3,2,1,0:T(8,128)S(1)}, f32[3,3,32,128]{3,2,1,0:T(8,128)S(1)}, u32[]{:S(2)}, u32[]{:S(2)}) collective-permute-start(f32[3,3,32,128]{3,2,1,0:T(8,128)S(1)} %get-tuple-element.10), channel_id=1, source_target_pairs={{1,2},{2,1},{3,4},{4,3},{5,6},{6,5},{7,8},{8,7},{9,10},{10,9},{11,... | collective-permute-start | bytes 442376 | tf_op jit(solution)/shard_map/ppermute | solution.py:466
  10.6 3.3 %collective-permute-start.1 = (f32[3,4,32,128]{3,2,1,0:T(8,128)}, f32[3,4,32,128]{3,2,1,0:T(8,128)S(1)}, u32[]{:S(2)}, u32[]{:S(2)}) collective-permute-start(f32[3,4,32,128]{3,2,1,0:T(8,128)} %cond_hbm.1), channel_id=1, source_target_pairs={{0,1},{1,0},{2,3},{3,2},{4,5},{5,4},{6,7},{7,6},{8,9},{9,8},{10,11... | collective-permute-start | bytes 589832 | tf_op jit(solution)/shard_map/ppermute | solution.py:468
  14.6 3.3 %all-to-all-done = f32[16,16,128]{2,1,0:T(8,128)S(1)} async-done(((f32[16,16,128]{2,1,0:T(8,128)}), f32[16,16,128]{2,1,0:T(8,128)S(1)}, u32[]{:S(2)}, u32[]{:S(2)}) %all-to-all-start) | async-done | bytes 131104 | tf_op jit(solution)/shard_map/all_to_all | solution.py:469
  17.8 0.0 collective-permute-start
  17.9 2.0 %scatter_source.1 = (f32[6,6,12,4,8,128]{5,4,3,2,1,0:T(8,128)S(1)}, f32[3,4,4,8,128]{4,3,2,1,0:T(8,128)S(1)}) custom-call(f32[2,128,128]{2,1,0:T(8,128)S(1)} %copy_bitcast_fusion.list_ref, f32[3,4,32,128]{3,2,1,0:T(8,128)} %cond_hbm.1, f32[1]{0:T(128)S(6)} %copy.14.omega_ref), custom_call_target="tpu_custom_call" | custom-call | flops 1610612736 | bytes 4194304 | tf_op jit(solution)/shard_map/scatter_source/pallas_call | solution.py:399
  19.8 0.0 collective-permute-done.2.other_ref
  19.8 0.0 collective-permute-done.1.mate_ref
  19.8 0.0 collective-permute-done.list_ref
  19.9 4.3 %krylov_basis.1 = (f32[16,128]{1,0:T(8,128)S(1)}, f32[6,6,12,4,8,128]{5,4,3,2,1,0:T(8,128)S(1)}) custom-call(f32[128,128]{1,0:T(8,128)S(1)} %collective-permute-done.list_ref, f32[3,4,32,128]{3,2,1,0:T(8,128)S(1)} %collective-permute-done.1.mate_ref, f32[3,3,32,128]{3,2,1,0:T(8,128)S(1)} %collective-permute-done.2.other_ref, ...), custom_call_target="tpu_custom_call", output_to_operand_aliasing={{1}: (5, {})} | custom-call | tf_op jit(solution)/shard_map/krylov_basis/pallas_call | solution.py:416
  24.1 9.4 %all_to_all.16 = f32[16,1,128]{2,1,0:T(1,128)S(1)} all-to-all(f32[16,1,128]{2,1,0:T(1,128)S(1)} %bitcast.16), channel_id=1, replica_groups=mesh['period'=2,'gx'=16] {'gx'}, dimensions={0} | all-to-all | bytes 16384 | tf_op jit(solution)/shard_map/all_to_all | solution.py:474
  33.5 1.4 %combine_basis.1 = (f32[6,4,32,128]{3,2,1,0:T(8,128)}, f32[6,4,32,128]{3,2,1,0:T(8,128)}) custom-call(f32[16,128]{1,0:T(8,128)S(1)} %bitcast.15, f32[6,6,12,4,8,128]{5,4,3,2,1,0:T(8,128)S(1)} %get-tuple-element.15.basis), custom_call_target="tpu_custom_call" | custom-call | tf_op jit(solution)/shard_map/combine_basis/pallas_call | solution.py:437
  (2 shorter events, 0.0 us)
Async XLA Ops:
  2.5 15.3 %all-to-all-start = ((f32[16,16,128]{2,1,0:T(8,128)}), f32[16,16,128]{2,1,0:T(8,128)S(1)}, u32[]{:S(2)}, u32[]{:S(2)}) async-start(f32[16,16,128]{2,1,0:T(8,128)} %bitcast.1), calls=%async_computation | async-start | bytes 262144 | tf_op jit(solution)/shard_map/all_to_all | solution.py:469
  9.9 9.9 %collective-permute-start.2 = (f32[3,3,32,128]{3,2,1,0:T(8,128)S(1)}, f32[3,3,32,128]{3,2,1,0:T(8,128)S(1)}, u32[]{:S(2)}, u32[]{:S(2)}) collective-permute-start(f32[3,3,32,128]{3,2,1,0:T(8,128)S(1)} %get-tuple-element.10), channel_id=1, source_target_pairs={{1,2},{2,1},{3,4},{4,3},{5,6},{6,5},{7,8},{8,7},{9,10},{10,9},{11,... | collective-permute-start | bytes 442376 | tf_op jit(solution)/shard_map/ppermute | solution.py:466
  10.6 9.3 %collective-permute-start.1 = (f32[3,4,32,128]{3,2,1,0:T(8,128)}, f32[3,4,32,128]{3,2,1,0:T(8,128)S(1)}, u32[]{:S(2)}, u32[]{:S(2)}) collective-permute-start(f32[3,4,32,128]{3,2,1,0:T(8,128)} %cond_hbm.1), channel_id=1, source_target_pairs={{0,1},{1,0},{2,3},{3,2},{4,5},{5,4},{6,7},{7,6},{8,9},{9,8},{10,11... | collective-permute-start | bytes 589832 | tf_op jit(solution)/shard_map/ppermute | solution.py:468
  17.8 2.0 %collective-permute-start = (f32[128,128]{1,0:T(8,128)S(1)}, f32[128,128]{1,0:T(8,128)S(1)}, u32[]{:S(2)}, u32[]{:S(2)}) collective-permute-start(f32[128,128]{1,0:T(8,128)S(1)} %slice_bitcast_fusion), channel_id=1, source_target_pairs={{0,1},{1,0},{2,3},{3,2},{4,5},{5,4},{6,7},{7,6},{8,9},{9,8},{10,11... | collective-permute-start | bytes 196616 | tf_op jit(solution)/shard_map/ppermute | solution.py:471

commit v6 on v5

--- a/solution.py
+++ b/solution.py
@@ -14,6 +14,7 @@
 FORMS = 2 * ITERS
 PAIRS = [(i // 2, (i + 1) // 2) for i in range(FORMS)]
 HALO = ITERS - 1
+STEP = 5
 VMEM_LIMIT = 40 * 1024 * 1024
 FULL_LIMIT = 62 * 1024 * 1024
 CONTRACT_LANES = (((1,), (1,)), ((), ()))
@@ -143,7 +144,6 @@
     conductivity = pltpu.make_async_copy(cond_hbm, cond_ref, arrived)
     conductivity.start()
     depth, folds = mine_ref.shape[1], mine_ref.shape[2]
-    basis[0] = jnp.zeros(basis.shape[1:], jnp.float32)
     cols = basis.shape[5]
     outer, own = (scatter_slab(list_ref[j], left.at[j], right.at[j], depth, folds, cols) for j in range(2))
     store_slab(own, basis, depth)
@@ -231,45 +231,46 @@
             )
             for q in range(3):
                 other = coupled[q] * here[3 * (1 - part) + q]
-                value = weight * curls[q] - (centre * here[3 * part + q] + older[3 * part + q])
+                rest = centre * here[3 * part + q]
+                if older[3 * part + q] is not None:
+                    rest = rest + older[3 * part + q]
+                value = weight * curls[q] - rest
                 new.append(value + other if part == 0 else value - other)
         return new
 
-    last_pair = 3 * depth - 3
-
-    def apply(k, _):
-        first = [edges(k, k - 1 + d) for d in range(4)]
-        for d in range(3):
-            keep_faces(k - 1 + d, faces_of(first[d], first[d + 1]))
-
-        def step(i, _):
-            p = k + 2 * i
-            ahead = jnp.minimum(p + 2, last_pair)
-            fields = [edges(k, p + d) for d in range(2)]
-            older = [edges(k - 1, p + d) for d in range(2)]
-            coupled = [[coupling[q, p + d - (depth - HALO)] for q in range(3)] for d in range(2)]
-            face = [[faces[c, p + d] for c in range(channels)] for d in range(2)]
-            before = [faces[c, p - 1] * jnp.where(p == depth, keep_low, 1.0) for c in (1, 2, 4, 5)]
-            middle = [face[0][c] * jnp.where(p + 1 == depth, keep_low, 1.0) for c in (1, 2, 4, 5)]
-            following = [edges(k, ahead + d) for d in range(3)]
-            next_faces = [faces_of(following[d], following[d + 1]) for d in range(2)]
-            new = [
-                plane(fields[0], older[0], coupled[0], face[0], before),
-                plane(fields[1], older[1], coupled[1], face[1], middle),
-            ]
-            for d in range(2):
+    def apply(k):
+        end = 3 * depth - k
+
+        def step(p, count):
+            after = range(p + count, min(p + 2 * count, end))
+            fields = [edges(k, p + d) for d in range(count)]
+            older = [edges(k - 1, p + d) if k > 1 else [None] * channels for d in range(count)]
+            coupled = [[coupling[q, p + d - (depth - HALO)] for q in range(3)] for d in range(count)]
+            face = [[faces[c, p + d] for c in range(channels)] for d in range(-1, count)]
+            following = [edges(k, x) for x in range(p + count, after.stop + 1)] if after else []
+            next_faces = [faces_of(following[d], following[d + 1]) for d in range(len(after))]
+            new = []
+            for d in range(count):
+                before = [face[d][c] for c in (1, 2, 4, 5)]
+                if p + d == depth:
+                    before = [f * keep_low for f in before]
+                new.append(plane(fields[d], older[d], coupled[d], face[d + 1], before))
+                if p + d == 2 * depth:
+                    new[d] = [f * keep_high for f in new[d]]
+            for d in range(count):
                 for c in range(channels):
                     basis[k + 1, c, p + d] = new[d][c]
-            for d in range(2):
-                keep_faces(ahead + d, next_faces[d])
-            return 0
-
-        lax.fori_loop(0, (3 * depth - 2 * k) // 2, step, 0)
-        for c in range(channels):
-            basis[k + 1, c, 2 * depth] = basis[k + 1, c, 2 * depth] * keep_high
-        return 0
-
-    lax.fori_loop(1, BASIS, apply, 0)
+            for x, values in zip(after, next_faces):
+                keep_faces(x, values)
+
+        first = [edges(k, x) for x in range(k - 1, min(k + STEP, end) + 1)]
+        for d in range(len(first) - 1):
+            keep_faces(k - 1 + d, faces_of(first[d], first[d + 1]))
+        for p in range(k, end, STEP):
+            step(p, min(STEP, end - p))
+
+    for k in range(1, BASIS):
+        apply(k)
 
     def plane_forms(p, sums):
         sums = list(sums)

time: 35.2 us -> 34.7 us (0.986)
  Pallas kernels: 9.49 us -> 8.95 us
    pallas_call x1, Pallas kernels: 4.28 us -> 3.73 us  [krylov(): pl.pallas_call(functools.partial(field_kernel, n), out_shape=(jax.ShapeDt...]
where the time goes in v6:
time: 34.7 us; the launch traced here: 34.4 us
  starting transfers between devices  11.4 us (33%)
  blocking collectives  9.38 us (27%)
  Pallas kernels  8.95 us (26%)
  waiting for transfers between devices  3.28 us (9%)
  between operations  1.35 us (4%)
    all_to_all x1, blocking collectives, per_device(): forms = lax.all_to_all(forms, 'gx', 0, 0, tiled=True)  9.38 us
    all_to_all x1, starting transfers between devices, per_device(): recv = lax.all_to_all(packed.reshape(n, 2 * half, -1), 'gx', 0, 0)  7.39 us
    pallas_call x1, Pallas kernels, krylov(): pl.pallas_call(functools.partial(field_kernel, n), out_shape=(jax.ShapeDt...  3.73 us
    ppermute x1, starting transfers between devices, per_device(): mate = lax.ppermute(late, 'gx', [(i, i ^ 1) for i in range(n)])  3.33 us
    all_to_all x1, waiting for transfers between devices, per_device(): recv = lax.all_to_all(packed.reshape(n, 2 * half, -1), 'gx', 0, 0)  3.27 us
    pallas_call x1, Pallas kernels, krylov(): pl.pallas_call(scatter_kernel, out_shape=(bases, jax.ShapeDtypeStruct((3,...  1.95 us
    pallas_call x1, Pallas kernels, per_device(): pl.pallas_call(functools.partial(bin_kernel, n, half, rows, cols, depth /...  1.85 us
    pallas_call x1, Pallas kernels, combine(): pl.pallas_call(combine_kernel, out_shape=(out, out), in_specs=[vmem()] *...  1.41 us
  transfers between devices with their start and end apart: 4, of which 1 were waited for; matrix products, arithmetic and copies ran while one was open for 0% of the time, Pallas kernels for 6%

profile of v6, /device:TPU:0, one launch (start us, length us, event | category | flops | bytes accessed | tf_op | source)
XLA Modules:
  0.0 34.4 jit_solution(13544110484056129464)
XLA Ops:
  0.6 1.9 %bin_sites.1 = (f32[256,128]{1,0:T(8,128)}, f32[3,3,32,128]{3,2,1,0:T(8,128)S(1)}) custom-call(s32[1,128]{1,0:T(1,128)} %bitcast.18, s32[3,128]{1,0:T(4,128)} %refs_1_.1, s32[8,128]{1,0:T(8,128)} %refs_2_.1, f32[6,8,128]{2,1,0:T(8,128)} %refs_3_.1, f32[3,4,32,128]{3,2,1,0:T(8,128)} %cond_hbm.1), custom_call_target="tpu_custom_call" | custom-call | tf_op jit(solution)/shard_map/bin_sites/pallas_call | solution.py:455
  2.5 7.4 %all-to-all-start = ((f32[16,16,128]{2,1,0:T(8,128)}), f32[16,16,128]{2,1,0:T(8,128)S(1)}, u32[]{:S(2)}, u32[]{:S(2)}) async-start(f32[16,16,128]{2,1,0:T(8,128)} %bitcast.1), calls=%async_computation | async-start | bytes 262144 | tf_op jit(solution)/shard_map/all_to_all | solution.py:470
  9.9 0.7 %collective-permute-start.2 = (f32[3,3,32,128]{3,2,1,0:T(8,128)S(1)}, f32[3,3,32,128]{3,2,1,0:T(8,128)S(1)}, u32[]{:S(2)}, u32[]{:S(2)}) collective-permute-start(f32[3,3,32,128]{3,2,1,0:T(8,128)S(1)} %get-tuple-element.10), channel_id=1, source_target_pairs={{1,2},{2,1},{3,4},{4,3},{5,6},{6,5},{7,8},{8,7},{9,10},{10,9},{11,... | collective-permute-start | bytes 442376 | tf_op jit(solution)/shard_map/ppermute | solution.py:467
  10.6 3.3 %collective-permute-start.1 = (f32[3,4,32,128]{3,2,1,0:T(8,128)}, f32[3,4,32,128]{3,2,1,0:T(8,128)S(1)}, u32[]{:S(2)}, u32[]{:S(2)}) collective-permute-start(f32[3,4,32,128]{3,2,1,0:T(8,128)} %cond_hbm.1), channel_id=1, source_target_pairs={{0,1},{1,0},{2,3},{3,2},{4,5},{5,4},{6,7},{7,6},{8,9},{9,8},{10,11... | collective-permute-start | bytes 589832 | tf_op jit(solution)/shard_map/ppermute | solution.py:469
  14.6 3.3 %all-to-all-done = f32[16,16,128]{2,1,0:T(8,128)S(1)} async-done(((f32[16,16,128]{2,1,0:T(8,128)}), f32[16,16,128]{2,1,0:T(8,128)S(1)}, u32[]{:S(2)}, u32[]{:S(2)}) %all-to-all-start) | async-done | bytes 131104 | tf_op jit(solution)/shard_map/all_to_all | solution.py:470
  17.8 0.0 collective-permute-start
  17.9 2.0 %scatter_source.1 = (f32[6,6,12,4,8,128]{5,4,3,2,1,0:T(8,128)S(1)}, f32[3,4,4,8,128]{4,3,2,1,0:T(8,128)S(1)}) custom-call(f32[2,128,128]{2,1,0:T(8,128)S(1)} %copy_bitcast_fusion.list_ref, f32[3,4,32,128]{3,2,1,0:T(8,128)} %cond_hbm.1, f32[1]{0:T(128)S(6)} %copy.14.omega_ref), custom_call_target="tpu_custom_call" | custom-call | flops 1610612736 | bytes 4194304 | tf_op jit(solution)/shard_map/scatter_source/pallas_call | solution.py:400
  19.8 0.0 collective-permute-done.2.other_ref
  19.8 0.0 collective-permute-done.1.mate_ref
  19.8 0.0 collective-permute-done.list_ref
  19.9 3.7 %krylov_basis.1 = (f32[16,128]{1,0:T(8,128)S(1)}, f32[6,6,12,4,8,128]{5,4,3,2,1,0:T(8,128)S(1)}) custom-call(f32[128,128]{1,0:T(8,128)S(1)} %collective-permute-done.list_ref, f32[3,4,32,128]{3,2,1,0:T(8,128)S(1)} %collective-permute-done.1.mate_ref, f32[3,3,32,128]{3,2,1,0:T(8,128)S(1)} %collective-permute-done.2.other_ref, ...), custom_call_target="tpu_custom_call", output_to_operand_aliasing={{1}: (5, {})} | custom-call | tf_op jit(solution)/shard_map/krylov_basis/pallas_call | solution.py:417
  23.6 9.4 %all_to_all.16 = f32[16,1,128]{2,1,0:T(1,128)S(1)} all-to-all(f32[16,1,128]{2,1,0:T(1,128)S(1)} %bitcast.16), channel_id=1, replica_groups=mesh['period'=2,'gx'=16] {'gx'}, dimensions={0} | all-to-all | bytes 16384 | tf_op jit(solution)/shard_map/all_to_all | solution.py:475
  33.0 1.4 %combine_basis.1 = (f32[6,4,32,128]{3,2,1,0:T(8,128)}, f32[6,4,32,128]{3,2,1,0:T(8,128)}) custom-call(f32[16,128]{1,0:T(8,128)S(1)} %bitcast.15, f32[6,6,12,4,8,128]{5,4,3,2,1,0:T(8,128)S(1)} %get-tuple-element.15.basis), custom_call_target="tpu_custom_call" | custom-call | tf_op jit(solution)/shard_map/combine_basis/pallas_call | solution.py:438
  (2 shorter events, 0.0 us)
Async XLA Ops:
  2.5 15.3 %all-to-all-start = ((f32[16,16,128]{2,1,0:T(8,128)}), f32[16,16,128]{2,1,0:T(8,128)S(1)}, u32[]{:S(2)}, u32[]{:S(2)}) async-start(f32[16,16,128]{2,1,0:T(8,128)} %bitcast.1), calls=%async_computation | async-start | bytes 262144 | tf_op jit(solution)/shard_map/all_to_all | solution.py:470
  9.9 9.9 %collective-permute-start.2 = (f32[3,3,32,128]{3,2,1,0:T(8,128)S(1)}, f32[3,3,32,128]{3,2,1,0:T(8,128)S(1)}, u32[]{:S(2)}, u32[]{:S(2)}) collective-permute-start(f32[3,3,32,128]{3,2,1,0:T(8,128)S(1)} %get-tuple-element.10), channel_id=1, source_target_pairs={{1,2},{2,1},{3,4},{4,3},{5,6},{6,5},{7,8},{8,7},{9,10},{10,9},{11,... | collective-permute-start | bytes 442376 | tf_op jit(solution)/shard_map/ppermute | solution.py:467
  10.6 9.3 %collective-permute-start.1 = (f32[3,4,32,128]{3,2,1,0:T(8,128)}, f32[3,4,32,128]{3,2,1,0:T(8,128)S(1)}, u32[]{:S(2)}, u32[]{:S(2)}) collective-permute-start(f32[3,4,32,128]{3,2,1,0:T(8,128)} %cond_hbm.1), channel_id=1, source_target_pairs={{0,1},{1,0},{2,3},{3,2},{4,5},{5,4},{6,7},{7,6},{8,9},{9,8},{10,11... | collective-permute-start | bytes 589832 | tf_op jit(solution)/shard_map/ppermute | solution.py:469
  17.8 2.0 %collective-permute-start = (f32[128,128]{1,0:T(8,128)S(1)}, f32[128,128]{1,0:T(8,128)S(1)}, u32[]{:S(2)}, u32[]{:S(2)}) collective-permute-start(f32[128,128]{1,0:T(8,128)S(1)} %slice_bitcast_fusion), channel_id=1, source_target_pairs={{0,1},{1,0},{2,3},{3,2},{4,5},{5,4},{6,7},{7,6},{8,9},{9,8},{10,11... | collective-permute-start | bytes 196616 | tf_op jit(solution)/shard_map/ppermute | solution.py:472

commit v7 on v6

--- a/solution.py
+++ b/solution.py
@@ -165,7 +165,10 @@
     keep_low = jnp.where(me > 0, 1.0, 0.0).astype(jnp.float32)
     keep_high = jnp.where(me < n - 1, 1.0, 0.0).astype(jnp.float32)
 
-    store_slab(scatter_slab(list_ref[...], left, right, depth, folds, cols), basis, 2 * depth * (1 - me % 2))
+    @pl.when(me >= 0)
+    def _():
+        store_slab(scatter_slab(list_ref[...], left, right, depth, folds, cols), basis, 2 * depth * (1 - me % 2))
+
 
     scale = omega_ref[0] * (2.0 / RADIUS)
     even = me % 2 == 0
@@ -270,7 +273,7 @@
             step(p, min(STEP, end - p))
 
     for k in range(1, BASIS):
-        apply(k)
+        pl.when(me >= 0)(functools.partial(apply, k))
 
     def plane_forms(p, sums):
         sums = list(sums)
@@ -285,7 +288,7 @@
         return tuple(sums)
 
     zero = jnp.zeros((8, cols), jnp.float32)
-    sums = lax.fori_loop(depth, 2 * depth, plane_forms, (zero,) * (2 * FORMS))
+    sums = lax.fori_loop(depth, 2 * depth, plane_forms, (zero,) * (2 * FORMS), unroll=2)
     folded = jnp.concatenate([jnp.sum(total, axis=0, keepdims=True) for total in sums], axis=0)
     totals = jnp.sum(folded, axis=1, keepdims=True)
     diagonal = lax.broadcasted_iota(jnp.int32, folded.shape, 0) == lax.broadcasted_iota(jnp.int32, folded.shape, 1)
@@ -446,7 +449,16 @@
     )(forms, basis)
 
 
-def per_device(n, site_owner, site_cell, stencil_code, site_residual, conductivity, omega):
+def outer_pairs(periods, n):
+    pairs = []
+    for p in range(periods):
+        pairs += [(p * n + i, p * n + ((i + 1) ^ 1) - 1) for i in range(1, n - 1)]
+        if periods % 2 == 0:
+            pairs += [(p * n + i, (p ^ 1) * n + i) for i in (0, n - 1)]
+    return pairs
+
+
+def per_device(periods, n, site_owner, site_cell, stencil_code, site_residual, conductivity, omega):
     depth, rows, cols = conductivity.shape[1:]
     sites = site_owner.shape[0]
     cap = 2 * sites // n
@@ -464,9 +476,8 @@
         compiler_params=params(),
         name="bin_sites",
     )(*(pltpu.with_memory_space_constraint(x, pltpu.HBM) for x in (*listed, conductivity)))
-    other = lax.ppermute(cut, "gx", [(i, ((i + 1) ^ 1) - 1) for i in range(1, n - 1)])
-    late, _ = lax.optimization_barrier((conductivity, cut))
-    mate = lax.ppermute(late, "gx", [(i, i ^ 1) for i in range(n)])
+    other = lax.ppermute(cut, ("period", "gx"), outer_pairs(periods, n))
+    mate = lax.ppermute(conductivity, "gx", [(i, i ^ 1) for i in range(n)])
     recv = lax.all_to_all(packed.reshape(n, 2 * half, -1), "gx", 0, 0)
     lists = recv.reshape(n, 2, half, -1).transpose(1, 0, 2, 3).reshape(2, n * half, -1)
     mate_list = lax.ppermute(lists[1], "gx", [(i, i ^ 1) for i in range(n)])
@@ -487,7 +498,7 @@
         P("period"),
     )
     return jax.shard_map(
-        functools.partial(per_device, mesh.shape["gx"]),
+        functools.partial(per_device, mesh.shape["period"], mesh.shape["gx"]),
         mesh=mesh,
         in_specs=placed,
         out_specs=(P("period", "gx", None, None), P("period", "gx", None, None)),

time: 34.7 us -> 33.8 us (0.974)
  waiting for transfers between devices: 3.28 us -> 5.39 us
  starting transfers between devices: 11.4 us -> 9.3 us
  Pallas kernels: 8.95 us -> 8.48 us
  blocking collectives: 9.38 us -> 8.97 us
    all_to_all x1, waiting for transfers between devices: 3.27 us -> 5.38 us  [per_device(): recv = lax.all_to_all(packed.reshape(n, 2 * half, -1), 'gx', 0, 0)]
    ppermute x2, starting transfers between devices: 4 us -> 1.9 us  [the longest x1 1.49 us: per_device(): other = lax.ppermute(cut, ('period', 'gx'), outer_pairs(periods, n))]
    pallas_call x1, Pallas kernels: 3.73 us -> 3.27 us  [krylov(): pl.pallas_call(functools.partial(field_kernel, n), out_shape=(jax.ShapeDt...]
    all_to_all x1, blocking collectives: 9.38 us -> 8.97 us  [per_device(): forms = lax.all_to_all(forms, 'gx', 0, 0, tiled=True)]
where the time goes in v7:
time: 33.8 us; the launch traced here: 33.5 us
  starting transfers between devices  9.3 us (28%)
  blocking collectives  8.97 us (27%)
  Pallas kernels  8.48 us (25%)
  waiting for transfers between devices  5.39 us (16%)
  between operations  1.35 us (4%)
    all_to_all x1, blocking collectives, per_device(): forms = lax.all_to_all(forms, 'gx', 0, 0, tiled=True)  8.97 us
    all_to_all x1, starting transfers between devices, per_device(): recv = lax.all_to_all(packed.reshape(n, 2 * half, -1), 'gx', 0, 0)  7.39 us
    all_to_all x1, waiting for transfers between devices, per_device(): recv = lax.all_to_all(packed.reshape(n, 2 * half, -1), 'gx', 0, 0)  5.38 us
    pallas_call x1, Pallas kernels, krylov(): pl.pallas_call(functools.partial(field_kernel, n), out_shape=(jax.ShapeDt...  3.27 us
    pallas_call x1, Pallas kernels, krylov(): pl.pallas_call(scatter_kernel, out_shape=(bases, jax.ShapeDtypeStruct((3,...  1.95 us
    pallas_call x1, Pallas kernels, per_device(): pl.pallas_call(functools.partial(bin_kernel, n, half, rows, cols, depth /...  1.85 us
    ppermute x1, starting transfers between devices, per_device(): other = lax.ppermute(cut, ('period', 'gx'), outer_pairs(periods, n))  1.49 us
    pallas_call x1, Pallas kernels, combine(): pl.pallas_call(combine_kernel, out_shape=(out, out), in_specs=[vmem()] *...  1.41 us
  transfers between devices with their start and end apart: 4, of which 1 were waited for; matrix products, arithmetic and copies ran while one was open for 0% of the time, Pallas kernels for 6%

profile of v7, /device:TPU:0, one launch (start us, length us, event | category | flops | bytes accessed | tf_op | source)
XLA Modules:
  0.0 33.5 jit_solution(14559611975425365055)
XLA Ops:
  0.6 1.9 %bin_sites.1 = (f32[256,128]{1,0:T(8,128)}, f32[3,3,32,128]{3,2,1,0:T(8,128)S(1)}) custom-call(s32[1,128]{1,0:T(1,128)} %bitcast.18, s32[3,128]{1,0:T(4,128)} %refs_1_.1, s32[8,128]{1,0:T(8,128)} %refs_2_.1, f32[6,8,128]{2,1,0:T(8,128)} %refs_3_.1, f32[3,4,32,128]{3,2,1,0:T(8,128)} %cond_hbm.1), custom_call_target="tpu_custom_call" | custom-call | tf_op jit(solution)/shard_map/bin_sites/pallas_call | solution.py:467
  2.5 7.4 %all-to-all-start = ((f32[16,16,128]{2,1,0:T(8,128)}), f32[16,16,128]{2,1,0:T(8,128)S(1)}, u32[]{:S(2)}, u32[]{:S(2)}) async-start(f32[16,16,128]{2,1,0:T(8,128)} %bitcast.1), calls=%async_computation | async-start | bytes 262144 | tf_op jit(solution)/shard_map/all_to_all | solution.py:481
  9.9 0.4 %collective-permute-start.1 = (f32[3,4,32,128]{3,2,1,0:T(8,128)}, f32[3,4,32,128]{3,2,1,0:T(8,128)S(1)}, u32[]{:S(2)}, u32[]{:S(2)}) collective-permute-start(f32[3,4,32,128]{3,2,1,0:T(8,128)} %cond_hbm.1), channel_id=1, source_target_pairs={{0,1},{1,0},{2,3},{3,2},{4,5},{5,4},{6,7},{7,6},{8,9},{9,8},{10,11... | collective-permute-start | bytes 589832 | tf_op jit(solution)/shard_map/ppermute | solution.py:480
  10.3 1.5 %collective-permute-start.2 = (f32[3,3,32,128]{3,2,1,0:T(8,128)S(1)}, f32[3,3,32,128]{3,2,1,0:T(8,128)S(1)}, u32[]{:S(2)}, u32[]{:S(2)}) collective-permute-start(f32[3,3,32,128]{3,2,1,0:T(8,128)S(1)} %get-tuple-element.9), channel_id=1, source_target_pairs={{1,2},{2,1},{3,4},{4,3},{5,6},{6,5},{7,8},{8,7},{9,10},{10,9},{11,... | collective-permute-start | bytes 442376 | tf_op jit(solution)/shard_map/ppermute | solution.py:479
  12.4 5.4 %all-to-all-done = f32[16,16,128]{2,1,0:T(8,128)S(1)} async-done(((f32[16,16,128]{2,1,0:T(8,128)}), f32[16,16,128]{2,1,0:T(8,128)S(1)}, u32[]{:S(2)}, u32[]{:S(2)}) %all-to-all-start) | async-done | bytes 131104 | tf_op jit(solution)/shard_map/all_to_all | solution.py:481
  17.8 0.0 collective-permute-start
  17.9 2.0 %scatter_source.1 = (f32[6,6,12,4,8,128]{5,4,3,2,1,0:T(8,128)S(1)}, f32[3,4,4,8,128]{4,3,2,1,0:T(8,128)S(1)}) custom-call(f32[2,128,128]{2,1,0:T(8,128)S(1)} %copy_bitcast_fusion.list_ref, f32[3,4,32,128]{3,2,1,0:T(8,128)} %cond_hbm.1, f32[1]{0:T(128)S(6)} %copy.14.omega_ref), custom_call_target="tpu_custom_call" | custom-call | flops 1610612736 | bytes 4194304 | tf_op jit(solution)/shard_map/scatter_source/pallas_call | solution.py:403
  19.8 0.0 collective-permute-done.2.other_ref
  19.8 0.0 collective-permute-done.1.mate_ref
  19.8 0.0 collective-permute-done.list_ref
  19.9 3.3 %krylov_basis.1 = (f32[16,128]{1,0:T(8,128)S(1)}, f32[6,6,12,4,8,128]{5,4,3,2,1,0:T(8,128)S(1)}) custom-call(f32[128,128]{1,0:T(8,128)S(1)} %collective-permute-done.list_ref, f32[3,4,32,128]{3,2,1,0:T(8,128)S(1)} %collective-permute-done.1.mate_ref, f32[3,3,32,128]{3,2,1,0:T(8,128)S(1)} %collective-permute-done.2.other_ref, ...), custom_call_target="tpu_custom_call", output_to_operand_aliasing={{1}: (5, {})} | custom-call | tf_op jit(solution)/shard_map/krylov_basis/pallas_call | solution.py:420
  23.1 9.0 %all_to_all.16 = f32[16,1,128]{2,1,0:T(1,128)S(1)} all-to-all(f32[16,1,128]{2,1,0:T(1,128)S(1)} %bitcast.16), channel_id=1, replica_groups=mesh['period'=2,'gx'=16] {'gx'}, dimensions={0} | all-to-all | bytes 16384 | tf_op jit(solution)/shard_map/all_to_all | solution.py:486
  32.1 1.4 %combine_basis.1 = (f32[6,4,32,128]{3,2,1,0:T(8,128)}, f32[6,4,32,128]{3,2,1,0:T(8,128)}) custom-call(f32[16,128]{1,0:T(8,128)S(1)} %bitcast.15, f32[6,6,12,4,8,128]{5,4,3,2,1,0:T(8,128)S(1)} %get-tuple-element.13.basis), custom_call_target="tpu_custom_call" | custom-call | tf_op jit(solution)/shard_map/combine_basis/pallas_call | solution.py:441
  (2 shorter events, 0.0 us)
Async XLA Ops:
  2.5 15.3 %all-to-all-start = ((f32[16,16,128]{2,1,0:T(8,128)}), f32[16,16,128]{2,1,0:T(8,128)S(1)}, u32[]{:S(2)}, u32[]{:S(2)}) async-start(f32[16,16,128]{2,1,0:T(8,128)} %bitcast.1), calls=%async_computation | async-start | bytes 262144 | tf_op jit(solution)/shard_map/all_to_all | solution.py:481
  9.9 9.9 %collective-permute-start.1 = (f32[3,4,32,128]{3,2,1,0:T(8,128)}, f32[3,4,32,128]{3,2,1,0:T(8,128)S(1)}, u32[]{:S(2)}, u32[]{:S(2)}) collective-permute-start(f32[3,4,32,128]{3,2,1,0:T(8,128)} %cond_hbm.1), channel_id=1, source_target_pairs={{0,1},{1,0},{2,3},{3,2},{4,5},{5,4},{6,7},{7,6},{8,9},{9,8},{10,11... | collective-permute-start | bytes 589832 | tf_op jit(solution)/shard_map/ppermute | solution.py:480
  10.3 9.5 %collective-permute-start.2 = (f32[3,3,32,128]{3,2,1,0:T(8,128)S(1)}, f32[3,3,32,128]{3,2,1,0:T(8,128)S(1)}, u32[]{:S(2)}, u32[]{:S(2)}) collective-permute-start(f32[3,3,32,128]{3,2,1,0:T(8,128)S(1)} %get-tuple-element.9), channel_id=1, source_target_pairs={{1,2},{2,1},{3,4},{4,3},{5,6},{6,5},{7,8},{8,7},{9,10},{10,9},{11,... | collective-permute-start | bytes 442376 | tf_op jit(solution)/shard_map/ppermute | solution.py:479
  17.8 2.0 %collective-permute-start = (f32[128,128]{1,0:T(8,128)S(1)}, f32[128,128]{1,0:T(8,128)S(1)}, u32[]{:S(2)}, u32[]{:S(2)}) collective-permute-start(f32[128,128]{1,0:T(8,128)S(1)} %slice_bitcast_fusion), channel_id=1, source_target_pairs={{0,1},{1,0},{2,3},{3,2},{4,5},{5,4},{6,7},{7,6},{8,9},{9,8},{10,11... | collective-permute-start | bytes 196616 | tf_op jit(solution)/shard_map/ppermute | solution.py:483

commit v8 on v7

--- a/solution.py
+++ b/solution.py
@@ -66,7 +66,6 @@
         [value_ref[...].reshape(channels * points, sites), row.astype(jnp.float32), lane.astype(jnp.float32)],
         axis=0,
     )
-    blank = jnp.zeros_like(data)
 
     named = lax.broadcasted_iota(jnp.int32, (n, sites), 0) == owner
     earlier = lax.broadcasted_iota(jnp.int32, (sites, sites), 0) < lax.broadcasted_iota(
@@ -88,16 +87,19 @@
     hit = jnp.zeros(slot.shape, jnp.bool_)
     for first_row in (2 * owner + 1, 2 * beside):
         hit = hit | (slot == first_row * half + place)
-    total = jnp.zeros(out_ref.shape, jnp.float32)
-    for part, stacked in (
-        (jnp.logical_not(second), [data, blank]),
-        (second, [blank, data]),
-    ):
-        chosen = jnp.where(hit & part, 1.0, 0.0).astype(jnp.bfloat16)
-        for piece in split_bf16(jnp.concatenate(stacked, axis=0)):
-            total = total + lax.dot_general(
-                chosen, piece, CONTRACT_LANES, preferred_element_type=jnp.float32
-            )
+    chosen = [jnp.where(hit & part, 1.0, 0.0).astype(jnp.bfloat16) for part in (jnp.logical_not(second), second)]
+    stacked = []
+    for piece in split_bf16(data):
+        blank = jnp.zeros_like(piece)
+        stacked += [jnp.concatenate([piece, blank], axis=1), jnp.concatenate([blank, piece], axis=1)]
+    both = lax.dot_general(
+        jnp.concatenate(chosen, axis=1),
+        jnp.concatenate(stacked, axis=0),
+        CONTRACT_LANES,
+        preferred_element_type=jnp.float32,
+    )
+    width = out_ref.shape[1]
+    total = both[:, :width] + both[:, width:]
     out_ref[...] = total
     copies[4].wait()
 
@@ -140,20 +142,14 @@
             basis[1, c, first_plane + x] = summed[first : first + rows, lanes].reshape(folds, 8, cols)
 
 
-def scatter_kernel(list_ref, cond_hbm, omega_ref, basis, mine_ref, left, right, cond_ref, arrived):
-    conductivity = pltpu.make_async_copy(cond_hbm, cond_ref, arrived)
+def scatter_kernel(list_ref, cond_hbm, basis, mine_ref, left, right, arrived):
+    conductivity = pltpu.make_async_copy(cond_hbm, mine_ref, arrived)
     conductivity.start()
-    depth, folds = mine_ref.shape[1], mine_ref.shape[2]
-    cols = basis.shape[5]
+    depth, folds, cols = basis.shape[2] // 3, basis.shape[3], basis.shape[5]
     outer, own = (scatter_slab(list_ref[j], left.at[j], right.at[j], depth, folds, cols) for j in range(2))
     store_slab(own, basis, depth)
     store_slab(outer, basis, 2 * depth * (lax.axis_index("gx") % 2))
     conductivity.wait()
-    scale = omega_ref[0] * (2.0 / RADIUS)
-    for q in range(3):
-        for j in range(folds):
-            for x in range(depth):
-                mine_ref[q, x, j] = cond_ref[q, x, pl.ds(j, 8, stride=folds)] * scale
 
 
 def field_kernel(
@@ -165,23 +161,24 @@
     keep_low = jnp.where(me > 0, 1.0, 0.0).astype(jnp.float32)
     keep_high = jnp.where(me < n - 1, 1.0, 0.0).astype(jnp.float32)
 
+    scale = omega_ref[0] * (2.0 / RADIUS)
+    even = me % 2 == 0
+
     @pl.when(me >= 0)
     def _():
-        store_slab(scatter_slab(list_ref[...], left, right, depth, folds, cols), basis, 2 * depth * (1 - me % 2))
-
-
-    scale = omega_ref[0] * (2.0 / RADIUS)
-    even = me % 2 == 0
-    for q in range(3):
-        coupling[q, HALO : HALO + depth] = mine_ref[q]
-        for j in range(folds):
-            fold = pl.ds(j, 8, stride=folds)
-            for i in range(HALO):
-                below, above = depth - HALO + i, i
-                coupling[q, i, j] = jnp.where(even, other_ref[q, i, fold], mate_ref[q, below, fold]) * scale
-                coupling[q, HALO + depth + i, j] = (
-                    jnp.where(even, mate_ref[q, above, fold], other_ref[q, i, fold]) * scale
-                )
+        third = scatter_slab(list_ref[...], left, right, depth, folds, cols)
+        for q in range(3):
+            for j in range(folds):
+                fold = pl.ds(j, 8, stride=folds)
+                for x in range(depth):
+                    coupling[q, HALO + x, j] = mine_ref[q, x, fold] * scale
+                for i in range(HALO):
+                    below, above = depth - HALO + i, i
+                    coupling[q, i, j] = jnp.where(even, other_ref[q, i, fold], mate_ref[q, below, fold]) * scale
+                    coupling[q, HALO + depth + i, j] = (
+                        jnp.where(even, mate_ref[q, above, fold], other_ref[q, i, fold]) * scale
+                    )
+        store_slab(third, basis, 2 * depth * (1 - me % 2))
 
     s_iota = lax.broadcasted_iota(jnp.int32, (8, cols), 0)
     z_iota = lax.broadcasted_iota(jnp.int32, (folds, 8, cols), 2)
@@ -275,20 +272,24 @@
     for k in range(1, BASIS):
         pl.when(me >= 0)(functools.partial(apply, k))
 
-    def plane_forms(p, sums):
+    def some_forms(p, sums):
         sums = list(sums)
-        for q in range(3):
-            re = [basis[k + 1, q, p] for k in range(BASIS)]
-            im = [basis[k + 1, 3 + q, p] for k in range(BASIS)]
+        for q, fold in [(q, fold) for q in range(3) for fold in range(folds)]:
+            re = [basis[k + 1, q, p, fold] for k in range(BASIS)]
+            im = [basis[k + 1, 3 + q, p, fold] for k in range(BASIS)]
             for f, (i, j) in enumerate(PAIRS):
                 real = re[i] * re[j] - im[i] * im[j]
-                imag = re[i] * im[j] + im[i] * re[j] if i != j else 2.0 * (re[i] * im[i])
-                for half, term in ((0, real), (1, imag)):
-                    sums[2 * f + half] = sums[2 * f + half] + jnp.sum(term, axis=0)
+                imag = re[i] * im[j] + im[i] * re[j] if i != j else re[i] * im[i]
+                sums[2 * f] = sums[2 * f] + real
+                sums[2 * f + 1] = sums[2 * f + 1] + imag
         return tuple(sums)
 
     zero = jnp.zeros((8, cols), jnp.float32)
-    sums = lax.fori_loop(depth, 2 * depth, plane_forms, (zero,) * (2 * FORMS), unroll=2)
+    sums = lax.fori_loop(depth, 2 * depth, some_forms, (zero,) * (2 * FORMS), unroll=2)
+    sums = list(sums)
+    for f, (i, j) in enumerate(PAIRS):
+        if i == j:
+            sums[2 * f + 1] = 2.0 * sums[2 * f + 1]
     folded = jnp.concatenate([jnp.sum(total, axis=0, keepdims=True) for total in sums], axis=0)
     totals = jnp.sum(folded, axis=1, keepdims=True)
     diagonal = lax.broadcasted_iota(jnp.int32, folded.shape, 0) == lax.broadcasted_iota(jnp.int32, folded.shape, 1)
@@ -402,13 +403,12 @@
     bases = jax.ShapeDtypeStruct((BASIS + 1, 6, 3 * depth, folds, 8, cols), jnp.float32)
     basis, mine = pl.pallas_call(
         scatter_kernel,
-        out_shape=(bases, jax.ShapeDtypeStruct((3, depth, folds, 8, cols), jnp.float32)),
-        in_specs=[vmem(), hbm(), smem()],
+        out_shape=(bases, jax.ShapeDtypeStruct(conductivity.shape, jnp.float32)),
+        in_specs=[vmem(), hbm()],
         out_specs=(vmem(), vmem()),
         scratch_shapes=[
             pltpu.VMEM((2, *left_shape), jnp.bfloat16),
             pltpu.VMEM((2, *right_shape), jnp.bfloat16),
-            pltpu.VMEM(conductivity.shape, jnp.float32),
             pltpu.SemaphoreType.DMA,
         ],
         cost_estimate=pl.CostEstimate(
@@ -416,7 +416,7 @@
         ),
         compiler_params=params(),
         name="scatter_source",
-    )(lists, pltpu.with_memory_space_constraint(conductivity, pltpu.HBM), omega)
+    )(lists, pltpu.with_memory_space_constraint(conductivity, pltpu.HBM))
     return pl.pallas_call(
         functools.partial(field_kernel, n),
         out_shape=(jax.ShapeDtypeStruct((n, cols), jnp.float32), bases),
@@ -449,22 +449,10 @@
     )(forms, basis)
 
 
-def outer_pairs(periods, n):
-    pairs = []
-    for p in range(periods):
-        pairs += [(p * n + i, p * n + ((i + 1) ^ 1) - 1) for i in range(1, n - 1)]
-        if periods % 2 == 0:
-            pairs += [(p * n + i, (p ^ 1) * n + i) for i in (0, n - 1)]
-    return pairs
-
-
-def per_device(periods, n, site_owner, site_cell, stencil_code, site_residual, conductivity, omega):
+def bin_sites(n, listed, conductivity):
     depth, rows, cols = conductivity.shape[1:]
-    sites = site_owner.shape[0]
-    cap = 2 * sites // n
-    half = cap // 2
-    listed = (site_owner.reshape(1, sites), site_cell, stencil_code, site_residual)
-    packed, cut = pl.pallas_call(
+    half = listed[0].shape[1] // n
+    return pl.pallas_call(
         functools.partial(bin_kernel, n, half, rows, cols, depth // 2),
         out_shape=(
             jax.ShapeDtypeStruct((n * 2 * half, 2 * 8 * 8), jnp.float32),
@@ -476,6 +464,24 @@
         compiler_params=params(),
         name="bin_sites",
     )(*(pltpu.with_memory_space_constraint(x, pltpu.HBM) for x in (*listed, conductivity)))
+
+
+def outer_pairs(periods, n):
+    pairs = []
+    for p in range(periods):
+        pairs += [(p * n + i, p * n + ((i + 1) ^ 1) - 1) for i in range(1, n - 1)]
+        if periods % 2 == 0:
+            pairs += [(p * n + i, (p ^ 1) * n + i) for i in (0, n - 1)]
+    return pairs
+
+
+def per_device(periods, n, site_owner, site_cell, stencil_code, site_residual, conductivity, omega):
+    depth, rows, cols = conductivity.shape[1:]
+    sites = site_owner.shape[0]
+    cap = 2 * sites // n
+    half = cap // 2
+    listed = (site_owner.reshape(1, sites), site_cell, stencil_code, site_residual)
+    packed, cut = bin_sites(n, listed, conductivity)
     other = lax.ppermute(cut, ("period", "gx"), outer_pairs(periods, n))
     mate = lax.ppermute(conductivity, "gx", [(i, i ^ 1) for i in range(n)])
     recv = lax.all_to_all(packed.reshape(n, 2 * half, -1), "gx", 0, 0)

time: 33.8 us -> 33.7 us (level)
  no operation moved by 1% of the time
where the time goes in v8:
time: 33.7 us; the launch traced here: 33.4 us
  starting transfers between devices  9.3 us (28%)
  blocking collectives  8.97 us (27%)
  Pallas kernels  8.37 us (25%)
  waiting for transfers between devices  5.39 us (16%)
  between operations  1.35 us (4%)
    all_to_all x1, blocking collectives, per_device(): forms = lax.all_to_all(forms, 'gx', 0, 0, tiled=True)  8.97 us
    all_to_all x1, starting transfers between devices, per_device(): recv = lax.all_to_all(packed.reshape(n, 2 * half, -1), 'gx', 0, 0)  7.4 us
    all_to_all x1, waiting for transfers between devices, per_device(): recv = lax.all_to_all(packed.reshape(n, 2 * half, -1), 'gx', 0, 0)  5.38 us
    pallas_call x1, Pallas kernels, krylov(): pl.pallas_call(functools.partial(field_kernel, n), out_shape=(jax.ShapeDt...  3.23 us
    pallas_call x1, Pallas kernels, krylov(): pl.pallas_call(scatter_kernel, out_shape=(bases, jax.ShapeDtypeStruct(con...  1.94 us
    pallas_call x1, Pallas kernels, bin_sites(): pl.pallas_call(functools.partial(bin_kernel, n, half, rows, cols, depth /...  1.8 us
    ppermute x1, starting transfers between devices, per_device(): other = lax.ppermute(cut, ('period', 'gx'), outer_pairs(periods, n))  1.49 us
    pallas_call x1, Pallas kernels, combine(): pl.pallas_call(combine_kernel, out_shape=(out, out), in_specs=[vmem()] *...  1.41 us
  transfers between devices with their start and end apart: 4, of which 1 were waited for; matrix products, arithmetic and copies ran while one was open for 0% of the time, Pallas kernels for 6%

profile of v8, /device:TPU:0, one launch (start us, length us, event | category | flops | bytes accessed | tf_op | source)
XLA Modules:
  0.0 33.4 jit_solution(18080182622300347533)
XLA Ops:
  0.6 1.8 %bin_sites.1 = (f32[256,128]{1,0:T(8,128)}, f32[3,3,32,128]{3,2,1,0:T(8,128)S(1)}) custom-call(s32[1,128]{1,0:T(1,128)} %bitcast.18, s32[3,128]{1,0:T(4,128)} %refs_1_.1, s32[8,128]{1,0:T(8,128)} %refs_2_.1, f32[6,8,128]{2,1,0:T(8,128)} %refs_3_.1, f32[3,4,32,128]{3,2,1,0:T(8,128)} %cond_hbm.1), custom_call_target="tpu_custom_call" | custom-call | tf_op jit(solution)/shard_map/bin_sites/pallas_call | solution.py:455
  2.4 7.4 %all-to-all-start = ((f32[16,16,128]{2,1,0:T(8,128)}), f32[16,16,128]{2,1,0:T(8,128)S(1)}, u32[]{:S(2)}, u32[]{:S(2)}) async-start(f32[16,16,128]{2,1,0:T(8,128)} %bitcast.1), calls=%async_computation | async-start | bytes 262144 | tf_op jit(solution)/shard_map/all_to_all | solution.py:487
  9.8 0.4 %collective-permute-start.1 = (f32[3,4,32,128]{3,2,1,0:T(8,128)}, f32[3,4,32,128]{3,2,1,0:T(8,128)S(1)}, u32[]{:S(2)}, u32[]{:S(2)}) collective-permute-start(f32[3,4,32,128]{3,2,1,0:T(8,128)} %cond_hbm.1), channel_id=1, source_target_pairs={{0,1},{1,0},{2,3},{3,2},{4,5},{5,4},{6,7},{7,6},{8,9},{9,8},{10,11... | collective-permute-start | bytes 589832 | tf_op jit(solution)/shard_map/ppermute | solution.py:486
  10.3 1.5 %collective-permute-start.2 = (f32[3,3,32,128]{3,2,1,0:T(8,128)S(1)}, f32[3,3,32,128]{3,2,1,0:T(8,128)S(1)}, u32[]{:S(2)}, u32[]{:S(2)}) collective-permute-start(f32[3,3,32,128]{3,2,1,0:T(8,128)S(1)} %get-tuple-element.9), channel_id=1, source_target_pairs={{1,2},{2,1},{3,4},{4,3},{5,6},{6,5},{7,8},{8,7},{9,10},{10,9},{11,... | collective-permute-start | bytes 442376 | tf_op jit(solution)/shard_map/ppermute | solution.py:485
  12.4 5.4 %all-to-all-done = f32[16,16,128]{2,1,0:T(8,128)S(1)} async-done(((f32[16,16,128]{2,1,0:T(8,128)}), f32[16,16,128]{2,1,0:T(8,128)S(1)}, u32[]{:S(2)}, u32[]{:S(2)}) %all-to-all-start) | async-done | bytes 131104 | tf_op jit(solution)/shard_map/all_to_all | solution.py:487
  17.8 0.0 collective-permute-start
  17.8 1.9 %scatter_source.1 = (f32[6,6,12,4,8,128]{5,4,3,2,1,0:T(8,128)S(1)}, f32[3,4,32,128]{3,2,1,0:T(8,128)S(1)}) custom-call(f32[2,128,128]{2,1,0:T(8,128)S(1)} %copy_bitcast_fusion.list_ref, f32[3,4,32,128]{3,2,1,0:T(8,128)} %cond_hbm.1), custom_call_target="tpu_custom_call" | custom-call | flops 1610612736 | bytes 4194304 | tf_op jit(solution)/shard_map/scatter_source/pallas_call | solution.py:404
  19.8 0.0 collective-permute-done.2.other_ref
  19.8 0.0 collective-permute-done.1.mate_ref
  19.8 0.0 collective-permute-done.list_ref
  19.8 3.2 %krylov_basis.1 = (f32[16,128]{1,0:T(8,128)S(1)}, f32[6,6,12,4,8,128]{5,4,3,2,1,0:T(8,128)S(1)}) custom-call(f32[128,128]{1,0:T(8,128)S(1)} %collective-permute-done.list_ref, f32[3,4,32,128]{3,2,1,0:T(8,128)S(1)} %collective-permute-done.1.mate_ref, f32[3,3,32,128]{3,2,1,0:T(8,128)S(1)} %collective-permute-done.2.other_ref, ...), custom_call_target="tpu_custom_call", output_to_operand_aliasing={{1}: (5, {})} | custom-call | tf_op jit(solution)/shard_map/krylov_basis/pallas_call | solution.py:420
  23.0 9.0 %all_to_all.16 = f32[16,1,128]{2,1,0:T(1,128)S(1)} all-to-all(f32[16,1,128]{2,1,0:T(1,128)S(1)} %bitcast.16), channel_id=1, replica_groups=mesh['period'=2,'gx'=16] {'gx'}, dimensions={0} | all-to-all | bytes 16384 | tf_op jit(solution)/shard_map/all_to_all | solution.py:492
  32.0 1.4 %combine_basis.1 = (f32[6,4,32,128]{3,2,1,0:T(8,128)}, f32[6,4,32,128]{3,2,1,0:T(8,128)}) custom-call(f32[16,128]{1,0:T(8,128)S(1)} %bitcast.15, f32[6,6,12,4,8,128]{5,4,3,2,1,0:T(8,128)S(1)} %get-tuple-element.13.basis), custom_call_target="tpu_custom_call" | custom-call | tf_op jit(solution)/shard_map/combine_basis/pallas_call | solution.py:441
  (2 shorter events, 0.0 us)
Async XLA Ops:
  2.4 15.3 %all-to-all-start = ((f32[16,16,128]{2,1,0:T(8,128)}), f32[16,16,128]{2,1,0:T(8,128)S(1)}, u32[]{:S(2)}, u32[]{:S(2)}) async-start(f32[16,16,128]{2,1,0:T(8,128)} %bitcast.1), calls=%async_computation | async-start | bytes 262144 | tf_op jit(solution)/shard_map/all_to_all | solution.py:487
  9.8 9.9 %collective-permute-start.1 = (f32[3,4,32,128]{3,2,1,0:T(8,128)}, f32[3,4,32,128]{3,2,1,0:T(8,128)S(1)}, u32[]{:S(2)}, u32[]{:S(2)}) collective-permute-start(f32[3,4,32,128]{3,2,1,0:T(8,128)} %cond_hbm.1), channel_id=1, source_target_pairs={{0,1},{1,0},{2,3},{3,2},{4,5},{5,4},{6,7},{7,6},{8,9},{9,8},{10,11... | collective-permute-start | bytes 589832 | tf_op jit(solution)/shard_map/ppermute | solution.py:486
  10.3 9.5 %collective-permute-start.2 = (f32[3,3,32,128]{3,2,1,0:T(8,128)S(1)}, f32[3,3,32,128]{3,2,1,0:T(8,128)S(1)}, u32[]{:S(2)}, u32[]{:S(2)}) collective-permute-start(f32[3,3,32,128]{3,2,1,0:T(8,128)S(1)} %get-tuple-element.9), channel_id=1, source_target_pairs={{1,2},{2,1},{3,4},{4,3},{5,6},{6,5},{7,8},{8,7},{9,10},{10,9},{11,... | collective-permute-start | bytes 442376 | tf_op jit(solution)/shard_map/ppermute | solution.py:485
  17.8 2.0 %collective-permute-start = (f32[128,128]{1,0:T(8,128)S(1)}, f32[128,128]{1,0:T(8,128)S(1)}, u32[]{:S(2)}, u32[]{:S(2)}) collective-permute-start(f32[128,128]{1,0:T(8,128)S(1)} %slice_bitcast_fusion), channel_id=1, source_target_pairs={{0,1},{1,0},{2,3},{3,2},{4,5},{5,4},{6,7},{7,6},{8,9},{9,8},{10,11... | collective-permute-start | bytes 196616 | tf_op jit(solution)/shard_map/ppermute | solution.py:489

commit v9 on v8

--- a/solution.py
+++ b/solution.py
@@ -8,8 +8,7 @@
 from jax.sharding import PartitionSpec as P
 
 ITERS = 4
-CENTRE = 5.0
-RADIUS = 5.0
+CENTRE = 4.0
 BASIS = ITERS + 1
 FORMS = 2 * ITERS
 PAIRS = [(i // 2, (i + 1) // 2) for i in range(FORMS)]
@@ -161,7 +160,7 @@
     keep_low = jnp.where(me > 0, 1.0, 0.0).astype(jnp.float32)
     keep_high = jnp.where(me < n - 1, 1.0, 0.0).astype(jnp.float32)
 
-    scale = omega_ref[0] * (2.0 / RADIUS)
+    scale = omega_ref[0]
     even = me % 2 == 0
 
     @pl.when(me >= 0)
@@ -199,9 +198,6 @@
     def behind_z(f):
         return f - jnp.where(z_first, 0.0, pltpu.roll(f, 1, 2))
 
-    weight = 2.0 / RADIUS
-    centre = 2.0 * CENTRE / RADIUS
-
     def edges(k, p):
         return [basis[k, c, p] for c in range(channels)]
 
@@ -219,7 +215,7 @@
         for c in range(channels):
             faces[c, p] = values[c]
 
-    def plane(here, older, coupled, face, face_before):
+    def plane(here, coupled, face, face_before):
         new = []
         for part in range(2):
             hx, hy, hz = face[3 * part : 3 * part + 3]
@@ -231,10 +227,7 @@
             )
             for q in range(3):
                 other = coupled[q] * here[3 * (1 - part) + q]
-                rest = centre * here[3 * part + q]
-                if older[3 * part + q] is not None:
-                    rest = rest + older[3 * part + q]
-                value = weight * curls[q] - rest
+                value = curls[q] - CENTRE * here[3 * part + q]
                 new.append(value + other if part == 0 else value - other)
         return new
 
@@ -244,7 +237,6 @@
         def step(p, count):
             after = range(p + count, min(p + 2 * count, end))
             fields = [edges(k, p + d) for d in range(count)]
-            older = [edges(k - 1, p + d) if k > 1 else [None] * channels for d in range(count)]
             coupled = [[coupling[q, p + d - (depth - HALO)] for q in range(3)] for d in range(count)]
             face = [[faces[c, p + d] for c in range(channels)] for d in range(-1, count)]
             following = [edges(k, x) for x in range(p + count, after.stop + 1)] if after else []
@@ -254,7 +246,7 @@
                 before = [face[d][c] for c in (1, 2, 4, 5)]
                 if p + d == depth:
                     before = [f * keep_low for f in before]
-                new.append(plane(fields[d], older[d], coupled[d], face[d + 1], before))
+                new.append(plane(fields[d], coupled[d], face[d + 1], before))
                 if p + d == 2 * depth:
                     new[d] = [f * keep_high for f in new[d]]
             for d in range(count):
@@ -328,17 +320,11 @@
     field_at = [none] * BASIS
     rho = moments[0]
     for n in range(ITERS):
-        applied = [c_add(c_scale(CENTRE, direc[0]), c_scale(RADIUS / 2, direc[1]))]
-        for l in range(1, len(direc) - 1):
-            near = c_scale(RADIUS / 2, c_add(direc[l + 1], direc[l - 1]))
-            applied.append(c_add(c_scale(CENTRE, direc[l]), near))
+        applied = [c_add(c_scale(CENTRE, direc[l]), direc[l + 1]) for l in range(len(direc) - 1)]
         step = c_div(rho, c_mul(direc_at[n], applied[n]))
         applied_at = [c_scale(CENTRE, direc_at[j]) if j <= n else none for j in range(BASIS)]
         for j in range(n + 1):
-            spread = c_scale(RADIUS / 2, direc_at[j])
-            applied_at[j + 1] = c_add(applied_at[j + 1], spread)
-            if j > 0:
-                applied_at[j - 1] = c_add(applied_at[j - 1], spread)
+            applied_at[j + 1] = c_add(applied_at[j + 1], direc_at[j])
         for j in range(n + 1):
             field_at[j] = c_add(field_at[j], c_mul(step, direc_at[j]))
         for j in range(n + 2):
@@ -364,8 +350,7 @@
         for i in range(2 * FORMS)
     ]
     forms = [(sums[2 * f], sums[2 * f + 1]) for f in range(FORMS)]
-    moments = forms[:2] + [c_sub(forms[f], forms[f - 2]) for f in range(2, FORMS)]
-    field_at, resid_at = step_scalars(moments)
+    field_at, resid_at = step_scalars(forms)
 
     def copies(p):
         return [

time: 33.7 us -> 33.5 us (level)
  no operation moved by 1% of the time
where the time goes in v9:
time: 33.5 us; the launch traced here: 33.2 us
  starting transfers between devices  9.3 us (28%)
  blocking collectives  8.97 us (27%)
  Pallas kernels  8.19 us (24%)
  waiting for transfers between devices  5.39 us (16%)
  between operations  1.35 us (4%)
    all_to_all x1, blocking collectives, per_device(): forms = lax.all_to_all(forms, 'gx', 0, 0, tiled=True)  8.97 us
    all_to_all x1, starting transfers between devices, per_device(): recv = lax.all_to_all(packed.reshape(n, 2 * half, -1), 'gx', 0, 0)  7.4 us
    all_to_all x1, waiting for transfers between devices, per_device(): recv = lax.all_to_all(packed.reshape(n, 2 * half, -1), 'gx', 0, 0)  5.38 us
    pallas_call x1, Pallas kernels, krylov(): pl.pallas_call(functools.partial(field_kernel, n), out_shape=(jax.ShapeDt...  3.06 us
    pallas_call x1, Pallas kernels, krylov(): pl.pallas_call(scatter_kernel, out_shape=(bases, jax.ShapeDtypeStruct(con...  1.94 us
    pallas_call x1, Pallas kernels, bin_sites(): pl.pallas_call(functools.partial(bin_kernel, n, half, rows, cols, depth /...  1.8 us
    ppermute x1, starting transfers between devices, per_device(): other = lax.ppermute(cut, ('period', 'gx'), outer_pairs(periods, n))  1.49 us
    pallas_call x1, Pallas kernels, combine(): pl.pallas_call(combine_kernel, out_shape=(out, out), in_specs=[vmem()] *...  1.38 us
  transfers between devices with their start and end apart: 4, of which 1 were waited for; matrix products, arithmetic and copies ran while one was open for 0% of the time, Pallas kernels for 6%

profile of v9, /device:TPU:0, one launch (start us, length us, event | category | flops | bytes accessed | tf_op | source)
XLA Modules:
  0.0 33.2 jit_solution(12894558090850754125)
XLA Ops:
  0.6 1.8 %bin_sites.1 = (f32[256,128]{1,0:T(8,128)}, f32[3,3,32,128]{3,2,1,0:T(8,128)S(1)}) custom-call(s32[1,128]{1,0:T(1,128)} %bitcast.18, s32[3,128]{1,0:T(4,128)} %refs_1_.1, s32[8,128]{1,0:T(8,128)} %refs_2_.1, f32[6,8,128]{2,1,0:T(8,128)} %refs_3_.1, f32[3,4,32,128]{3,2,1,0:T(8,128)} %cond_hbm.1), custom_call_target="tpu_custom_call" | custom-call | tf_op jit(solution)/shard_map/bin_sites/pallas_call | solution.py:440
  2.4 7.4 %all-to-all-start = ((f32[16,16,128]{2,1,0:T(8,128)}), f32[16,16,128]{2,1,0:T(8,128)S(1)}, u32[]{:S(2)}, u32[]{:S(2)}) async-start(f32[16,16,128]{2,1,0:T(8,128)} %bitcast.1), calls=%async_computation | async-start | bytes 262144 | tf_op jit(solution)/shard_map/all_to_all | solution.py:472
  9.8 0.4 %collective-permute-start.1 = (f32[3,4,32,128]{3,2,1,0:T(8,128)}, f32[3,4,32,128]{3,2,1,0:T(8,128)S(1)}, u32[]{:S(2)}, u32[]{:S(2)}) collective-permute-start(f32[3,4,32,128]{3,2,1,0:T(8,128)} %cond_hbm.1), channel_id=1, source_target_pairs={{0,1},{1,0},{2,3},{3,2},{4,5},{5,4},{6,7},{7,6},{8,9},{9,8},{10,11... | collective-permute-start | bytes 589832 | tf_op jit(solution)/shard_map/ppermute | solution.py:471
  10.3 1.5 %collective-permute-start.2 = (f32[3,3,32,128]{3,2,1,0:T(8,128)S(1)}, f32[3,3,32,128]{3,2,1,0:T(8,128)S(1)}, u32[]{:S(2)}, u32[]{:S(2)}) collective-permute-start(f32[3,3,32,128]{3,2,1,0:T(8,128)S(1)} %get-tuple-element.9), channel_id=1, source_target_pairs={{1,2},{2,1},{3,4},{4,3},{5,6},{6,5},{7,8},{8,7},{9,10},{10,9},{11,... | collective-permute-start | bytes 442376 | tf_op jit(solution)/shard_map/ppermute | solution.py:470
  12.4 5.4 %all-to-all-done = f32[16,16,128]{2,1,0:T(8,128)S(1)} async-done(((f32[16,16,128]{2,1,0:T(8,128)}), f32[16,16,128]{2,1,0:T(8,128)S(1)}, u32[]{:S(2)}, u32[]{:S(2)}) %all-to-all-start) | async-done | bytes 131104 | tf_op jit(solution)/shard_map/all_to_all | solution.py:472
  17.8 0.0 collective-permute-start
  17.8 1.9 %scatter_source.1 = (f32[6,6,12,4,8,128]{5,4,3,2,1,0:T(8,128)S(1)}, f32[3,4,32,128]{3,2,1,0:T(8,128)S(1)}) custom-call(f32[2,128,128]{2,1,0:T(8,128)S(1)} %copy_bitcast_fusion.list_ref, f32[3,4,32,128]{3,2,1,0:T(8,128)} %cond_hbm.1), custom_call_target="tpu_custom_call" | custom-call | flops 1610612736 | bytes 4194304 | tf_op jit(solution)/shard_map/scatter_source/pallas_call | solution.py:389
  19.8 0.0 collective-permute-done.2.other_ref
  19.8 0.0 collective-permute-done.1.mate_ref
  19.8 0.0 collective-permute-done.list_ref
  19.8 3.1 %krylov_basis.1 = (f32[16,128]{1,0:T(8,128)S(1)}, f32[6,6,12,4,8,128]{5,4,3,2,1,0:T(8,128)S(1)}) custom-call(f32[128,128]{1,0:T(8,128)S(1)} %collective-permute-done.list_ref, f32[3,4,32,128]{3,2,1,0:T(8,128)S(1)} %collective-permute-done.1.mate_ref, f32[3,3,32,128]{3,2,1,0:T(8,128)S(1)} %collective-permute-done.2.other_ref, ...), custom_call_target="tpu_custom_call", output_to_operand_aliasing={{1}: (5, {})} | custom-call | tf_op jit(solution)/shard_map/krylov_basis/pallas_call | solution.py:405
  22.9 9.0 %all_to_all.16 = f32[16,1,128]{2,1,0:T(1,128)S(1)} all-to-all(f32[16,1,128]{2,1,0:T(1,128)S(1)} %bitcast.16), channel_id=1, replica_groups=mesh['period'=2,'gx'=16] {'gx'}, dimensions={0} | all-to-all | bytes 16384 | tf_op jit(solution)/shard_map/all_to_all | solution.py:477
  31.8 1.4 %combine_basis.1 = (f32[6,4,32,128]{3,2,1,0:T(8,128)}, f32[6,4,32,128]{3,2,1,0:T(8,128)}) custom-call(f32[16,128]{1,0:T(8,128)S(1)} %bitcast.15, f32[6,6,12,4,8,128]{5,4,3,2,1,0:T(8,128)S(1)} %get-tuple-element.13.basis), custom_call_target="tpu_custom_call" | custom-call | tf_op jit(solution)/shard_map/combine_basis/pallas_call | solution.py:426
  (2 shorter events, 0.0 us)
Async XLA Ops:
  2.4 15.3 %all-to-all-start = ((f32[16,16,128]{2,1,0:T(8,128)}), f32[16,16,128]{2,1,0:T(8,128)S(1)}, u32[]{:S(2)}, u32[]{:S(2)}) async-start(f32[16,16,128]{2,1,0:T(8,128)} %bitcast.1), calls=%async_computation | async-start | bytes 262144 | tf_op jit(solution)/shard_map/all_to_all | solution.py:472
  9.8 9.9 %collective-permute-start.1 = (f32[3,4,32,128]{3,2,1,0:T(8,128)}, f32[3,4,32,128]{3,2,1,0:T(8,128)S(1)}, u32[]{:S(2)}, u32[]{:S(2)}) collective-permute-start(f32[3,4,32,128]{3,2,1,0:T(8,128)} %cond_hbm.1), channel_id=1, source_target_pairs={{0,1},{1,0},{2,3},{3,2},{4,5},{5,4},{6,7},{7,6},{8,9},{9,8},{10,11... | collective-permute-start | bytes 589832 | tf_op jit(solution)/shard_map/ppermute | solution.py:471
  10.3 9.5 %collective-permute-start.2 = (f32[3,3,32,128]{3,2,1,0:T(8,128)S(1)}, f32[3,3,32,128]{3,2,1,0:T(8,128)S(1)}, u32[]{:S(2)}, u32[]{:S(2)}) collective-permute-start(f32[3,3,32,128]{3,2,1,0:T(8,128)S(1)} %get-tuple-element.9), channel_id=1, source_target_pairs={{1,2},{2,1},{3,4},{4,3},{5,6},{6,5},{7,8},{8,7},{9,10},{10,9},{11,... | collective-permute-start | bytes 442376 | tf_op jit(solution)/shard_map/ppermute | solution.py:470
  17.8 2.0 %collective-permute-start = (f32[128,128]{1,0:T(8,128)S(1)}, f32[128,128]{1,0:T(8,128)S(1)}, u32[]{:S(2)}, u32[]{:S(2)}) collective-permute-start(f32[128,128]{1,0:T(8,128)S(1)} %slice_bitcast_fusion), channel_id=1, source_target_pairs={{0,1},{1,0},{2,3},{3,2},{4,5},{5,4},{6,7},{7,6},{8,9},{9,8},{10,11... | collective-permute-start | bytes 196616 | tf_op jit(solution)/shard_map/ppermute | solution.py:474

commit v10 on v9

--- a/solution.py
+++ b/solution.py
@@ -13,7 +13,7 @@
 FORMS = 2 * ITERS
 PAIRS = [(i // 2, (i + 1) // 2) for i in range(FORMS)]
 HALO = ITERS - 1
-STEP = 5
+STEP = 4
 VMEM_LIMIT = 40 * 1024 * 1024
 FULL_LIMIT = 62 * 1024 * 1024
 CONTRACT_LANES = (((1,), (1,)), ((), ()))
@@ -371,7 +371,7 @@
             copy.start()
         return 0
 
-    lax.fori_loop(0, depth, plane, 0)
+    lax.fori_loop(0, depth, plane, 0, unroll=True)
     for p in range(depth):
         for copy in copies(p):
             copy.wait()

time: 33.5 us -> 33.5 us (level)
  no operation moved by 1% of the time
where the time goes in v10:
time: 33.5 us; the launch traced here: 33.2 us
  starting transfers between devices  9.3 us (28%)
  blocking collectives  8.97 us (27%)
  Pallas kernels  8.19 us (24%)
  waiting for transfers between devices  5.39 us (16%)
  between operations  1.35 us (4%)
    all_to_all x1, blocking collectives, per_device(): forms = lax.all_to_all(forms, 'gx', 0, 0, tiled=True)  8.97 us
    all_to_all x1, starting transfers between devices, per_device(): recv = lax.all_to_all(packed.reshape(n, 2 * half, -1), 'gx', 0, 0)  7.4 us
    all_to_all x1, waiting for transfers between devices, per_device(): recv = lax.all_to_all(packed.reshape(n, 2 * half, -1), 'gx', 0, 0)  5.38 us
    pallas_call x1, Pallas kernels, krylov(): pl.pallas_call(functools.partial(field_kernel, n), out_shape=(jax.ShapeDt...  3.08 us
    pallas_call x1, Pallas kernels, krylov(): pl.pallas_call(scatter_kernel, out_shape=(bases, jax.ShapeDtypeStruct(con...  1.94 us
    pallas_call x1, Pallas kernels, bin_sites(): pl.pallas_call(functools.partial(bin_kernel, n, half, rows, cols, depth /...  1.8 us
    ppermute x1, starting transfers between devices, per_device(): other = lax.ppermute(cut, ('period', 'gx'), outer_pairs(periods, n))  1.49 us
    pallas_call x1, Pallas kernels, combine(): pl.pallas_call(combine_kernel, out_shape=(out, out), in_specs=[vmem()] *...  1.37 us
  transfers between devices with their start and end apart: 4, of which 1 were waited for; matrix products, arithmetic and copies ran while one was open for 0% of the time, Pallas kernels for 6%

profile of v10, /device:TPU:0, one launch (start us, length us, event | category | flops | bytes accessed | tf_op | source)
XLA Modules:
  0.0 33.2 jit_solution(16499138795457895925)
XLA Ops:
  0.6 1.8 %bin_sites.1 = (f32[256,128]{1,0:T(8,128)}, f32[3,3,32,128]{3,2,1,0:T(8,128)S(1)}) custom-call(s32[1,128]{1,0:T(1,128)} %bitcast.18, s32[3,128]{1,0:T(4,128)} %refs_1_.1, s32[8,128]{1,0:T(8,128)} %refs_2_.1, f32[6,8,128]{2,1,0:T(8,128)} %refs_3_.1, f32[3,4,32,128]{3,2,1,0:T(8,128)} %cond_hbm.1), custom_call_target="tpu_custom_call" | custom-call | tf_op jit(solution)/shard_map/bin_sites/pallas_call | solution.py:440
  2.4 7.4 %all-to-all-start = ((f32[16,16,128]{2,1,0:T(8,128)}), f32[16,16,128]{2,1,0:T(8,128)S(1)}, u32[]{:S(2)}, u32[]{:S(2)}) async-start(f32[16,16,128]{2,1,0:T(8,128)} %bitcast.1), calls=%async_computation | async-start | bytes 262144 | tf_op jit(solution)/shard_map/all_to_all | solution.py:472
  9.8 0.4 %collective-permute-start.1 = (f32[3,4,32,128]{3,2,1,0:T(8,128)}, f32[3,4,32,128]{3,2,1,0:T(8,128)S(1)}, u32[]{:S(2)}, u32[]{:S(2)}) collective-permute-start(f32[3,4,32,128]{3,2,1,0:T(8,128)} %cond_hbm.1), channel_id=1, source_target_pairs={{0,1},{1,0},{2,3},{3,2},{4,5},{5,4},{6,7},{7,6},{8,9},{9,8},{10,11... | collective-permute-start | bytes 589832 | tf_op jit(solution)/shard_map/ppermute | solution.py:471
  10.3 1.5 %collective-permute-start.2 = (f32[3,3,32,128]{3,2,1,0:T(8,128)S(1)}, f32[3,3,32,128]{3,2,1,0:T(8,128)S(1)}, u32[]{:S(2)}, u32[]{:S(2)}) collective-permute-start(f32[3,3,32,128]{3,2,1,0:T(8,128)S(1)} %get-tuple-element.9), channel_id=1, source_target_pairs={{1,2},{2,1},{3,4},{4,3},{5,6},{6,5},{7,8},{8,7},{9,10},{10,9},{11,... | collective-permute-start | bytes 442376 | tf_op jit(solution)/shard_map/ppermute | solution.py:470
  12.4 5.4 %all-to-all-done = f32[16,16,128]{2,1,0:T(8,128)S(1)} async-done(((f32[16,16,128]{2,1,0:T(8,128)}), f32[16,16,128]{2,1,0:T(8,128)S(1)}, u32[]{:S(2)}, u32[]{:S(2)}) %all-to-all-start) | async-done | bytes 131104 | tf_op jit(solution)/shard_map/all_to_all | solution.py:472
  17.8 0.0 collective-permute-start
  17.8 1.9 %scatter_source.1 = (f32[6,6,12,4,8,128]{5,4,3,2,1,0:T(8,128)S(1)}, f32[3,4,32,128]{3,2,1,0:T(8,128)S(1)}) custom-call(f32[2,128,128]{2,1,0:T(8,128)S(1)} %copy_bitcast_fusion.list_ref, f32[3,4,32,128]{3,2,1,0:T(8,128)} %cond_hbm.1), custom_call_target="tpu_custom_call" | custom-call | flops 1610612736 | bytes 4194304 | tf_op jit(solution)/shard_map/scatter_source/pallas_call | solution.py:389
  19.8 0.0 collective-permute-done.2.other_ref
  19.8 0.0 collective-permute-done.1.mate_ref
  19.8 0.0 collective-permute-done.list_ref
  19.8 3.1 %krylov_basis.1 = (f32[16,128]{1,0:T(8,128)S(1)}, f32[6,6,12,4,8,128]{5,4,3,2,1,0:T(8,128)S(1)}) custom-call(f32[128,128]{1,0:T(8,128)S(1)} %collective-permute-done.list_ref, f32[3,4,32,128]{3,2,1,0:T(8,128)S(1)} %collective-permute-done.1.mate_ref, f32[3,3,32,128]{3,2,1,0:T(8,128)S(1)} %collective-permute-done.2.other_ref, ...), custom_call_target="tpu_custom_call", output_to_operand_aliasing={{1}: (5, {})} | custom-call | tf_op jit(solution)/shard_map/krylov_basis/pallas_call | solution.py:405
  22.9 9.0 %all_to_all.16 = f32[16,1,128]{2,1,0:T(1,128)S(1)} all-to-all(f32[16,1,128]{2,1,0:T(1,128)S(1)} %bitcast.16), channel_id=1, replica_groups=mesh['period'=2,'gx'=16] {'gx'}, dimensions={0} | all-to-all | bytes 16384 | tf_op jit(solution)/shard_map/all_to_all | solution.py:477
  31.8 1.4 %combine_basis.1 = (f32[6,4,32,128]{3,2,1,0:T(8,128)}, f32[6,4,32,128]{3,2,1,0:T(8,128)}) custom-call(f32[16,128]{1,0:T(8,128)S(1)} %bitcast.15, f32[6,6,12,4,8,128]{5,4,3,2,1,0:T(8,128)S(1)} %get-tuple-element.13.basis), custom_call_target="tpu_custom_call" | custom-call | tf_op jit(solution)/shard_map/combine_basis/pallas_call | solution.py:426
  (2 shorter events, 0.0 us)
Async XLA Ops:
  2.4 15.3 %all-to-all-start = ((f32[16,16,128]{2,1,0:T(8,128)}), f32[16,16,128]{2,1,0:T(8,128)S(1)}, u32[]{:S(2)}, u32[]{:S(2)}) async-start(f32[16,16,128]{2,1,0:T(8,128)} %bitcast.1), calls=%async_computation | async-start | bytes 262144 | tf_op jit(solution)/shard_map/all_to_all | solution.py:472
  9.8 9.9 %collective-permute-start.1 = (f32[3,4,32,128]{3,2,1,0:T(8,128)}, f32[3,4,32,128]{3,2,1,0:T(8,128)S(1)}, u32[]{:S(2)}, u32[]{:S(2)}) collective-permute-start(f32[3,4,32,128]{3,2,1,0:T(8,128)} %cond_hbm.1), channel_id=1, source_target_pairs={{0,1},{1,0},{2,3},{3,2},{4,5},{5,4},{6,7},{7,6},{8,9},{9,8},{10,11... | collective-permute-start | bytes 589832 | tf_op jit(solution)/shard_map/ppermute | solution.py:471
  10.3 9.5 %collective-permute-start.2 = (f32[3,3,32,128]{3,2,1,0:T(8,128)S(1)}, f32[3,3,32,128]{3,2,1,0:T(8,128)S(1)}, u32[]{:S(2)}, u32[]{:S(2)}) collective-permute-start(f32[3,3,32,128]{3,2,1,0:T(8,128)S(1)} %get-tuple-element.9), channel_id=1, source_target_pairs={{1,2},{2,1},{3,4},{4,3},{5,6},{6,5},{7,8},{8,7},{9,10},{10,9},{11,... | collective-permute-start | bytes 442376 | tf_op jit(solution)/shard_map/ppermute | solution.py:470
  17.8 2.0 %collective-permute-start = (f32[128,128]{1,0:T(8,128)S(1)}, f32[128,128]{1,0:T(8,128)S(1)}, u32[]{:S(2)}, u32[]{:S(2)}) collective-permute-start(f32[128,128]{1,0:T(8,128)S(1)} %slice_bitcast_fusion), channel_id=1, source_target_pairs={{0,1},{1,0},{2,3},{3,2},{4,5},{5,4},{6,7},{7,6},{8,9},{9,8},{10,11... | collective-permute-start | bytes 196616 | tf_op jit(solution)/shard_map/ppermute | solution.py:474
